TPU v7x, 32 devices: a whole 2x2x4 slice. The times are simulated.
32 devices in a mesh: dp: 8 (over y, x, core), seq: 4 (over z).
Axes of the slice: x: 2, y: 2, z: 4, core: 2. Of those that a mesh axis runs over, the one named last changes fastest.
Arguments:
- hidden: bfloat16 [16, 3, 1024, 1024], P('dp', None, 'seq'), may hold values from -6 to 6
- encoder_out: bfloat16 [16, 1024, 1024], P('dp', 'seq'), may hold values from -6 to 6
- cotangent: bfloat16 [16, 3, 1024, 1024], P('dp', None, 'seq'), may hold values from -6 to 6
- dec_lengths: int32 [16], P('dp'), may hold values from 512 to 1024, as said below
- enc_lengths: int32 [16], P('dp'), may hold values from 512 to 1024, as said below
- self_qkv: bfloat16 [3, 1024, 1024], replicated, may hold values from -0.1875 to 0.1875
- self_qv_bias: bfloat16 [2, 1024], replicated, may hold values from -3 to 3
- self_out: bfloat16 [1024, 1024], replicated, may hold values from -3 to 3
- self_out_bias: bfloat16 [1024], replicated, may hold values from -2 to 2
- rel_weight: bfloat16 [1024, 512], replicated, may hold values from -0.1875 to 0.1875
- rel_bias: bfloat16 [512], replicated, may hold values from -4 to 4
- cross_qkv: bfloat16 [3, 1024, 1024], replicated, may hold values from -0.1875 to 0.1875
- cross_qv_bias: bfloat16 [2, 1024], replicated, may hold values from -3 to 3
- cross_out: bfloat16 [1024, 1024], replicated, may hold values from -3 to 3
- cross_out_bias: bfloat16 [1024], replicated, may hold values from -2 to 2
- ffn_in: bfloat16 [1024, 4096], replicated, may hold values from -0.1875 to 0.1875
- ffn_in_bias: bfloat16 [4096], replicated, may hold values from -3 to 3
- ffn_out: bfloat16 [4096, 1024], replicated, may hold values from -0.09375 to 0.09375
- ffn_out_bias: bfloat16 [1024], replicated, may hold values from -2 to 2
- norm_gain: bfloat16 [3, 1024], replicated, may hold values from 0.5 to 1.5
- norm_bias: bfloat16 [3, 1024], replicated, may hold values from -2 to 2
Outputs:
- output: bfloat16 [16, 3, 1024, 1024], P('dp', None, 'seq')
- grad_hidden: bfloat16 [16, 3, 1024, 1024], P('dp', None, 'seq')
- grad_encoder: bfloat16 [16, 1024, 1024], P('dp', 'seq')
- grad_self_qkv: float32 [3145728], P(('dp', 'seq'))
- grad_self_qv_bias: float32 [2048], P('seq')
- grad_self_out: float32 [1048576], P(('dp', 'seq'))
- grad_self_out_bias: float32 [1024], P('seq')
- grad_rel_weight: float32 [524288], P(('dp', 'seq'))
- grad_rel_bias: float32 [512], P('seq')
- grad_cross_qkv: float32 [3145728], P(('dp', 'seq'))
- grad_cross_qv_bias: float32 [2048], P('seq')
- grad_cross_out: float32 [1048576], P(('dp', 'seq'))
- grad_cross_out_bias: float32 [1024], P('seq')
- grad_ffn_in: float32 [4194304], P(('dp', 'seq'))
- grad_ffn_in_bias: float32 [4096], P('seq')
- grad_ffn_out: float32 [4194304], P(('dp', 'seq'))
- grad_ffn_out_bias: float32 [1024], P('seq')
- grad_norm_gain: float32 [3072], P('seq')
- grad_norm_bias: float32 [3072], P('seq')
Inputs may be any that keep to these rules, and one draw needn't show every extreme that they name: `dec_lengths`: in each group of 2 consecutive sequences one, drawn from the seed, has all 1024 decoder positions valid. `enc_lengths`: in each group of 2 consecutive sequences one, drawn from the seed, has all 1024 encoder positions valid.
All inputs are finite; a program needn't handle non-finite values.
Results may differ from a plain program's by a relative error of at most 0.028.
Values may be sent and summed in bfloat16 or wider, within the bound.
No kernel may reach another device: no remote copies, remote signals or barrier semaphores. Data moves between devices by JAX's collectives and lax.ppermute only.
A program may use at most 576 MiB of HBM per device.

v0:
```python
import math

import jax
import jax.numpy as jnp
from jax import lax
from jax.sharding import PartitionSpec as P

HEADS = 16
BUCKETS = 32
MAX_DIST = 128


HIGHEST = lax.Precision.HIGHEST
negative = -1e30
epsilon = 1e-05


def rounded(value):
    return lax.optimization_barrier(value.astype(jnp.bfloat16)).astype(jnp.float32)


def layer_norm(value, gain, shift):
    center = value - jnp.mean(value, -1, keepdims=True)
    spread = jnp.mean(center * center, -1, keepdims=True)
    return center * lax.rsqrt(spread + epsilon) * gain + shift


def gelu_exact(value):
    return jax.nn.gelu(value, approximate=False)


def bucket_of(distance):
    half = BUCKETS // 2
    counted = jnp.zeros_like(distance)
    for level in range(1, half):
        bound = math.ceil(half * (MAX_DIST / half) ** (level / half))
        counted = counted + (distance >= bound).astype(jnp.int32)
    return jnp.where(distance < half, distance, half + counted)


def self_logits(query_s, key_s, rel_s, keys_s, dec_len, offset_pos):
    streams, local_len, heads, size = query_s.shape
    full_len = keys_s.shape[0]
    scale = size ** (-0.5)
    positions = offset_pos + jnp.arange(local_len, dtype=jnp.int32)
    key_positions = jnp.arange(full_len, dtype=jnp.int32)
    distance = positions[:, None] - key_positions[None, :]
    one_hot = (
        bucket_of(jnp.maximum(distance, 0))[:, :, None] == jnp.arange(BUCKETS, dtype=jnp.int32)
    ).astype(jnp.float32)
    scores = scale * jnp.einsum(
        "sqhd,khd->shqk", query_s, keys_s, preferred_element_type=jnp.float32
    )
    scores = scores + jnp.einsum("sqhb,qkb->shqk", rel_s, one_hot, precision=HIGHEST)
    stream_ids = jnp.arange(streams, dtype=jnp.int32)
    allowed = (distance[None] >= jnp.minimum(stream_ids, 1)[:, None, None]) & (
        key_positions < dec_len
    )[None, None, :]
    scores = jnp.where(allowed[:, None], scores, negative)
    own_score = (
        scale * jnp.sum(query_s.astype(jnp.float32) * key_s.astype(jnp.float32), -1) + rel_s[..., 0]
    )
    own_score = jnp.where(
        (stream_ids > 0)[:, None, None], jnp.transpose(own_score, (0, 2, 1)), negative
    )
    return (scores, own_score, one_hot)


def self_forward(items, offset_pos):
    query_s, key_s, value_s, rel_s, keys_s, values_s, dec_len = items
    scores, own_score, one_hot = self_logits(query_s, key_s, rel_s, keys_s, dec_len, offset_pos)
    peak = jnp.maximum(jnp.max(scores, -1), own_score)
    log_total = peak + jnp.log(
        jnp.sum(jnp.exp(scores - peak[..., None]), -1) + jnp.exp(own_score - peak)
    )
    weights = jnp.exp(scores - log_total[..., None]).astype(jnp.bfloat16)
    own_weight = rounded(jnp.exp(own_score - log_total))
    mixed = jnp.einsum("shqk,khd->sqhd", weights, values_s, preferred_element_type=jnp.float32)
    mixed = mixed + jnp.transpose(own_weight, (0, 2, 1))[..., None] * value_s.astype(jnp.float32)
    return (mixed.astype(jnp.bfloat16), log_total)


def self_backward(items, offset_pos):
    query_s, key_s, value_s, rel_s, keys_s, values_s, dec_len, log_total, grad_s = items
    scores, own_score, one_hot = self_logits(query_s, key_s, rel_s, keys_s, dec_len, offset_pos)
    scale = query_s.shape[3] ** (-0.5)
    weights = jnp.exp(scores - log_total[..., None])
    own_weight = jnp.exp(own_score - log_total)
    grad_float = grad_s.astype(jnp.float32)
    grad_weights = jnp.einsum(
        "sqhd,khd->shqk", grad_s, values_s, preferred_element_type=jnp.float32
    )
    grad_own = jnp.transpose(jnp.sum(grad_float * value_s.astype(jnp.float32), -1), (0, 2, 1))
    delta = jnp.sum(grad_weights * weights, -1) + grad_own * own_weight
    grad_scores = (weights * (grad_weights - delta[..., None])).astype(jnp.bfloat16)
    grad_own_score = rounded(own_weight * (grad_own - delta))
    own_term = jnp.transpose(grad_own_score, (0, 2, 1))[..., None]
    grad_query = scale * (
        jnp.einsum("shqk,khd->sqhd", grad_scores, keys_s, preferred_element_type=jnp.float32)
        + own_term * key_s.astype(jnp.float32)
    )
    grad_keys = scale * jnp.einsum(
        "shqk,sqhd->khd", grad_scores, query_s, preferred_element_type=jnp.float32
    )
    grad_key_own = scale * own_term * query_s.astype(jnp.float32)
    grad_values = jnp.einsum(
        "shqk,sqhd->khd", weights.astype(jnp.bfloat16), grad_s, preferred_element_type=jnp.float32
    )
    grad_value_own = jnp.transpose(rounded(own_weight), (0, 2, 1))[..., None] * grad_float
    grad_rel = jnp.einsum(
        "shqk,qkb->sqhb", grad_scores.astype(jnp.float32), one_hot, precision=HIGHEST
    )
    grad_rel = grad_rel.at[..., 0].add(jnp.transpose(grad_own_score, (0, 2, 1)))
    return (grad_query, grad_key_own, grad_value_own, grad_keys, grad_values, grad_rel)


def cross_logits(query_s, keys_s, enc_len):
    scale = query_s.shape[3] ** (-0.5)
    scores = scale * jnp.einsum(
        "sqhd,khd->shqk", query_s, keys_s, preferred_element_type=jnp.float32
    )
    key_positions = jnp.arange(keys_s.shape[0], dtype=jnp.int32)
    return jnp.where(key_positions < enc_len, scores, negative)


def cross_forward(items):
    query_s, keys_s, values_s, enc_len = items
    scores = cross_logits(query_s, keys_s, enc_len)
    peak = jnp.max(scores, -1)
    log_total = peak + jnp.log(jnp.sum(jnp.exp(scores - peak[..., None]), -1))
    weights = jnp.exp(scores - log_total[..., None]).astype(jnp.bfloat16)
    mixed = jnp.einsum("shqk,khd->sqhd", weights, values_s, preferred_element_type=jnp.float32)
    return (mixed.astype(jnp.bfloat16), log_total)


def cross_backward(items):
    query_s, keys_s, values_s, enc_len, log_total, grad_s = items
    scale = query_s.shape[3] ** (-0.5)
    scores = cross_logits(query_s, keys_s, enc_len)
    weights = jnp.exp(scores - log_total[..., None])
    grad_weights = jnp.einsum(
        "sqhd,khd->shqk", grad_s, values_s, preferred_element_type=jnp.float32
    )
    delta = jnp.sum(grad_weights * weights, -1)
    grad_scores = (weights * (grad_weights - delta[..., None])).astype(jnp.bfloat16)
    grad_query = scale * jnp.einsum(
        "shqk,khd->sqhd", grad_scores, keys_s, preferred_element_type=jnp.float32
    )
    grad_keys = scale * jnp.einsum(
        "shqk,sqhd->khd", grad_scores, query_s, preferred_element_type=jnp.float32
    )
    grad_values = jnp.einsum(
        "shqk,sqhd->khd", weights.astype(jnp.bfloat16), grad_s, preferred_element_type=jnp.float32
    )
    return (grad_query, grad_keys, grad_values)


def column_sum(value):
    return jnp.sum(value.astype(jnp.float32), 0)


def on_device(
    hidden,
    encoder_out,
    cotangent,
    dec_lengths,
    enc_lengths,
    self_qkv,
    self_qv_bias,
    self_out,
    self_out_bias,
    rel_weight,
    rel_bias,
    cross_qkv,
    cross_qv_bias,
    cross_out,
    cross_out_bias,
    ffn_in,
    ffn_in_bias,
    ffn_out,
    ffn_out_bias,
    norm_gain,
    norm_bias,
):
    low_type = jnp.bfloat16
    high_type = jnp.float32
    seq_count, streams, local_len, width = hidden.shape
    seq_parts = lax.axis_size("seq")
    dp_parts = lax.axis_size("dp")
    full_len = local_len * seq_parts
    offset_pos = lax.axis_index("seq") * local_len
    heads = HEADS
    size = width // heads
    head_shape = (seq_count, streams, local_len, heads, size)
    all_shape = (seq_count, full_len, heads, size)
    kv_shape = (seq_count, full_len, width)
    rows = hidden.reshape(-1, width)
    row_count = rows.shape[0]
    gains = norm_gain.astype(high_type)
    shifts = norm_bias.astype(high_type)
    self_bias = self_qv_bias.astype(high_type)
    cross_bias = cross_qv_bias.astype(high_type)
    projected = jnp.einsum("rd,cde->cre", rows, self_qkv, preferred_element_type=high_type)
    query = (projected[0] + self_bias[0]).astype(low_type)
    key = projected[1].astype(low_type)
    value = (projected[2] + self_bias[1]).astype(low_type)
    rel_logits = jnp.dot(rows, rel_weight, preferred_element_type=high_type) + rel_bias.astype(
        high_type
    )
    rel_heads = rel_logits.reshape(seq_count, streams, local_len, heads, BUCKETS)
    key_main = key.reshape(seq_count, streams, local_len, width)[:, 0]
    value_main = value.reshape(seq_count, streams, local_len, width)[:, 0]
    keys_all, values_all = (
        lax.all_gather(key_main, "seq", axis=1, tiled=True),
        lax.all_gather(value_main, "seq", axis=1, tiled=True),
    )
    self_items = (
        query.reshape(head_shape),
        key.reshape(head_shape),
        value.reshape(head_shape),
        rel_heads,
        keys_all.reshape(all_shape),
        values_all.reshape(all_shape),
        dec_lengths,
    )
    attended, self_total = lax.map(lambda items: self_forward(items, offset_pos), self_items)
    attended = attended.reshape(row_count, width)
    self_branch = jnp.dot(
        attended, self_out, preferred_element_type=high_type
    ) + self_out_bias.astype(high_type)
    first_sum = rows.astype(high_type) + self_branch
    first_norm = layer_norm(first_sum, gains[0], shifts[0])
    first_low = first_norm.astype(low_type)
    cross_query = (
        jnp.dot(first_low, cross_qkv[0], preferred_element_type=high_type) + cross_bias[0]
    ).astype(low_type)
    encoder_rows = encoder_out.reshape(-1, width)
    encoder_proj = jnp.einsum(
        "rd,cde->cre", encoder_rows, cross_qkv[1:], preferred_element_type=high_type
    )
    cross_key = encoder_proj[0].astype(low_type).reshape(seq_count, local_len, width)
    cross_value = (
        (encoder_proj[1] + cross_bias[1]).astype(low_type).reshape(seq_count, local_len, width)
    )
    cross_keys, cross_values = (
        lax.all_gather(cross_key, "seq", axis=1, tiled=True),
        lax.all_gather(cross_value, "seq", axis=1, tiled=True),
    )
    cross_items = (
        cross_query.reshape(head_shape),
        cross_keys.reshape(all_shape),
        cross_values.reshape(all_shape),
        enc_lengths,
    )
    cross_mixed, cross_total = lax.map(cross_forward, cross_items)
    cross_mixed = cross_mixed.reshape(row_count, width)
    cross_branch = jnp.dot(
        cross_mixed, cross_out, preferred_element_type=high_type
    ) + cross_out_bias.astype(high_type)
    second_sum = first_norm + cross_branch
    second_norm = layer_norm(second_sum, gains[1], shifts[1])
    second_low = second_norm.astype(low_type)
    hidden_pre = jnp.dot(second_low, ffn_in, preferred_element_type=high_type) + ffn_in_bias.astype(
        high_type
    )
    activated = gelu_exact(hidden_pre).astype(low_type)
    ffn_branch = jnp.dot(
        activated, ffn_out, preferred_element_type=high_type
    ) + ffn_out_bias.astype(high_type)
    third_sum = second_norm + ffn_branch
    output = layer_norm(third_sum, gains[2], shifts[2]).astype(low_type).reshape(hidden.shape)
    third_value, norm_pull = jax.vjp(layer_norm, third_sum, gains[2], shifts[2])
    grad_third, grad_gain_ffn, grad_shift_ffn = norm_pull(
        cotangent.reshape(-1, width).astype(high_type)
    )
    grad_ffn = grad_third.astype(low_type)
    grad_ffn_out = jnp.einsum("rf,rd->fd", activated, grad_ffn, preferred_element_type=high_type)
    grad_ffn_out_bias = column_sum(grad_ffn)
    grad_activated = jnp.einsum("rd,fd->rf", grad_ffn, ffn_out, preferred_element_type=high_type)
    gelu_value, gelu_pull = jax.vjp(gelu_exact, hidden_pre)
    grad_pre = gelu_pull(grad_activated)[0].astype(low_type)
    grad_ffn_in = jnp.einsum("rd,rf->df", second_low, grad_pre, preferred_element_type=high_type)
    grad_ffn_in_bias = column_sum(grad_pre)
    grad_second = grad_third + jnp.einsum(
        "rf,df->rd", grad_pre, ffn_in, preferred_element_type=high_type
    )
    second_value, norm_pull = jax.vjp(layer_norm, second_sum, gains[1], shifts[1])
    grad_second_sum, grad_gain_cross, grad_shift_cross = norm_pull(grad_second)
    grad_cross = grad_second_sum.astype(low_type)
    grad_cross_out = jnp.einsum(
        "rd,re->de", cross_mixed, grad_cross, preferred_element_type=high_type
    )
    grad_cross_out_bias = column_sum(grad_cross)
    grad_cross_mixed = jnp.einsum(
        "re,de->rd", grad_cross, cross_out, preferred_element_type=high_type
    ).astype(low_type)
    cross_back_items = (
        cross_query.reshape(head_shape),
        cross_keys.reshape(all_shape),
        cross_values.reshape(all_shape),
        enc_lengths,
        cross_total,
        grad_cross_mixed.reshape(head_shape),
    )
    grad_cross_query, grad_cross_keys, grad_cross_values = lax.map(cross_backward, cross_back_items)
    cross_key_sum, cross_value_sum = (
        lax.psum_scatter(
            grad_cross_keys.reshape(kv_shape).astype(jnp.bfloat16),
            "seq",
            scatter_dimension=1,
            tiled=True,
        ).astype(jnp.float32),
        lax.psum_scatter(
            grad_cross_values.reshape(kv_shape).astype(jnp.bfloat16),
            "seq",
            scatter_dimension=1,
            tiled=True,
        ).astype(jnp.float32),
    )
    query_low = grad_cross_query.reshape(row_count, width).astype(low_type)
    encoder_grads = jnp.stack(
        [cross_key_sum.reshape(-1, width), cross_value_sum.reshape(-1, width)]
    ).astype(low_type)
    grad_cross_query_weight = jnp.einsum(
        "rd,re->de", first_low, query_low, preferred_element_type=high_type
    )
    grad_cross_kv_weight = jnp.einsum(
        "rd,cre->cde", encoder_rows, encoder_grads, preferred_element_type=high_type
    )
    grad_cross_qkv = jnp.concatenate([grad_cross_query_weight[None], grad_cross_kv_weight], 0)
    grad_cross_bias = jnp.stack([column_sum(query_low), column_sum(encoder_grads[1])])
    grad_encoder = jnp.einsum(
        "cre,cde->rd", encoder_grads, cross_qkv[1:], preferred_element_type=high_type
    )
    grad_encoder = grad_encoder.astype(low_type).reshape(encoder_out.shape)
    grad_first = grad_second_sum + jnp.einsum(
        "re,de->rd", query_low, cross_qkv[0], preferred_element_type=high_type
    )
    first_value, norm_pull = jax.vjp(layer_norm, first_sum, gains[0], shifts[0])
    grad_first_sum, grad_gain_self, grad_shift_self = norm_pull(grad_first)
    grad_self = grad_first_sum.astype(low_type)
    grad_self_out = jnp.einsum("rd,re->de", attended, grad_self, preferred_element_type=high_type)
    grad_self_out_bias = column_sum(grad_self)
    grad_attended = jnp.einsum(
        "re,de->rd", grad_self, self_out, preferred_element_type=high_type
    ).astype(low_type)
    self_back_items = (
        query.reshape(head_shape),
        key.reshape(head_shape),
        value.reshape(head_shape),
        rel_heads,
        keys_all.reshape(all_shape),
        values_all.reshape(all_shape),
        dec_lengths,
        self_total,
        grad_attended.reshape(head_shape),
    )
    grad_query, grad_key_own, grad_value_own, grad_keys, grad_values, grad_rel = lax.map(
        lambda items: self_backward(items, offset_pos), self_back_items
    )
    key_sum, value_sum = (
        lax.psum_scatter(
            grad_keys.reshape(kv_shape).astype(jnp.bfloat16), "seq", scatter_dimension=1, tiled=True
        ).astype(jnp.float32),
        lax.psum_scatter(
            grad_values.reshape(kv_shape).astype(jnp.bfloat16),
            "seq",
            scatter_dimension=1,
            tiled=True,
        ).astype(jnp.float32),
    )
    own_shape = (seq_count, streams, local_len, width)
    key_total = jnp.concatenate([key_sum[:, None], grad_key_own.reshape(own_shape)[:, 1:]], 1)
    value_total = jnp.concatenate([value_sum[:, None], grad_value_own.reshape(own_shape)[:, 1:]], 1)
    stacked_grad = jnp.stack(
        [
            grad_query.reshape(row_count, width),
            key_total.reshape(row_count, width),
            value_total.reshape(row_count, width),
        ]
    ).astype(low_type)
    rel_low = grad_rel.reshape(row_count, heads * BUCKETS).astype(low_type)
    grad_self_qkv = jnp.einsum("rd,cre->cde", rows, stacked_grad, preferred_element_type=high_type)
    grad_self_bias = jnp.stack([column_sum(stacked_grad[0]), column_sum(stacked_grad[2])])
    grad_rel_weight = jnp.einsum("rd,rb->db", rows, rel_low, preferred_element_type=high_type)
    grad_rel_bias = column_sum(rel_low)
    grad_rows = grad_first_sum + jnp.einsum(
        "cre,cde->rd", stacked_grad, self_qkv, preferred_element_type=high_type
    )
    grad_rows = grad_rows + jnp.einsum(
        "rb,db->rd", rel_low, rel_weight, preferred_element_type=high_type
    )
    grad_hidden = grad_rows.astype(low_type).reshape(hidden.shape)
    matrices = [
        grad_self_qkv,
        grad_self_out,
        grad_rel_weight,
        grad_cross_qkv,
        grad_cross_out,
        grad_ffn_in,
        grad_ffn_out,
    ]
    vectors = [
        grad_self_bias.reshape(-1),
        grad_self_out_bias,
        grad_rel_bias,
        grad_cross_bias.reshape(-1),
        grad_cross_out_bias,
        grad_ffn_in_bias,
        grad_ffn_out_bias,
        jnp.stack([grad_gain_self, grad_gain_cross, grad_gain_ffn]).reshape(-1),
        jnp.stack([grad_shift_self, grad_shift_cross, grad_shift_ffn]).reshape(-1),
    ]
    vec_blocks = [piece.reshape(seq_parts, -1) for piece in vectors]
    mat_blocks = [piece.reshape(dp_parts, seq_parts, -1) for piece in matrices]
    reduced = (
        lax.psum_scatter(
            mat_blocks[0].astype(jnp.bfloat16), "seq", scatter_dimension=1, tiled=True
        ).astype(jnp.float32),
        lax.psum_scatter(
            mat_blocks[1].astype(jnp.bfloat16), "seq", scatter_dimension=1, tiled=True
        ).astype(jnp.float32),
        lax.psum_scatter(
            mat_blocks[2].astype(jnp.bfloat16), "seq", scatter_dimension=1, tiled=True
        ).astype(jnp.float32),
        lax.psum_scatter(
            mat_blocks[3].astype(jnp.bfloat16), "seq", scatter_dimension=1, tiled=True
        ).astype(jnp.float32),
        lax.psum_scatter(
            mat_blocks[4].astype(jnp.bfloat16), "seq", scatter_dimension=1, tiled=True
        ).astype(jnp.float32),
        lax.psum_scatter(
            mat_blocks[5].astype(jnp.bfloat16), "seq", scatter_dimension=1, tiled=True
        ).astype(jnp.float32),
        lax.psum_scatter(
            mat_blocks[6].astype(jnp.bfloat16), "seq", scatter_dimension=1, tiled=True
        ).astype(jnp.float32),
        lax.psum_scatter(
            vec_blocks[0].astype(jnp.bfloat16), "seq", scatter_dimension=0, tiled=True
        ).astype(jnp.float32),
        lax.psum_scatter(
            vec_blocks[1].astype(jnp.bfloat16), "seq", scatter_dimension=0, tiled=True
        ).astype(jnp.float32),
        lax.psum_scatter(
            vec_blocks[2].astype(jnp.bfloat16), "seq", scatter_dimension=0, tiled=True
        ).astype(jnp.float32),
        lax.psum_scatter(
            vec_blocks[3].astype(jnp.bfloat16), "seq", scatter_dimension=0, tiled=True
        ).astype(jnp.float32),
        lax.psum_scatter(
            vec_blocks[4].astype(jnp.bfloat16), "seq", scatter_dimension=0, tiled=True
        ).astype(jnp.float32),
        lax.psum_scatter(
            vec_blocks[5].astype(jnp.bfloat16), "seq", scatter_dimension=0, tiled=True
        ).astype(jnp.float32),
        lax.psum_scatter(
            vec_blocks[6].astype(jnp.bfloat16), "seq", scatter_dimension=0, tiled=True
        ).astype(jnp.float32),
        lax.psum_scatter(
            vec_blocks[7].astype(jnp.bfloat16), "seq", scatter_dimension=0, tiled=True
        ).astype(jnp.float32),
        lax.psum_scatter(
            vec_blocks[8].astype(jnp.bfloat16), "seq", scatter_dimension=0, tiled=True
        ).astype(jnp.float32),
    )
    mat_done = (
        lax.psum_scatter(
            reduced[0].astype(jnp.bfloat16), "dp", scatter_dimension=0, tiled=True
        ).astype(jnp.float32),
        lax.psum_scatter(
            reduced[1].astype(jnp.bfloat16), "dp", scatter_dimension=0, tiled=True
        ).astype(jnp.float32),
        lax.psum_scatter(
            reduced[2].astype(jnp.bfloat16), "dp", scatter_dimension=0, tiled=True
        ).astype(jnp.float32),
        lax.psum_scatter(
            reduced[3].astype(jnp.bfloat16), "dp", scatter_dimension=0, tiled=True
        ).astype(jnp.float32),
        lax.psum_scatter(
            reduced[4].astype(jnp.bfloat16), "dp", scatter_dimension=0, tiled=True
        ).astype(jnp.float32),
        lax.psum_scatter(
            reduced[5].astype(jnp.bfloat16), "dp", scatter_dimension=0, tiled=True
        ).astype(jnp.float32),
        lax.psum_scatter(
            reduced[6].astype(jnp.bfloat16), "dp", scatter_dimension=0, tiled=True
        ).astype(jnp.float32),
    )
    vec_part = [reduced[7 + index] for index in range(9)]
    vec_done = lax.psum(
        (
            vec_part[0],
            vec_part[1],
            vec_part[2],
            vec_part[3],
            vec_part[4],
            vec_part[5],
            vec_part[6],
            vec_part[7],
            vec_part[8],
        ),
        "dp",
    )
    mats = [piece.reshape(-1) for piece in mat_done]
    vecs = [piece.reshape(-1) for piece in vec_done]
    return (
        output,
        grad_hidden,
        grad_encoder,
        mats[0],
        vecs[0],
        mats[1],
        vecs[1],
        mats[2],
        vecs[2],
        mats[3],
        vecs[3],
        mats[4],
        vecs[4],
        mats[5],
        vecs[5],
        mats[6],
        vecs[6],
        vecs[7],
        vecs[8],
    )


def solution(mesh):
    return jax.shard_map(
        on_device,
        mesh=mesh,
        in_specs=(
            P("dp", None, "seq", None),
            P("dp", "seq", None),
            P("dp", None, "seq", None),
            P("dp"),
            P("dp"),
            P(),
            P(),
            P(),
            P(),
            P(),
            P(),
            P(),
            P(),
            P(),
            P(),
            P(),
            P(),
            P(),
            P(),
            P(),
            P(),
        ),
        out_specs=(
            P("dp", None, "seq", None),
            P("dp", None, "seq", None),
            P("dp", "seq", None),
            P(("dp", "seq")),
            P("seq"),
            P(("dp", "seq")),
            P("seq"),
            P(("dp", "seq")),
            P("seq"),
            P(("dp", "seq")),
            P("seq"),
            P(("dp", "seq")),
            P("seq"),
            P(("dp", "seq")),
            P("seq"),
            P(("dp", "seq")),
            P("seq"),
            P("seq"),
            P("seq"),
        ),
        check_vma=False,
    )
```

profile of v0, /device:TPU:0, one launch (start us, length us, event | category | flops | bytes accessed | tf_op | source)
XLA Modules:
  0.0 3152.3 jit_solution(1102070719601090586)
XLA Ops:
  150.9 49.6 %all-gather.11.cloned.1.call-done = bf16[2,1,1024,1024]{3,2,1,0:T(8,128)(2,1)} async-done(((bf16[2,1,256,1024]{3,2,1,0:T(8,128)(2,1)}), bf16[2,1,1024,1024]{3,2,1,0:T(8,128)(2,1)}) %all-gather.11.cloned.1.call-update) | async-done | bytes 4194320 | tf_op jit(solution)/shard_map/all_gather | solution.py:215
  208.7 361.1 %while.61 = (s32[]{:T(128)}, bf16[2,3,256,16,64]{2,4,1,3,0:T(8,128)(2,1)}, f32[2,3,16,256]{3,1,2,0:T(4,128)S(1)}, bf16[2,1024,16,64]{1,3,2,0:T(8,128)(2,1)}, s32...) while((s32[]{:T(128)}, ...), condition=%wide.region_4.5_spmd, body=%wide.region_0.4_spmd.sunk | while | flops 8182998528 | bytes 378182336 | solution.py:226
  241.6 32.0 %fusion.308 = f32[256,1024,3,16]{1,3,2,0:T(8,128)} fusion(f32[3,256,16,32]{3,2,0,1:T(8,128)} %dynamic-slice_bitcast_fusion.8, s32[256,1024]{1,0:T(8,128)} %get-tuple-element.1094), kind=kOutput, calls=%fused_computation.6.clone.1 | convolution fusion | flops 4840226816 | bytes 52953088 | tf_op jit(solution)/shard_map/while/body/eval_jaxpr/sqhb,qkb->shqk/dot_general | solution.py:54
  273.6 49.3 %copy.466 = f32[256,1024,3,16]{0,1,2,3:T(8,128)} copy(f32[256,1024,3,16]{1,3,2,0:T(8,128)} %fusion.308) | data formatting | bytes 100663296 | tf_op jit(solution)/shard_map/while/body/eval_jaxpr/sqhb,qkb->shqk/dot_general | solution.py:54
  322.8 32.9 %fusion.309 = (f32[3,16,256]{2,0,1:T(4,128)S(1)}, f32[3,16,256,1024]{2,3,0,1:T(8,128)}) fusion(f32[256,1024,3,16]{0,1,2,3:T(8,128)} %copy.466, bf16[2,3,256,16,64]{2,4,1,3,0:T(8,128)(2,1)} %get-tuple-element.1182, s32[]{:T(128)S(6)} %copy.495, bf16[2,1024,16,64]{1,3,2,0:T(8,128)(2,1)} %get-tuple-element.1181, ...), kind=kOutput, calls=%fused_computation.339.clone.1 | convolution fusion | flops 1660932096 | bytes 105169920 | tf_op jit(solution)/shard_map/while/body/eval_jaxpr/sqhd,khd->shqk/dot_general | solution.py:51
  416.3 31.9 %fusion.308 = f32[256,1024,3,16]{1,3,2,0:T(8,128)} fusion(f32[3,256,16,32]{3,2,0,1:T(8,128)} %dynamic-slice_bitcast_fusion.8, s32[256,1024]{1,0:T(8,128)} %get-tuple-element.1094), kind=kOutput, calls=%fused_computation.6.clone.1 | convolution fusion | flops 4840226816 | bytes 52953088 | tf_op jit(solution)/shard_map/while/body/eval_jaxpr/sqhb,qkb->shqk/dot_general | solution.py:54
  448.3 49.0 %copy.466 = f32[256,1024,3,16]{0,1,2,3:T(8,128)} copy(f32[256,1024,3,16]{1,3,2,0:T(8,128)} %fusion.308) | data formatting | bytes 100663296 | tf_op jit(solution)/shard_map/while/body/eval_jaxpr/sqhb,qkb->shqk/dot_general | solution.py:54
  497.2 32.4 %fusion.309 = (f32[3,16,256]{2,0,1:T(4,128)S(1)}, f32[3,16,256,1024]{2,3,0,1:T(8,128)}) fusion(f32[256,1024,3,16]{0,1,2,3:T(8,128)} %copy.466, bf16[2,3,256,16,64]{2,4,1,3,0:T(8,128)(2,1)} %get-tuple-element.1182, s32[]{:T(128)S(6)} %copy.495, bf16[2,1024,16,64]{1,3,2,0:T(8,128)(2,1)} %get-tuple-element.1181, ...), kind=kOutput, calls=%fused_computation.339.clone.1 | convolution fusion | flops 1660932096 | bytes 105169920 | tf_op jit(solution)/shard_map/while/body/eval_jaxpr/sqhd,khd->shqk/dot_general | solution.py:51
  635.1 129.7 %while.62 = (s32[]{:T(128)}, bf16[2,3,256,16,64]{2,4,1,3,0:T(8,128)(2,1)}, f32[2,3,16,256]{3,1,2,0:T(4,128)S(1)}, bf16[2,1024,16,64]{1,3,2,0:T(8,128)(2,1)}, s32...) while((s32[]{:T(128)}, ...), condition=%wide.region_10.11_spmd, body=%wide.region_7.10_spmd.sunk | while | flops 3360412672 | bytes 158799984 | solution.py:255
  790.7 74.5 %multiply_convert_fusion = (bf16[1536,4096]{1,0:T(8,128)(2,1)}, f32[1536,4096]{1,0:T(8,128)}, f32[1536,4096]{1,0:T(8,128)}) fusion(f32[4096]{0:T(1024)S(1)} %copy-done.52, bf16[1024,4096]{1,0:T(8,128)(2,1)} %param.46, f32[1536,1024]{1,0:T(8,128)S(1)} %get-tuple-element.811, f32[1024]{0:T(1024)S(1)} %bitcast.727, f32[1024]{0:T(1024)S(1)} %bitcast.714, ...), kind=kOutput, calls=%fused_computation.193 | convolution fusion | flops 13308002304 | bytes 77631488 | tf_op jit(solution)/shard_map/dot_general | solution.py:263
  895.5 33.5 %fusion.217 = (bf16[4096]{0:T(1024)(128)(2,1)}, bf16[1536,4096]{1,0:T(8,128)(2,1)}) fusion(f32[1536,4096]{1,0:T(8,128)} %get-tuple-element.780, bf16[1536,1024]{1,0:T(8,128)(2,1)S(1)} %get-tuple-element.768, bf16[4096,1024]{1,0:T(8,128)(2,1)} %param.48, f32[1536,4096]{1,0:T(8,128)} %get-tuple-element.812, f32[4096]{0:T(1024)S(1)} %copy-done.52), kind=kOutput, calls=%fused_computation.347 | convolution fusion | flops 12985561088 | bytes 74473472 | tf_op jit(solution)/shard_map/rd,fd->rf/dot_general | solution.py:279
  995.0 294.6 %while.63 = (s32[]{:T(128)}, bf16[2,3,256,16,64]{2,4,1,3,0:T(8,128)(2,1)}, bf16[2,1024,16,64]{1,3,2,0:T(8,128)(2,1)}, bf16[2,1024,16,64]{1,3,2,0:T(8,128)(2,1)},...) while((s32[]{:T(128)}, ...), condition=%wide.region_21.22_spmd, body=%wide.region_19.21_spmd.sunk | while | flops 8243631104 | bytes 401958016 | solution.py:305
  1037.7 36.2 %fusion.325 = (f32[3,16,256]{2,0,1:T(4,128)S(1)}, f32[16,1024,3,256]{3,1,2,0:T(8,128)}) fusion(f32[16,1024,3,256]{3,1,2,0:T(8,128)} %fusion.324, f32[3,16,256]{2,0,1:T(4,128)S(1)} %dynamic-slice_bitcast_fusion.9, pred[1024]{0:T(1024)(128)(4,1)S(1)} %iota_compare_fusion.19, bf16[2,3,256,16,64]{2,4,1,3,0:T(8,128)(2,1)} %get-tuple-element.1242, ...), kind=kOutput, calls=%fused_computation.74.clone.1 | convolution fusion | flops 1673515008 | bytes 104433664 | tf_op jit(solution)/shard_map/while/body/eval_jaxpr/sqhd,khd->shqk/dot_general | solution.py:141
  1073.9 40.3 %fusion.326 = bf16[3,16,256,1024]{2,3,0,1:T(8,128)(2,1)} fusion(f32[16,1024,3,256]{3,1,2,0:T(8,128)} %get-tuple-element.1121, f32[16,1024,3,256]{3,1,2,0:T(8,128)} %fusion.324, f32[3,16,256]{2,0,1:T(4,128)S(1)} %get-tuple-element.1122, f32[3,16,256]{2,0,1:T(4,128)S(1)} %dynamic-slice_bitcast_fusion.9, pred[1024]{0:T(1024)(128)(4,1)S(1)} %iota_compare_fusion.19), kind=kLoop, calls=%fused_computation.76.clone.1 | loop fusion | flops 75497472 | bytes 125928448 | tf_op jit(solution)/shard_map/while/body/eval_jaxpr/convert_element_type | solution.py:145
  1184.8 36.2 %fusion.325 = (f32[3,16,256]{2,0,1:T(4,128)S(1)}, f32[16,1024,3,256]{3,1,2,0:T(8,128)}) fusion(f32[16,1024,3,256]{3,1,2,0:T(8,128)} %fusion.324, f32[3,16,256]{2,0,1:T(4,128)S(1)} %dynamic-slice_bitcast_fusion.9, pred[1024]{0:T(1024)(128)(4,1)S(1)} %iota_compare_fusion.19, bf16[2,3,256,16,64]{2,4,1,3,0:T(8,128)(2,1)} %get-tuple-element.1242, ...), kind=kOutput, calls=%fused_computation.74.clone.1 | convolution fusion | flops 1673515008 | bytes 104433664 | tf_op jit(solution)/shard_map/while/body/eval_jaxpr/sqhd,khd->shqk/dot_general | solution.py:141
  1221.0 40.2 %fusion.326 = bf16[3,16,256,1024]{2,3,0,1:T(8,128)(2,1)} fusion(f32[16,1024,3,256]{3,1,2,0:T(8,128)} %get-tuple-element.1121, f32[16,1024,3,256]{3,1,2,0:T(8,128)} %fusion.324, f32[3,16,256]{2,0,1:T(4,128)S(1)} %get-tuple-element.1122, f32[3,16,256]{2,0,1:T(4,128)S(1)} %dynamic-slice_bitcast_fusion.9, pred[1024]{0:T(1024)(128)(4,1)S(1)} %iota_compare_fusion.19), kind=kLoop, calls=%fused_computation.76.clone.1 | loop fusion | flops 75497472 | bytes 125928448 | tf_op jit(solution)/shard_map/while/body/eval_jaxpr/convert_element_type | solution.py:145
  1370.2 730.5 %while.64 = (s32[]{:T(128)}, bf16[2,3,256,16,64]{2,4,1,3,0:T(8,128)(2,1)}, bf16[2,3,256,16,64]{2,4,3,1,0:T(8,128)(2,1)}, bf16[2,3,256,16,64]{2,4,3,1,0:T(8,128)(...) while((s32[]{:T(128)}, ...), condition=%wide.region_28.29_spmd, body=%wide.region_24.28_spmd.sunk | while | flops 13862585344 | bytes 725699840 | solution.py:358
  1440.6 31.8 %fusion.341 = f32[256,1024,3,16]{1,3,2,0:T(8,128)} fusion(f32[3,256,16,32]{3,2,0,1:T(8,128)} %dynamic-slice_bitcast_fusion.10, s32[256,1024]{1,0:T(8,128)S(1)} %get-tuple-element.1144), kind=kOutput, calls=%fused_computation.124.clone.1 | convolution fusion | flops 4840226816 | bytes 52953088 | tf_op jit(solution)/shard_map/while/body/eval_jaxpr/sqhb,qkb->shqk/dot_general | solution.py:54
  1472.4 49.0 %copy.473 = f32[256,1024,3,16]{0,1,2,3:T(8,128)} copy(f32[256,1024,3,16]{1,3,2,0:T(8,128)} %fusion.341) | data formatting | bytes 100663296 | tf_op jit(solution)/shard_map/while/body/eval_jaxpr/sqhb,qkb->shqk/dot_general | solution.py:54
  1521.4 51.4 %fusion.342 = (f32[3,16,256]{2,0,1:T(4,128)S(1)}, f32[3,16,256,1024]{2,3,0,1:T(8,128)}) fusion(f32[16,1024,3,256]{3,1,2,0:T(8,128)} %fusion.340, f32[3,16,256]{2,0,1:T(4,128)S(1)} %get-tuple-element.1143, f32[256,1024,3,16]{0,1,2,3:T(8,128)} %copy.473, bf16[2,3,256,16,64]{2,4,1,3,0:T(8,128)(2,1)} %get-tuple-element.1292, s32[]{:T(128)S(6)} %copy.529, ...), kind=kOutput, calls=%fused_computation.114.clone.3 | convolution fusion | flops 1686097920 | bytes 155550720 | tf_op jit(solution)/shard_map/while/body/eval_jaxpr/sqhd,khd->shqk/dot_general | solution.py:51
  1572.8 40.2 %fusion.344 = bf16[3,16,256,1024]{2,3,0,1:T(8,128)(2,1)} fusion(f32[3,16,256,1024]{2,3,0,1:T(8,128)} %get-tuple-element.1148, f32[16,1024,3,256]{3,1,2,0:T(8,128)} %fusion.340, f32[3,16,256]{2,0,1:T(4,128)S(1)} %get-tuple-element.1149), kind=kLoop, calls=%fused_computation.116.clone.1 | loop fusion | flops 37748736 | bytes 125878272 | tf_op jit(solution)/shard_map/while/body/eval_jaxpr/convert_element_type | solution.py:95
  1664.8 31.4 copy.475
  1790.4 31.8 %fusion.341 = f32[256,1024,3,16]{1,3,2,0:T(8,128)} fusion(f32[3,256,16,32]{3,2,0,1:T(8,128)} %dynamic-slice_bitcast_fusion.10, s32[256,1024]{1,0:T(8,128)S(1)} %get-tuple-element.1144), kind=kOutput, calls=%fused_computation.124.clone.1 | convolution fusion | flops 4840226816 | bytes 52953088 | tf_op jit(solution)/shard_map/while/body/eval_jaxpr/sqhb,qkb->shqk/dot_general | solution.py:54
  1822.3 49.0 %copy.473 = f32[256,1024,3,16]{0,1,2,3:T(8,128)} copy(f32[256,1024,3,16]{1,3,2,0:T(8,128)} %fusion.341) | data formatting | bytes 100663296 | tf_op jit(solution)/shard_map/while/body/eval_jaxpr/sqhb,qkb->shqk/dot_general | solution.py:54
  1871.3 51.3 %fusion.342 = (f32[3,16,256]{2,0,1:T(4,128)S(1)}, f32[3,16,256,1024]{2,3,0,1:T(8,128)}) fusion(f32[16,1024,3,256]{3,1,2,0:T(8,128)} %fusion.340, f32[3,16,256]{2,0,1:T(4,128)S(1)} %get-tuple-element.1143, f32[256,1024,3,16]{0,1,2,3:T(8,128)} %copy.473, bf16[2,3,256,16,64]{2,4,1,3,0:T(8,128)(2,1)} %get-tuple-element.1292, s32[]{:T(128)S(6)} %copy.529, ...), kind=kOutput, calls=%fused_computation.114.clone.3 | convolution fusion | flops 1686097920 | bytes 155550720 | tf_op jit(solution)/shard_map/while/body/eval_jaxpr/sqhd,khd->shqk/dot_general | solution.py:51
  1922.6 40.2 %fusion.344 = bf16[3,16,256,1024]{2,3,0,1:T(8,128)(2,1)} fusion(f32[3,16,256,1024]{2,3,0,1:T(8,128)} %get-tuple-element.1148, f32[16,1024,3,256]{3,1,2,0:T(8,128)} %fusion.340, f32[3,16,256]{2,0,1:T(4,128)S(1)} %get-tuple-element.1149), kind=kLoop, calls=%fused_computation.116.clone.1 | loop fusion | flops 37748736 | bytes 125878272 | tf_op jit(solution)/shard_map/while/body/eval_jaxpr/convert_element_type | solution.py:95
  2014.8 31.4 copy.475
  2407.8 117.4 %reduce-scatter.30.cloned.1.call-done = bf16[8,1,131072]{2,0,1:T(8,128)(2,1)} async-done(((bf16[8,4,131072]{2,0,1:T(8,128)(2,1)}), bf16[8,1,131072]{2,0,1:T(8,128)(2,1)}) %reduce-scatter.30.cloned.1.call-update) | async-done | bytes 2097168 | tf_op jit(solution)/shard_map/reduce_scatter | solution.py:432
  2532.0 140.9 %reduce-scatter.32.cloned.1.call-done = bf16[8,1,131072]{2,0,1:T(8,128)(2,1)} async-done(((bf16[8,4,131072]{2,0,1:T(8,128)(2,1)}), bf16[8,1,131072]{2,0,1:T(8,128)(2,1)}) %reduce-scatter.32.cloned.1.call-update) | async-done | bytes 2097168 | tf_op jit(solution)/shard_map/reduce_scatter | solution.py:435
  2679.7 106.9 %reduce-scatter.26.cloned.1.call-done = bf16[8,1,98304]{2,0,1:T(8,128)(2,1)} async-done(((bf16[8,4,98304]{2,0,1:T(8,128)(2,1)}), bf16[8,1,98304]{2,0,1:T(8,128)(2,1)}) %reduce-scatter.26.cloned.1.call-update) | async-done | bytes 1572880 | tf_op jit(solution)/shard_map/reduce_scatter | solution.py:426
  2792.1 108.0 %reduce-scatter.20.cloned.1.call-done = bf16[8,1,98304]{2,0,1:T(8,128)(2,1)} async-done(((bf16[8,4,98304]{2,0,1:T(8,128)(2,1)}), bf16[8,1,98304]{2,0,1:T(8,128)(2,1)}) %reduce-scatter.20.cloned.1.call-update) | async-done | bytes 1572880 | tf_op jit(solution)/shard_map/reduce_scatter | solution.py:417
  2959.3 174.0 %all-reduce.21.cloned.1.call-done = (bf16[8,1,98304]{2,1,0:T(2,128)(2,1)}, bf16[8,1,32768]{2,1,0:T(2,128)(2,1)}, bf16[8,1,16384]{2,1,0:T(2,128)(2,1)}, bf16[8,1,...) async-done(((bf16[8,1,98304]{2,1,0:T(2,128)(2,1)}, bf16[8,1,32768]{2,1,0:T(2,128)(2,1)}, ...) | async-done | bytes 8650768
  (546 shorter events, 1500.4 us)
Async XLA Ops:
  7.2 774.2 %copy-start = (bf16[1024,1024]{1,0:T(8,128)(2,1)S(1)}, bf16[1024,1024]{1,0:T(8,128)(2,1)}, u32[]{:S(2)}) copy-start(bf16[1024,1024]{1,0:T(8,128)(2,1)} %param.44) | copy-start | bytes 6291460
  7.2 137.4 %all-gather.13.cloned.1.call-start = ((), (), s32[]{:S(2)}) async-start(), calls=%async_computation.25 | async-start | bytes 5242880 | tf_op jit(solution)/shard_map/all_gather | solution.py:214
  36.0 164.5 %all-gather.11.cloned.1.call-start = ((), (), s32[]{:S(2)}) async-start(), calls=%async_computation.24 | async-start | bytes 5242880 | tf_op jit(solution)/shard_map/all_gather | solution.py:215
  56.4 564.0 %all-gather.9.cloned.1.call-start = ((), (), s32[]{:S(2)}) async-start(), calls=%async_computation.12 | async-start | bytes 5242880 | tf_op jit(solution)/shard_map/all_gather | solution.py:246
  64.1 562.5 %all-gather.7.cloned.1.call-start = ((), (), s32[]{:S(2)}) async-start(), calls=%async_computation.11 | async-start | bytes 5242880 | tf_op jit(solution)/shard_map/all_gather | solution.py:247
  67.8 2178.6 %reduce-scatter.16.cloned.1.call-start = ((), (), s32[]{:S(2)}) async-start(), calls=%async_computation.15 | async-start | bytes 5242880 | tf_op jit(solution)/shard_map/reduce_scatter | solution.py:307
  150.9 57.9 %copy-start.90 = (s32[2]{0:T(128)S(1)}, s32[2]{0:T(128)}, u32[]{:S(2)}) copy-start(s32[2]{0:T(128)} %param.34) | copy-start | bytes 28
  789.8 75.4 %copy-start.7 = (f32[1536,1024]{1,0:T(8,128)}, f32[1536,1024]{1,0:T(8,128)S(1)}, u32[]{:S(2)}) copy-start(f32[1536,1024]{1,0:T(8,128)S(1)} %get-tuple-element.811) | copy-start | bytes 18874372
  789.8 164.5 %copy-start.31 = (f32[1536]{0:T(1024)}, f32[1536]{0:T(1024)S(1)}, u32[]{:S(2)}) copy-start(f32[1536]{0:T(1024)S(1)} %broadcast_multiply_fusion.2) | copy-start | bytes 18436
  790.6 74.6 %copy-start.35 = (f32[1536]{0:T(1024)}, f32[1536]{0:T(1024)S(1)}, u32[]{:S(2)}) copy-start(f32[1536]{0:T(1024)S(1)} %multiply_reduce_fusion.5) | copy-start | bytes 18436
  790.6 163.7 %copy-start.44 = (f32[1536]{0:T(1024)}, f32[1536]{0:T(1024)S(1)}, u32[]{:S(2)}) copy-start(f32[1536]{0:T(1024)S(1)} %fusion.175) | copy-start | bytes 18436
  790.7 74.5 %copy-start.66 = (f32[1024]{0:T(1024)S(1)}, f32[1024]{0:T(1024)}, u32[]{:S(2)}) copy-start(f32[1024]{0:T(1024)} %convert_element_type.702) | copy-start | bytes 12292
  790.7 74.5 %copy-start.83 = (bf16[4096,1024]{1,0:T(8,128)(2,1)S(1)}, bf16[4096,1024]{1,0:T(8,128)(2,1)}, u32[]{:S(2)}) copy-start(bf16[4096,1024]{1,0:T(8,128)(2,1)} %param.48) | copy-start | bytes 25165828
  895.5 33.5 %copy-start.17 = (bf16[1536,1024]{1,0:T(8,128)(2,1)}, bf16[1536,1024]{1,0:T(8,128)(2,1)S(1)}, u32[]{:S(2)}) copy-start(bf16[1536,1024]{1,0:T(8,128)(2,1)S(1)} %get-tuple-element.768) | copy-start | bytes 9437188
  929.0 25.3 copy-start.36
  1295.8 950.6 %reduce-scatter.18.cloned.1.call-start = ((), (), s32[]{:S(2)}) async-start(), calls=%async_computation.16 | async-start | bytes 5242880 | tf_op jit(solution)/shard_map/reduce_scatter | solution.py:313
  1363.0 940.9 %reduce-scatter.12.cloned.1.call-start = ((), (), s32[]{:S(2)}) async-start(), calls=%async_computation.13 | async-start | bytes 5242880 | tf_op jit(solution)/shard_map/reduce_scatter | solution.py:362
  1401.7 38.9 %copy-start.2 = (s32[256,1024]{1,0:T(8,128)}, s32[256,1024]{1,0:T(8,128)S(1)}, u32[]{:S(2)}) copy-start(s32[256,1024]{1,0:T(8,128)S(1)} %get-tuple-element.1144) | copy-start | bytes 3145732 | tf_op jit(solution)/shard_map/while
  1664.8 31.4 copy-start.3
  1751.8 38.6 %copy-start.2 = (s32[256,1024]{1,0:T(8,128)}, s32[256,1024]{1,0:T(8,128)S(1)}, u32[]{:S(2)}) copy-start(s32[256,1024]{1,0:T(8,128)S(1)} %get-tuple-element.1144) | copy-start | bytes 3145732 | tf_op jit(solution)/shard_map/while
  2014.8 31.4 copy-start.3
  2100.7 211.2 %reduce-scatter.14.cloned.1.call-start = ((), (), s32[]{:S(2)}) async-start(), calls=%async_computation.14 | async-start | bytes 5242880 | tf_op jit(solution)/shard_map/reduce_scatter | solution.py:365
  2101.5 276.1 %reduce-scatter.24.cloned.1.call-start = ((), (), s32[]{:S(2)}) async-start(), calls=%async_computation.19 | async-start | bytes 1310720 | tf_op jit(solution)/shard_map/reduce_scatter | solution.py:423
  2120.1 259.6 %reduce-scatter.28.cloned.1.call-start = ((), (), s32[]{:S(2)}) async-start(), calls=%async_computation.21 | async-start | bytes 2621440 | tf_op jit(solution)/shard_map/reduce_scatter | solution.py:429
  2133.6 249.0 %reduce-scatter.22.cloned.1.call-start = ((), (), s32[]{:S(2)}) async-start(), calls=%async_computation.18 | async-start | bytes 2621440 | tf_op jit(solution)/shard_map/reduce_scatter | solution.py:420
  2147.2 378.0 %reduce-scatter.30.cloned.1.call-start = ((), (), s32[]{:S(2)}) async-start(), calls=%async_computation.22 | async-start | bytes 10485760 | tf_op jit(solution)/shard_map/reduce_scatter | solution.py:432
  2191.3 481.6 %reduce-scatter.32.cloned.1.call-start = ((), (), s32[]{:S(2)}) async-start(), calls=%async_computation.23 | async-start | bytes 10485760 | tf_op jit(solution)/shard_map/reduce_scatter | solution.py:435
  2233.7 552.9 %reduce-scatter.26.cloned.1.call-start = ((), (), s32[]{:S(2)}) async-start(), calls=%async_computation.20 | async-start | bytes 7864320 | tf_op jit(solution)/shard_map/reduce_scatter | solution.py:426
  2280.5 619.6 %reduce-scatter.20.cloned.1.call-start = ((), (), s32[]{:S(2)}) async-start(), calls=%async_computation.17 | async-start | bytes 7864320 | tf_op jit(solution)/shard_map/reduce_scatter | solution.py:417
  2363.3 769.9 %all-reduce.21.cloned.1.call-start = ((), (), s32[]{:S(2)}) async-start(), calls=%async_computation.26 | async-start | bytes 34603008
  2906.1 28.0 copy-start.87
  2954.4 191.1 %copy-start.1 = (bf16[1024,1024]{1,0:T(8,128)(2,1)S(1)}, bf16[1024,1024]{1,0:T(8,128)(2,1)}, u32[]{:S(2)}) copy-start(bf16[1024,1024]{1,0:T(8,128)(2,1)} %param.44) | copy-start | bytes 6291460
  (83 other events, 658.5 us)
Sparse Core Ops, SparseCore 0:
  36.1 83.4 all-gather.12
  121.2 79.2 all-gather.10
  202.1 79.2 all-gather.8
  283.4 79.2 all-gather.6
  1295.9 75.2 reduce-scatter.15
  1373.5 77.2 reduce-scatter.17
  2100.9 75.9 reduce-scatter.11
  2179.3 77.2 reduce-scatter.13
  2259.5 27.6 reduce-scatter.23
  2289.4 42.5 reduce-scatter.27
  2334.3 43.1 reduce-scatter.21
  2379.8 145.3 reduce-scatter.29
  2527.7 145.1 reduce-scatter.31
  2675.1 111.4 reduce-scatter.25
  2788.8 111.2 reduce-scatter.19
  2906.6 226.6 all-reduce.20
where the time goes:
time: 3170 us; the launch traced here: 3150 us
  matrix products  1130 us (36%)
  local copies, waits for them, and re-layouts  847 us (27%)
  waiting for transfers between devices  698 us (22%)
  other arithmetic  371 us (12%)
  blocking collectives  45.8 us (1%)
  loops' own time  43.7 us (1%)
    dot_general x4, local copies, waits for them, and re-layouts, self_logits(): jnp.einsum('sqhb,qkb->shqk', rel_s, one_hot, precision=HIGHEST)  196 us
    unnamed x17, waiting for transfers between devices  175 us
    dot_general x4, matrix products, self_logits(): jnp.einsum('sqhd,khd->shqk', query_s, keys_s, preferred_element_type=jnp....  168 us
    reduce_scatter x1, waiting for transfers between devices, on_device(): lax.psum_scatter(mat_blocks[6].astype(jnp.bfloat16), 'seq', scatter_dimen...  141 us
    dot_general x4, matrix products, self_logits(): jnp.einsum('sqhb,qkb->shqk', rel_s, one_hot, precision=HIGHEST)  128 us
    reduce_scatter x1, waiting for transfers between devices, on_device(): lax.psum_scatter(mat_blocks[5].astype(jnp.bfloat16), 'seq', scatter_dimen...  117 us
    reduce_scatter x1, waiting for transfers between devices, on_device(): lax.psum_scatter(mat_blocks[0].astype(jnp.bfloat16), 'seq', scatter_dimen...  108 us
    reduce_scatter x1, waiting for transfers between devices, on_device(): lax.psum_scatter(mat_blocks[3].astype(jnp.bfloat16), 'seq', scatter_dimen...  107 us
  transfers between devices with their start and end apart: 16, of which 6 were waited for; matrix products, arithmetic and copies ran while one was open for 52% of the time, Pallas kernels for 0%

commit v1 on v0

--- a/solution.py
+++ b/solution.py
@@ -1,18 +1,426 @@
+import functools
 import math
 
 import jax
 import jax.numpy as jnp
+import numpy as np
 from jax import lax
+from jax.experimental import pallas as pl
+from jax.experimental.pallas import tpu as pltpu
 from jax.sharding import PartitionSpec as P
 
 HEADS = 16
 BUCKETS = 32
 MAX_DIST = 128
-
-
-HIGHEST = lax.Precision.HIGHEST
-negative = -1e30
-epsilon = 1e-05
+SIZE = 64
+SCALE = 0.125
+TILE = 128
+NEGATIVE = -1e30
+EPSILON = 1e-05
+VMEM_LIMIT = 56 * 2**20
+
+low_type = jnp.bfloat16
+high_type = jnp.float32
+
+
+def contract(left, right, left_dim, right_dim):
+    return lax.dot_general(
+        left, right, (((left_dim,), (right_dim,)), ((), ())), preferred_element_type=high_type
+    )
+
+
+def split_two(value):
+    top = value.astype(low_type)
+    return top, (value - top.astype(high_type)).astype(low_type)
+
+
+def feature_rows(first, value):
+    a = value.astype(low_type).astype(high_type)
+    b = (value - a).astype(low_type).astype(high_type)
+    c = value - a - b
+    count = value.shape[1]
+    at = lax.broadcasted_iota(jnp.int32, (16, count), 0)
+    out = jnp.where(at == 0, first, 0.0)
+    for index, piece in enumerate((a, b, c)):
+        out = jnp.where(at == index + 1, piece, out)
+    return out.astype(low_type)
+
+
+def key_features(valid):
+    mask = jnp.where(valid, 0.0, NEGATIVE)[:, None, :]
+    ones = jnp.ones_like(mask)
+    return jnp.concatenate([mask, ones, ones, ones] + [jnp.zeros_like(mask)] * 12, 1).astype(
+        low_type
+    )
+
+
+def bucket_table():
+    half = BUCKETS // 2
+    distance = (TILE - np.arange(2 * TILE)) % (2 * TILE)
+    counted = np.zeros_like(distance)
+    for level in range(1, half):
+        counted = counted + (distance >= math.ceil(half * (MAX_DIST / half) ** (level / half)))
+    bucket = np.where(distance < half, distance, half + counted)
+    table = (bucket[None, :] == np.arange(BUCKETS)[:, None]).astype(np.float32)
+    table[BUCKETS - 1] = -(bucket < BUCKETS - 1).astype(np.float32)
+    return table
+
+
+def near_bias(rel, table):
+    top, rest = split_two(rel)
+    return contract(
+        jnp.concatenate([top, rest], 0), jnp.concatenate([table, table], 0), 0, 0
+    )
+
+
+def cross_forward_kernel(q_ref, k_ref, v_ref, mark_ref, o_ref, total_ref):
+    count, keys = q_ref.shape[1], k_ref.shape[1]
+    k1 = jnp.concatenate([k_ref[...], mark_ref[...]], 0)
+    v1 = jnp.concatenate([v_ref[...], jnp.ones((16, keys), low_type)], 0)
+    zero = jnp.zeros((1, count), high_type)
+    q1 = jnp.concatenate([q_ref[...], feature_rows(1.0, zero)], 0)
+    scores = contract(k1, q1, 0, 0)
+    peak = jnp.max(scores, 0, keepdims=True)
+    weights = jnp.exp(scores - peak).astype(low_type)
+    mixed = contract(v1, weights, 1, 0)
+    total = mixed[SIZE : SIZE + 1]
+    o_ref[...] = (mixed[:SIZE] * (1.0 / total)).astype(low_type)
+    total_ref[...] = peak + jnp.log(total)
+
+
+def cross_backward_kernel(
+    q_ref, k_ref, v_ref, mark_ref, o_ref, total_ref, do_ref, dq_ref, dk_ref, dv_ref, dk_acc, dv_acc, *, step
+):
+    count, keys = q_ref.shape[1], k_ref.shape[1]
+    k = k_ref[...]
+    k1 = jnp.concatenate([k, mark_ref[...]], 0)
+    v1 = jnp.concatenate([v_ref[...], mark_ref[...]], 0)
+    for n in range(0, count, step):
+        q, do = q_ref[:, n : n + step], do_ref[:, n : n + step]
+        delta = jnp.sum(
+            do.astype(high_type) * o_ref[:, n : n + step].astype(high_type), 0, keepdims=True
+        )
+        q1 = jnp.concatenate([q, feature_rows(1.0, -total_ref[:, n : n + step])], 0)
+        do1 = jnp.concatenate([do, feature_rows(0.0, -delta)], 0)
+        weights = jnp.exp(contract(q1, k1, 0, 0))
+        grad_scores = (weights * contract(do1, v1, 0, 0)).astype(low_type)
+        weights = weights.astype(low_type)
+        dq_ref[:, n : n + step] = (contract(k, grad_scores, 1, 1) * SCALE).astype(low_type)
+        dk = contract(q, grad_scores, 1, 0)
+        dv = contract(do, weights, 1, 0)
+        if n == 0:
+            dk_acc[...] = dk
+            dv_acc[...] = dv
+        else:
+            dk_acc[...] += dk
+            dv_acc[...] += dv
+    dk_ref[...] = dk_acc[...].astype(low_type)
+    dv_ref[...] = dv_acc[...].astype(low_type)
+
+
+def self_forward_kernel(q_ref, k_ref, v_ref, rel_ref, mark_ref, table_ref, o_ref, total_ref, *, T, S):
+    n, tile = S * T, min(TILE, T)
+    keys = k_ref.shape[1] - n + T
+    q, rel = q_ref[...], rel_ref[...]
+    k1 = jnp.concatenate([k_ref[:, :keys], mark_ref[...]], 0)
+    v1 = jnp.concatenate([v_ref[:, :keys], jnp.ones((16, keys), low_type)], 0)
+    q1 = jnp.concatenate([q, feature_rows(1.0, rel[BUCKETS - 1 :])], 0)
+    scores = contract(q1, k1, 0, 0)
+    near = near_bias(rel, table_ref[...])
+    at = lax.broadcasted_iota(jnp.int32, (tile, tile), 0)
+    to = lax.broadcasted_iota(jnp.int32, (tile, tile), 1)
+    weights, peaks = [], []
+    for s in range(S):
+        for r in range(T // tile):
+            row, first = s * T + r * tile, keys - T + r * tile - TILE
+            bias = pltpu.roll(near[row : row + tile], 0, 1, stride=1, stride_axis=0)
+            block = scores[row : row + tile]
+            left = block[:, first : first + TILE] + bias[:, :TILE]
+            right = block[:, first + TILE : first + TILE + tile] + bias[:, TILE : TILE + tile]
+            right = jnp.where((to <= at) if s == 0 else (to < at), right, NEGATIVE)
+            parts = [left, right]
+            peak = jnp.max(
+                jnp.maximum(left, right) if tile == TILE else jnp.concatenate(parts, 1),
+                1,
+                keepdims=True,
+            )
+            if first > 0:
+                far = block[:, :first]
+                peak = jnp.maximum(peak, jnp.max(far, 1, keepdims=True))
+                parts = [far] + parts
+            parts = [jnp.exp(part - peak).astype(low_type) for part in parts]
+            if first + TILE + tile < keys:
+                parts.append(jnp.zeros((tile, keys - first - TILE - tile), low_type))
+            weights.append(jnp.concatenate(parts, 1))
+            peaks.append(jnp.broadcast_to(peak, (tile, tile)).T[0:1])
+    mixed = contract(v1, jnp.concatenate(weights, 0), 1, 1)
+    peak = jnp.concatenate(peaks, 1)
+    total, mixed = mixed[SIZE : SIZE + 1], mixed[:SIZE]
+    own_k = k_ref[:, keys:].astype(high_type)
+    own_v = v_ref[:, keys:].astype(high_type)
+    own = jnp.sum(q[:, T:].astype(high_type) * own_k, 0, keepdims=True) + rel[0:1, T:]
+    top = jnp.maximum(peak[:, T:], own)
+    main_part, own_part = jnp.exp(peak[:, T:] - top), jnp.exp(own - top)
+    joined = total[:, T:] * main_part + own_part
+    inverse = 1.0 / joined
+    o_ref[:, :T] = (mixed[:, :T] * (1.0 / total[:, :T])).astype(low_type)
+    o_ref[:, T:] = (mixed[:, T:] * (main_part * inverse) + own_v * (own_part * inverse)).astype(
+        low_type
+    )
+    total_ref[:, :T] = peak[:, :T] + jnp.log(total[:, :T])
+    total_ref[:, T:] = top + jnp.log(joined)
+
+
+def self_backward_kernel(
+    q_ref,
+    k_ref,
+    v_ref,
+    rel_ref,
+    mark_ref,
+    table_ref,
+    o_ref,
+    total_ref,
+    do_ref,
+    dq_ref,
+    dk_ref,
+    dv_ref,
+    drel_ref,
+    *,
+    T,
+    S,
+):
+    n, tile = S * T, min(TILE, T)
+    keys = k_ref.shape[1] - n + T
+    q, rel, do, total = q_ref[...], rel_ref[...], do_ref[...], total_ref[...]
+    table = table_ref[...]
+    k1 = jnp.concatenate([k_ref[:, :keys], mark_ref[...]], 0)
+    v1 = jnp.concatenate([v_ref[:, :keys], mark_ref[...]], 0)
+    do_high = do.astype(high_type)
+    delta = jnp.sum(do_high * o_ref[...].astype(high_type), 0, keepdims=True)
+    q1 = jnp.concatenate([q, feature_rows(1.0, rel[BUCKETS - 1 :] - total)], 0)
+    do1 = jnp.concatenate([do, feature_rows(0.0, -delta)], 0)
+    scores = contract(q1, k1, 0, 0)
+    slopes = contract(do1, v1, 0, 0)
+    near = near_bias(rel, table)
+    at = lax.broadcasted_iota(jnp.int32, (tile, tile), 0)
+    to = lax.broadcasted_iota(jnp.int32, (tile, tile), 1)
+    mirror = (at + to == tile - 1).astype(high_type).astype(low_type)
+    weights, grads, rels = [], [], []
+    for s in range(S):
+        for r in range(T // tile):
+            row, first = s * T + r * tile, keys - T + r * tile - TILE
+            bias = pltpu.roll(near[row : row + tile], 0, 1, stride=1, stride_axis=0)
+            block, slope = scores[row : row + tile], slopes[row : row + tile]
+            left = block[:, first : first + TILE] + bias[:, :TILE]
+            right = block[:, first + TILE : first + TILE + tile] + bias[:, TILE : TILE + tile]
+            right = jnp.where((to <= at) if s == 0 else (to < at), right, NEGATIVE)
+            part = jnp.exp(jnp.concatenate([left, right], 1))
+            grad = (part * slope[:, first : first + TILE + tile]).astype(low_type)
+            turned = contract(mirror, grad, 1, 0)
+            if tile < TILE:
+                turned = jnp.concatenate([turned, jnp.zeros((tile, TILE - tile), high_type)], 1)
+            turned = pltpu.roll(turned, 2 * TILE - tile + 1, 1, stride=1, stride_axis=0)
+            turned = turned.astype(low_type)
+            top, rest = split_two(contract(table, turned, 1, 1))
+            both = contract(jnp.concatenate([top, rest], 0), mirror, 1, 0)
+            rels.append(both[:BUCKETS] + both[BUCKETS:])
+            parts, pieces = [part.astype(low_type)], [grad]
+            if first > 0:
+                part = jnp.exp(block[:, :first])
+                pieces = [(part * slope[:, :first]).astype(low_type)] + pieces
+                parts = [part.astype(low_type)] + parts
+            if first + TILE + tile < keys:
+                zero = jnp.zeros((tile, keys - first - TILE - tile), low_type)
+                parts.append(zero)
+                pieces.append(zero)
+            weights.append(jnp.concatenate(parts, 1))
+            grads.append(jnp.concatenate(pieces, 1))
+    weights, grads = jnp.concatenate(weights, 0), jnp.concatenate(grads, 0)
+    dq = contract(k1, grads, 1, 1)
+    dk_ref[:, :keys] = contract(q, grads, 1, 0).astype(low_type)
+    dv_ref[:, :keys] = contract(do, weights, 1, 0).astype(low_type)
+    row_sums = dq[SIZE + 1 : SIZE + 2]
+    own_k = k_ref[:, keys:].astype(high_type)
+    own_v = v_ref[:, keys:].astype(high_type)
+    own_q, own_do = q[:, T:].astype(high_type), do_high[:, T:]
+    own = jnp.sum(own_q * own_k, 0, keepdims=True) + rel[0:1, T:]
+    own_part = jnp.exp(own - total[:, T:])
+    own_grad = own_part * (jnp.sum(own_do * own_v, 0, keepdims=True) - delta[:, T:])
+    own_grad = own_grad.astype(low_type).astype(high_type)
+    dq_ref[:, :T] = (dq[:SIZE, :T] * SCALE).astype(low_type)
+    dq_ref[:, T:] = ((dq[:SIZE, T:] + own_grad * own_k) * SCALE).astype(low_type)
+    dk_ref[:, keys:] = (own_grad * own_q).astype(low_type)
+    dv_ref[:, keys:] = (own_part.astype(low_type).astype(high_type) * own_do).astype(low_type)
+    bucket = lax.broadcasted_iota(jnp.int32, (BUCKETS, n), 0)
+    drel = jnp.concatenate(rels, 1) + jnp.where(bucket == BUCKETS - 1, row_sums, 0.0)
+    own_all = jnp.concatenate([jnp.zeros((1, T), high_type), own_grad], 1)
+    drel_ref[...] = (drel + jnp.where(bucket == 0, own_all, 0.0)).astype(low_type)
+
+
+def per_head(rows, count):
+    return pl.BlockSpec((rows, count), lambda b, h: (h, b))
+
+
+def per_sequence(keys):
+    return pl.BlockSpec((None, 16, keys), lambda b, h: (b, 0, 0))
+
+
+def per_total(count):
+    return pl.BlockSpec((None, None, 1, count), lambda b, h: (b, h, 0, 0))
+
+
+def like(array):
+    return jax.ShapeDtypeStruct(array.shape, low_type)
+
+
+def cost(B, rows, keys, products):
+    return pl.CostEstimate(
+        flops=2 * B * HEADS * rows * keys * 256 * products,
+        bytes_accessed=B * HEADS * SIZE * (rows + keys) * 4 * products,
+        transcendentals=B * HEADS * rows * keys,
+    )
+
+
+def cross_forward(q, k, v, mark):
+    B, _, keys = mark.shape
+    count = q.shape[1] // B
+    return pl.pallas_call(
+        cross_forward_kernel,
+        grid=(B, HEADS),
+        in_specs=[per_head(SIZE, count), per_head(SIZE, keys), per_head(SIZE, keys), per_sequence(keys)],
+        out_specs=[per_head(SIZE, count), per_total(count)],
+        out_shape=[like(q), jax.ShapeDtypeStruct((B, HEADS, 1, count), high_type)],
+        cost_estimate=cost(B, count, keys, 2),
+        compiler_params=pltpu.CompilerParams(vmem_limit_bytes=VMEM_LIMIT),
+        name="cross_forward",
+    )(q, k, v, mark)
+
+
+def cross_backward(q, k, v, mark, o, total, do):
+    B, _, keys = mark.shape
+    count = q.shape[1] // B
+    row, key = per_head(SIZE, count), per_head(SIZE, keys)
+    return pl.pallas_call(
+        functools.partial(cross_backward_kernel, step=count // 2),
+        grid=(B, HEADS),
+        in_specs=[row, key, key, per_sequence(keys), row, per_total(count), row],
+        out_specs=[row, key, key],
+        out_shape=[like(q), like(k), like(v)],
+        scratch_shapes=[pltpu.VMEM((SIZE, keys), high_type)] * 2,
+        cost_estimate=cost(B, count, keys, 5),
+        compiler_params=pltpu.CompilerParams(vmem_limit_bytes=VMEM_LIMIT),
+        name="cross_backward",
+    )(q, k, v, mark, o, total, do)
+
+
+def self_forward(q, k, v, rel, mark, table, T, S):
+    B, _, keys = mark.shape
+    count = S * T
+    row, key, rels = per_head(SIZE, count), per_head(SIZE, keys + count - T), per_head(BUCKETS, count)
+    return pl.pallas_call(
+        functools.partial(self_forward_kernel, T=T, S=S),
+        grid=(B, HEADS),
+        in_specs=[row, key, key, rels, per_sequence(keys), pl.BlockSpec(table.shape, lambda b, h: (0, 0))],
+        out_specs=[row, per_total(count)],
+        out_shape=[like(q), jax.ShapeDtypeStruct((B, HEADS, 1, count), high_type)],
+        cost_estimate=cost(B, count, keys, 2),
+        compiler_params=pltpu.CompilerParams(vmem_limit_bytes=VMEM_LIMIT),
+        name="self_forward",
+    )(q, k, v, rel, mark, table)
+
+
+def self_backward(q, k, v, rel, mark, table, o, total, do, T, S):
+    B, _, keys = mark.shape
+    count = S * T
+    row, key, rels = per_head(SIZE, count), per_head(SIZE, keys + count - T), per_head(BUCKETS, count)
+    return pl.pallas_call(
+        functools.partial(self_backward_kernel, T=T, S=S),
+        grid=(B, HEADS),
+        in_specs=[
+            row,
+            key,
+            key,
+            rels,
+            per_sequence(keys),
+            pl.BlockSpec(table.shape, lambda b, h: (0, 0)),
+            row,
+            per_total(count),
+            row,
+        ],
+        out_specs=[row, key, key, rels],
+        out_shape=[like(q), like(k), like(v), like(rel)],
+        cost_estimate=cost(B, count, keys, 5),
+        compiler_params=pltpu.CompilerParams(vmem_limit_bytes=VMEM_LIMIT),
+        name="self_backward",
+    )(q, k, v, rel, mark, table, o, total, do)
+
+
+def ffn_kernel(x_ref, w_ref, b_ref, g_ref, slope_ref):
+    u = contract(x_ref[...], w_ref[...], 1, 0) + b_ref[...]
+    z = jnp.abs(u) * (0.5**0.5)
+    t = 1.0 / (1.0 + 0.3275911 * z)
+    bell = jnp.exp(-z * z)
+    poly = t * (
+        0.254829592
+        + t * (-0.284496736 + t * (1.421413741 + t * (-1.453152027 + t * 1.061405429)))
+    )
+    tail = 0.5 * poly * bell
+    phi = jnp.where(u < 0.0, tail, 1.0 - tail)
+    g_ref[...] = (u * phi).astype(low_type)
+    slope_ref[...] = (phi + u * (bell * (2.0 * math.pi) ** -0.5)).astype(low_type)
+
+
+def ffn_first(x, w, b):
+    rows, width = x.shape
+    hidden = w.shape[1]
+    tm, tn = math.gcd(rows, 512), math.gcd(hidden, 1024)
+    block = pl.BlockSpec((tm, tn), lambda j, i: (i, j))
+    out = jax.ShapeDtypeStruct((rows, hidden), low_type)
+    return pl.pallas_call(
+        ffn_kernel,
+        grid=(hidden // tn, rows // tm),
+        in_specs=[
+            pl.BlockSpec((tm, width), lambda j, i: (i, 0)),
+            pl.BlockSpec((width, tn), lambda j, i: (0, j)),
+            pl.BlockSpec((1, tn), lambda j, i: (0, j)),
+        ],
+        out_specs=[block, block],
+        out_shape=[out, out],
+        cost_estimate=pl.CostEstimate(
+            flops=2 * rows * width * hidden, bytes_accessed=4 * rows * hidden, transcendentals=rows * hidden
+        ),
+        compiler_params=pltpu.CompilerParams(vmem_limit_bytes=VMEM_LIMIT),
+        name="ffn_first",
+    )(x, w, b)
+
+
+def column_sum(value):
+    return jnp.sum(value.astype(high_type), 0)
+
+
+def row_sum(value):
+    return jnp.sum(value.astype(high_type), 1)
+
+
+def dot(spec, left, right):
+    return jnp.einsum(spec, left, right, preferred_element_type=high_type)
+
+
+def norm_parts(value):
+    center = value - jnp.mean(value, -1, keepdims=True)
+    inverse = lax.rsqrt(jnp.mean(center * center, -1, keepdims=True) + EPSILON)
+    return center * inverse, inverse
+
+
+def norm_back(value, grad, gain):
+    unit, inverse = norm_parts(value)
+    scaled = grad * gain
+    back = inverse * (
+        scaled
+        - jnp.mean(scaled, -1, keepdims=True)
+        - unit * jnp.mean(scaled * unit, -1, keepdims=True)
+    )
+    return back, jnp.sum(grad * unit, 0), jnp.sum(grad, 0)
 
 
 def rounded(value):
@@ -22,7 +430,7 @@
 def layer_norm(value, gain, shift):
     center = value - jnp.mean(value, -1, keepdims=True)
     spread = jnp.mean(center * center, -1, keepdims=True)
-    return center * lax.rsqrt(spread + epsilon) * gain + shift
+    return center * lax.rsqrt(spread + EPSILON) * gain + shift
 
 
 def gelu_exact(value):
@@ -51,22 +459,22 @@
     scores = scale * jnp.einsum(
         "sqhd,khd->shqk", query_s, keys_s, preferred_element_type=jnp.float32
     )
-    scores = scores + jnp.einsum("sqhb,qkb->shqk", rel_s, one_hot, precision=HIGHEST)
+    scores = scores + jnp.einsum("sqhb,qkb->shqk", rel_s, one_hot, precision=lax.Precision.HIGHEST)
     stream_ids = jnp.arange(streams, dtype=jnp.int32)
     allowed = (distance[None] >= jnp.minimum(stream_ids, 1)[:, None, None]) & (
         key_positions < dec_len
     )[None, None, :]
-    scores = jnp.where(allowed[:, None], scores, negative)
+    scores = jnp.where(allowed[:, None], scores, NEGATIVE)
     own_score = (
         scale * jnp.sum(query_s.astype(jnp.float32) * key_s.astype(jnp.float32), -1) + rel_s[..., 0]
     )
     own_score = jnp.where(
-        (stream_ids > 0)[:, None, None], jnp.transpose(own_score, (0, 2, 1)), negative
+        (stream_ids > 0)[:, None, None], jnp.transpose(own_score, (0, 2, 1)), NEGATIVE
     )
     return (scores, own_score, one_hot)
 
 
-def self_forward(items, offset_pos):
+def plain_self_forward(items, offset_pos):
     query_s, key_s, value_s, rel_s, keys_s, values_s, dec_len = items
     scores, own_score, one_hot = self_logits(query_s, key_s, rel_s, keys_s, dec_len, offset_pos)
     peak = jnp.maximum(jnp.max(scores, -1), own_score)
@@ -80,7 +488,7 @@
     return (mixed.astype(jnp.bfloat16), log_total)
 
 
-def self_backward(items, offset_pos):
+def plain_self_backward(items, offset_pos):
     query_s, key_s, value_s, rel_s, keys_s, values_s, dec_len, log_total, grad_s = items
     scores, own_score, one_hot = self_logits(query_s, key_s, rel_s, keys_s, dec_len, offset_pos)
     scale = query_s.shape[3] ** (-0.5)
@@ -108,7 +516,7 @@
     )
     grad_value_own = jnp.transpose(rounded(own_weight), (0, 2, 1))[..., None] * grad_float
     grad_rel = jnp.einsum(
-        "shqk,qkb->sqhb", grad_scores.astype(jnp.float32), one_hot, precision=HIGHEST
+        "shqk,qkb->sqhb", grad_scores.astype(jnp.float32), one_hot, precision=lax.Precision.HIGHEST
     )
     grad_rel = grad_rel.at[..., 0].add(jnp.transpose(grad_own_score, (0, 2, 1)))
     return (grad_query, grad_key_own, grad_value_own, grad_keys, grad_values, grad_rel)
@@ -120,10 +528,10 @@
         "sqhd,khd->shqk", query_s, keys_s, preferred_element_type=jnp.float32
     )
     key_positions = jnp.arange(keys_s.shape[0], dtype=jnp.int32)
-    return jnp.where(key_positions < enc_len, scores, negative)
-
-
-def cross_forward(items):
+    return jnp.where(key_positions < enc_len, scores, NEGATIVE)
+
+
+def plain_cross_forward(items):
     query_s, keys_s, values_s, enc_len = items
     scores = cross_logits(query_s, keys_s, enc_len)
     peak = jnp.max(scores, -1)
@@ -133,7 +541,7 @@
     return (mixed.astype(jnp.bfloat16), log_total)
 
 
-def cross_backward(items):
+def plain_cross_backward(items):
     query_s, keys_s, values_s, enc_len, log_total, grad_s = items
     scale = query_s.shape[3] ** (-0.5)
     scores = cross_logits(query_s, keys_s, enc_len)
@@ -155,11 +563,7 @@
     return (grad_query, grad_keys, grad_values)
 
 
-def column_sum(value):
-    return jnp.sum(value.astype(jnp.float32), 0)
-
-
-def on_device(
+def plain_on_device(
     hidden,
     encoder_out,
     cotangent,
@@ -182,8 +586,6 @@
     norm_gain,
     norm_bias,
 ):
-    low_type = jnp.bfloat16
-    high_type = jnp.float32
     seq_count, streams, local_len, width = hidden.shape
     seq_parts = lax.axis_size("seq")
     dp_parts = lax.axis_size("dp")
@@ -223,7 +625,7 @@
         values_all.reshape(all_shape),
         dec_lengths,
     )
-    attended, self_total = lax.map(lambda items: self_forward(items, offset_pos), self_items)
+    attended, self_total = lax.map(lambda items: plain_self_forward(items, offset_pos), self_items)
     attended = attended.reshape(row_count, width)
     self_branch = jnp.dot(
         attended, self_out, preferred_element_type=high_type
@@ -252,7 +654,7 @@
         cross_values.reshape(all_shape),
         enc_lengths,
     )
-    cross_mixed, cross_total = lax.map(cross_forward, cross_items)
+    cross_mixed, cross_total = lax.map(plain_cross_forward, cross_items)
     cross_mixed = cross_mixed.reshape(row_count, width)
     cross_branch = jnp.dot(
         cross_mixed, cross_out, preferred_element_type=high_type
@@ -302,7 +704,7 @@
         cross_total,
         grad_cross_mixed.reshape(head_shape),
     )
-    grad_cross_query, grad_cross_keys, grad_cross_values = lax.map(cross_backward, cross_back_items)
+    grad_cross_query, grad_cross_keys, grad_cross_values = lax.map(plain_cross_backward, cross_back_items)
     cross_key_sum, cross_value_sum = (
         lax.psum_scatter(
             grad_cross_keys.reshape(kv_shape).astype(jnp.bfloat16),
@@ -356,7 +758,7 @@
         grad_attended.reshape(head_shape),
     )
     grad_query, grad_key_own, grad_value_own, grad_keys, grad_values, grad_rel = lax.map(
-        lambda items: self_backward(items, offset_pos), self_back_items
+        lambda items: plain_self_backward(items, offset_pos), self_back_items
     )
     key_sum, value_sum = (
         lax.psum_scatter(
@@ -526,53 +928,244 @@
     )
 
 
+def on_device(
+    hidden,
+    encoder_out,
+    cotangent,
+    dec_lengths,
+    enc_lengths,
+    self_qkv,
+    self_qv_bias,
+    self_out,
+    self_out_bias,
+    rel_weight,
+    rel_bias,
+    cross_qkv,
+    cross_qv_bias,
+    cross_out,
+    cross_out_bias,
+    ffn_in,
+    ffn_in_bias,
+    ffn_out,
+    ffn_out_bias,
+    norm_gain,
+    norm_bias,
+):
+    B, S, T, width = hidden.shape
+    if T % TILE:
+        return plain_on_device(
+            hidden,
+            encoder_out,
+            cotangent,
+            dec_lengths,
+            enc_lengths,
+            self_qkv,
+            self_qv_bias,
+            self_out,
+            self_out_bias,
+            rel_weight,
+            rel_bias,
+            cross_qkv,
+            cross_qv_bias,
+            cross_out,
+            cross_out_bias,
+            ffn_in,
+            ffn_in_bias,
+            ffn_out,
+            ffn_out_bias,
+            norm_gain,
+            norm_bias,
+        )
+    seq_parts = lax.axis_size("seq")
+    keys = T * seq_parts
+    far = keys - T
+    place = lax.axis_index("seq")
+    up = [(i, i + 1) for i in range(seq_parts - 1)]
+    down = [(i + 1, i) for i in range(seq_parts - 1)]
+    gains, shifts = norm_gain.astype(high_type), norm_bias.astype(high_type)
+    self_bias, cross_bias = self_qv_bias.astype(high_type), cross_qv_bias.astype(high_type)
+    table = jnp.asarray(bucket_table(), low_type)
+
+    x = hidden.reshape(B * S * T, width)
+    rows = B * S * T
+    moving, pieces = hidden[:, 0], []
+    for _ in range(seq_parts - 1):
+        moving = lax.ppermute(moving, "seq", up)
+        pieces.append(moving)
+    x_all = jnp.concatenate(pieces[::-1] + [hidden.reshape(B, S * T, width)], 1)
+    x_keys = x_all.reshape(-1, width)
+    key_at = place * T - far + jnp.arange(keys, dtype=jnp.int32)
+    self_mark = key_features((key_at >= 0) & (key_at < dec_lengths[:, None]))
+    cross_mark = key_features(jnp.arange(keys, dtype=jnp.int32) < enc_lengths[:, None])
+
+    q = ((dot("de,rd->er", self_qkv[0], x) + self_bias[0][:, None]) * SCALE).astype(low_type)
+    rel = dot("db,rd->br", rel_weight, x) + rel_bias.astype(high_type)[:, None]
+    k = dot("de,rd->er", self_qkv[1], x_keys).astype(low_type)
+    v = (dot("de,rd->er", self_qkv[2], x_keys) + self_bias[1][:, None]).astype(low_type)
+    attended, self_total = self_forward(q, k, v, rel, self_mark, table, T, S)
+    first_sum = (
+        x.astype(high_type)
+        + dot("er,ed->rd", attended, self_out)
+        + self_out_bias.astype(high_type)
+    )
+    first_unit, _ = norm_parts(first_sum)
+    first_norm = first_unit * gains[0] + shifts[0]
+    first_low = first_norm.astype(low_type)
+
+    e_all = lax.all_gather(encoder_out, "seq", axis=1, tiled=True).reshape(-1, width)
+    qc = ((dot("de,rd->er", cross_qkv[0], first_low) + cross_bias[0][:, None]) * SCALE).astype(
+        low_type
+    )
+    kc = dot("de,rd->er", cross_qkv[1], e_all).astype(low_type)
+    vc = (dot("de,rd->er", cross_qkv[2], e_all) + cross_bias[1][:, None]).astype(low_type)
+    cross_mixed, cross_total = cross_forward(qc, kc, vc, cross_mark)
+    second_sum = (
+        first_norm
+        + dot("er,ed->rd", cross_mixed, cross_out)
+        + cross_out_bias.astype(high_type)
+    )
+    second_unit, _ = norm_parts(second_sum)
+    second_norm = second_unit * gains[1] + shifts[1]
+    second_low = second_norm.astype(low_type)
+
+    activated, slope = ffn_first(second_low, ffn_in, ffn_in_bias.astype(high_type)[None])
+    third_sum = (
+        second_norm + dot("rf,fd->rd", activated, ffn_out) + ffn_out_bias.astype(high_type)
+    )
+    third_unit, _ = norm_parts(third_sum)
+    output = (third_unit * gains[2] + shifts[2]).astype(low_type).reshape(hidden.shape)
+
+    grad_third, grad_gain_ffn, grad_shift_ffn = norm_back(
+        third_sum, cotangent.reshape(rows, width).astype(high_type), gains[2]
+    )
+    grad_ffn = grad_third.astype(low_type)
+
+    def over_dp(piece):
+        return lax.psum_scatter(piece.astype(low_type), "dp", scatter_dimension=0, tiled=True)
+
+    def over_seq(piece):
+        return (
+            lax.psum_scatter(piece, "seq", scatter_dimension=0, tiled=True)
+            .astype(high_type)
+            .reshape(-1)
+        )
+
+    grad_pre = (dot("rd,fd->rf", grad_ffn, ffn_out) * slope.astype(high_type)).astype(low_type)
+    mat_ffn_out = over_dp(dot("rf,rd->fd", activated, grad_ffn))
+    mat_ffn_in = over_dp(dot("rd,rf->df", second_low, grad_pre))
+    grad_second = grad_third + dot("rf,df->rd", grad_pre, ffn_in)
+    grad_second_sum, grad_gain_cross, grad_shift_cross = norm_back(
+        second_sum, grad_second, gains[1]
+    )
+    grad_cross = grad_second_sum.astype(low_type)
+    mat_cross_out = over_dp(dot("er,rd->ed", cross_mixed, grad_cross))
+    grad_cross_mixed = dot("ed,rd->er", cross_out, grad_cross).astype(low_type)
+    dqc, dkc, dvc = cross_backward(
+        qc, kc, vc, cross_mark, cross_mixed, cross_total, grad_cross_mixed
+    )
+    grad_encoder = dot("er,de->rd", dkc, cross_qkv[1]) + dot("er,de->rd", dvc, cross_qkv[2])
+    grad_encoder = lax.psum_scatter(
+        grad_encoder.astype(low_type).reshape(B, keys, width),
+        "seq",
+        scatter_dimension=1,
+        tiled=True,
+    )
+    mat_cross_qkv = over_dp(
+        jnp.concatenate(
+            [
+                dot("rd,er->de", first_low, dqc),
+                dot("rd,er->de", e_all, dkc),
+                dot("rd,er->de", e_all, dvc),
+            ]
+        )
+    )
+    grad_first = grad_second_sum + dot("er,de->rd", dqc, cross_qkv[0])
+    grad_first_sum, grad_gain_self, grad_shift_self = norm_back(first_sum, grad_first, gains[0])
+    grad_self = grad_first_sum.astype(low_type)
+    mat_self_out = over_dp(dot("er,rd->ed", attended, grad_self))
+    grad_attended = dot("ed,rd->er", self_out, grad_self).astype(low_type)
+    dq, dk, dv, drel = self_backward(
+        q, k, v, rel, self_mark, table, attended, self_total, grad_attended, T, S
+    )
+    count = far + S * T
+    dk_parts, dv_parts = dk.reshape(width, B, count), dv.reshape(width, B, count)
+    away = dot("ebr,de->brd", dk_parts[:, :, :far], self_qkv[1]) + dot(
+        "ebr,de->brd", dv_parts[:, :, :far], self_qkv[2]
+    )
+    away = away.astype(low_type)
+    moving = away[:, :T]
+    for hop in range(1, seq_parts):
+        moving = lax.ppermute(moving, "seq", down).astype(high_type)
+        if hop < seq_parts - 1:
+            moving = (moving + away[:, hop * T : (hop + 1) * T].astype(high_type)).astype(low_type)
+    home = (
+        grad_first_sum.reshape(B, S * T, width)
+        + dot("ebr,de->brd", dq.reshape(width, B, S * T), self_qkv[0])
+        + dot("ebr,de->brd", dk_parts[:, :, far:], self_qkv[1])
+        + dot("ebr,de->brd", dv_parts[:, :, far:], self_qkv[2])
+        + dot("jbr,dj->brd", drel.reshape(-1, B, S * T), rel_weight)
+    ).reshape(B, S, T, width)
+    mat_self_qkv = over_dp(
+        jnp.concatenate(
+            [
+                dot("rd,er->de", x, dq),
+                dot("rd,er->de", x_keys, dk),
+                dot("rd,er->de", x_keys, dv),
+            ]
+        )
+    )
+    mat_rel = over_dp(dot("rd,jr->dj", x, drel))
+    grad_hidden = jnp.concatenate(
+        [(home[:, :1] + moving[:, None]).astype(low_type), home[:, 1:].astype(low_type)], 1
+    )
+
+    vectors = [
+        jnp.stack([row_sum(dq), row_sum(dv)]),
+        column_sum(grad_self),
+        row_sum(drel),
+        jnp.stack([row_sum(dqc), row_sum(dvc)]),
+        column_sum(grad_cross),
+        column_sum(grad_pre),
+        column_sum(grad_ffn),
+        jnp.stack([grad_gain_self, grad_gain_cross, grad_gain_ffn]),
+        jnp.stack([grad_shift_self, grad_shift_cross, grad_shift_ffn]),
+    ]
+    blocks = [piece.reshape(seq_parts, -1) for piece in vectors]
+    ends = np.cumsum([piece.shape[1] for piece in blocks])
+    summed = lax.psum(jnp.concatenate(blocks, 1), ("dp", "seq"))
+    mine = lax.dynamic_index_in_dim(summed, place, 0, keepdims=False)
+    vecs = [mine[end - piece.shape[1] : end] for piece, end in zip(blocks, ends, strict=True)]
+    return (
+        output,
+        grad_hidden,
+        grad_encoder,
+        over_seq(mat_self_qkv),
+        vecs[0],
+        over_seq(mat_self_out),
+        vecs[1],
+        over_seq(mat_rel),
+        vecs[2],
+        over_seq(mat_cross_qkv),
+        vecs[3],
+        over_seq(mat_cross_out),
+        vecs[4],
+        over_seq(mat_ffn_in),
+        vecs[5],
+        over_seq(mat_ffn_out),
+        vecs[6],
+        vecs[7],
+        vecs[8],
+    )
+
+
 def solution(mesh):
+    rows, vector, matrix = P("dp", None, "seq", None), P("seq"), P(("dp", "seq"))
     return jax.shard_map(
         on_device,
         mesh=mesh,
-        in_specs=(
-            P("dp", None, "seq", None),
-            P("dp", "seq", None),
-            P("dp", None, "seq", None),
-            P("dp"),
-            P("dp"),
-            P(),
-            P(),
-            P(),
-            P(),
-            P(),
-            P(),
-            P(),
-            P(),
-            P(),
-            P(),
-            P(),
-            P(),
-            P(),
-            P(),
-            P(),
-            P(),
-        ),
-        out_specs=(
-            P("dp", None, "seq", None),
-            P("dp", None, "seq", None),
-            P("dp", "seq", None),
-            P(("dp", "seq")),
-            P("seq"),
-            P(("dp", "seq")),
-            P("seq"),
-            P(("dp", "seq")),
-            P("seq"),
-            P(("dp", "seq")),
-            P("seq"),
-            P(("dp", "seq")),
-            P("seq"),
-            P(("dp", "seq")),
-            P("seq"),
-            P(("dp", "seq")),
-            P("seq"),
-            P("seq"),
-            P("seq"),
-        ),
+        in_specs=(rows, P("dp", "seq", None), rows, P("dp"), P("dp")) + (P(),) * 16,
+        out_specs=(rows, rows, P("dp", "seq", None))
+        + (matrix, vector) * 7
+        + (vector, vector),
         check_vma=False,
     )

time: 3170 us -> 1480 us (0.47)
  matrix products: 1130 us -> 328 us
  local copies, waits for them, and re-layouts: 847 us -> 53.3 us
  Pallas kernels: 0 us -> 345 us
  other arithmetic: 371 us -> 97.2 us
  waiting for transfers between devices: 698 us -> 593 us
  blocking collectives: 45.8 us -> 0 us
  loops' own time: 43.7 us -> 0 us
  starting transfers between devices: 1.04 us -> 42.9 us
    dot_general x56 -> x34, matrix products: 1100 us -> 328 us  [dot(): return jnp.einsum(spec, left, right, preferred_element_type=high_type)]
    pallas_call x0 -> x5, Pallas kernels: none -> 345 us  [the longest x1 125 us: self_backward(): pl.pallas_call(functools.partial(self_backward_kernel, T=T, S=S), grid=(B...]
    convert_element_type x35 -> x0, local copies, waits for them, and re-layouts: 223 us -> none  [the longest x2 62.7 us: self_backward(): (weights * (grad_weights - delta[..., None])).astype(jnp.bfloat16)]
    dot_general x4 -> x0, local copies, waits for them, and re-layouts: 196 us -> none  [self_logits(): jnp.einsum('sqhb,qkb->shqk', rel_s, one_hot, precision=HIGHEST)]
    unnamed x17 -> x18, waiting for transfers between devices: 175 us -> 2.57 us
    convert_element_type x22 -> x5, other arithmetic: 178 us -> 9.36 us  [the longest x2 3.58 us: on_device(): (moving + away[:, hop * T:(hop + 1) * T].astype(high_type)).astype(low_type)]
    ppermute x0 -> x6, waiting for transfers between devices: none -> 101 us  [the longest x3 79.3 us: on_device(): moving = lax.ppermute(moving, 'seq', up)]
    reduce_sum x26 -> x13, other arithmetic: 134 us -> 39.5 us  [the longest x3 17.2 us: column_sum(): return jnp.sum(value.astype(high_type), 0)]
  transfers between devices with their start and end apart: 16 -> 23, of which waited for: 6 -> 18; matrix products, arithmetic and copies ran while one was open for 52% -> 22% of each run, Pallas kernels for 0% -> 5%
where the time goes in v1:
time: 1480 us; the launch traced here: 1470 us
  waiting for transfers between devices  593 us (40%)
  Pallas kernels  345 us (23%)
  matrix products  328 us (22%)
  other arithmetic  97.2 us (7%)
  local copies, waits for them, and re-layouts  53.3 us (4%)
  starting transfers between devices  42.9 us (3%)
  between operations  15.4 us (1%)
    dot_general x34, matrix products, dot(): return jnp.einsum(spec, left, right, preferred_element_type=high_type)  328 us
    reduce_scatter x6, waiting for transfers between devices, over_dp(): lax.psum_scatter(piece.astype(low_type), 'dp', scatter_dimension=0, tiled...  257 us
    reduce_scatter x7, waiting for transfers between devices, over_seq(): lax.psum_scatter(piece, 'seq', scatter_dimension=0, tiled=True)  146 us
    pallas_call x1, Pallas kernels, self_backward(): pl.pallas_call(functools.partial(self_backward_kernel, T=T, S=S), grid=(B...  125 us
    ppermute x3, waiting for transfers between devices, on_device(): moving = lax.ppermute(moving, 'seq', up)  79.3 us
    reduce_scatter x1, waiting for transfers between devices, on_device(): lax.psum_scatter(grad_encoder.astype(low_type).reshape(B, keys, width), '...  76.4 us
    pallas_call x1, Pallas kernels, self_forward(): pl.pallas_call(functools.partial(self_forward_kernel, T=T, S=S), grid=(B,...  69.6 us
    pallas_call x1, Pallas kernels, cross_backward(): pl.pallas_call(functools.partial(cross_backward_kernel, step=count // 2),...  64.8 us
  transfers between devices with their start and end apart: 23, of which 18 were waited for; matrix products, arithmetic and copies ran while one was open for 22% of the time, Pallas kernels for 5%

profile of v1, /device:TPU:0, one launch (start us, length us, event | category | flops | bytes accessed | tf_op | source)
XLA Modules:
  0.0 1474.5 jit_solution(15587414444557518828)
XLA Ops:
  27.9 27.7 %collective-permute-done = bf16[2,256,1024]{2,1,0:T(8,128)(2,1)} collective-permute-done((bf16[2,256,1024]{2,1,0:T(8,128)(2,1)}, bf16[2,256,1024]{2,1,0:T(8,128)(2,1)}, u32[]{:S(2)}, u32[]{:S(2)}) %collective-permute-start) | collective-permute-done | bytes 1048608 | tf_op jit(solution)/shard_map/ppermute | solution.py:993
  55.6 20.3 %collective-permute-start.1 = (bf16[2,256,1024]{2,1,0:T(8,128)(2,1)}, bf16[2,256,1024]{2,1,0:T(8,128)(2,1)S(1)}, u32[]{:S(2)}, u32[]{:S(2)}) collective-permute-start(bf16[2,256,1024]{2,1,0:T(8,128)(2,1)} %collective-permute-done), channel_id=1, source_target_pairs={{0,1},{1,2},{2,3},{4,5},{5,6},{6,7},{8,9},{9,10},{10,11},{12,13},{... | collective-permute-start | bytes 3145736 | tf_op jit(solution)/shard_map/ppermute | solution.py:993
  82.4 37.3 %collective-permute-done.1 = bf16[2,256,1024]{2,1,0:T(8,128)(2,1)S(1)} collective-permute-done((bf16[2,256,1024]{2,1,0:T(8,128)(2,1)}, bf16[2,256,1024]{2,1,0:T(8,128)(2,1)S(1)}, u32[]{:S(2)}, u32[]{:S(2)}) %collective-permute-start.1) | collective-permute-done | bytes 1048608 | tf_op jit(solution)/shard_map/ppermute | solution.py:993
  119.7 11.7 collective-permute-start.2
  138.4 14.3 collective-permute-done.2
  178.5 69.6 %self_forward.1 = (bf16[1024,1536]{1,0:T(8,128)(2,1)}, f32[2,16,1,768]{3,2,1,0:T(1,128)}) custom-call(bf16[1024,1536]{1,0:T(8,128)(2,1)} %multiply_convert_fusion.2.q_ref, bf16[1024,3072]{1,0:T(8,128)(2,1)} %convert_bitcast_fusion.k_ref, bf16[1024,3072]{1,0:T(8,128)(2,1)} %fusion.v_ref, f32[512,1536]{1,0:T(8,128)} %convolution_add_fusion.2.rel_ref, ...), custom_call_target="tpu_custom_call" | custom-call | flops 25769803776 | bytes 29360128 | tf_op jit(solution)/shard_map/self_forward/pallas_call | solution.py:320
  282.4 46.1 %cross_forward.1 = (bf16[1024,1536]{1,0:T(8,128)(2,1)}, f32[2,16,1,768]{3,2,1,0:T(1,128)}) custom-call(bf16[1024,1536]{1,0:T(8,128)(2,1)} %fusion.12.q_ref, bf16[1024,2048]{1,0:T(8,128)(2,1)} %convolution_convert_fusion.4.k_ref, bf16[1024,2048]{1,0:T(8,128)(2,1)} %add_convert_fusion.2.v_ref, bf16[2,16,1024]{2,1,0:T(8,128)(2,1)} %get-tuple-element.81.mark_ref), custom_call_target="tpu_custom_call" | custom-call | flops 25769803776 | bytes 29360128 | tf_op jit(solution)/shard_map/cross_forward/pallas_call | solution.py:287
  340.8 39.6 %ffn_first.1 = (bf16[1536,4096]{1,0:T(8,128)(2,1)}, bf16[1536,4096]{1,0:T(8,128)(2,1)}) custom-call(bf16[1536,1024]{1,0:T(8,128)(2,1)} %fusion.9.x_ref, bf16[1024,4096]{1,0:T(8,128)(2,1)} %w_ref.1, f32[1,4096]{1,0:T(1,128)} %bitcast.252), custom_call_target="tpu_custom_call" | custom-call | flops 12884901888 | bytes 25165824 | tf_op jit(solution)/shard_map/ffn_first/pallas_call | solution.py:379
  380.4 19.7 %fusion.79 = (f32[1536]{0:T(1024)S(1)}, f32[1536,1024]{1,0:T(8,128)S(1)}) fusion(f32[1024]{0:T(1024)S(1)} %copy-done.44, bf16[1536,4096]{1,0:T(8,128)(2,1)} %get-tuple-element.34, bf16[4096,1024]{1,0:T(8,128)(2,1)} %param.39, f32[1024]{0:T(1024)S(1)} %bitcast.248, f32[1024]{0:T(1024)S(1)} %bitcast.236, f32[1536]{0:T(1024)S(1)} %add_rsqrt_fusion.1, ...), kind=kOutput, calls=%fused_computation.182 | convolution fusion | flops 12895909888 | bytes 33585152 | tf_op jit(solution)/shard_map/rf,fd->rd/dot_general | solution.py:406
  411.1 21.5 %convert_reduce_fusion = (f32[4096]{0:T(1024)}, bf16[1536,4096]{1,0:T(8,128)(2,1)}) fusion(bf16[1536,4096]{1,0:T(8,128)(2,1)} %get-tuple-element.35, bf16[4096,1024]{1,0:T(8,128)(2,1)} %param.39, f32[1536,1024]{1,0:T(8,128)} %get-tuple-element.60), kind=kOutput, calls=%fused_computation | convolution fusion | flops 12917927936 | bytes 39862272 | tf_op jit(solution)/shard_map/rd,fd->rf/dot_general | solution.py:406
  432.6 25.8 %multiply_reduce_fusion = (f32[1024]{0:T(1024)}, f32[1536]{0:T(1024)S(1)}, f32[1536]{0:T(1024)S(1)}, f32[1024]{0:T(1024)}, f32[1536,1024]{1,0:T(8,128)}) fusion(f32[1536,1024]{1,0:T(8,128)} %copy-done.2, f32[1536]{0:T(1024)S(1)} %add_rsqrt_fusion.1, f32[1536]{0:T(1024)S(1)} %broadcast_multiply_fusion.7, f32[1024]{0:T(1024)S(1)} %bitcast.237, ...), kind=kOutput, calls=%fused_computation.24 | convolution fusion | flops 12900625408 | bytes 39882752 | tf_op jit(solution)/shard_map/rf,df->rd/dot_general | solution.py:406
  469.5 64.8 %cross_backward.1 = (bf16[1024,1536]{1,0:T(8,128)(2,1)}, bf16[1024,2048]{1,0:T(8,128)(2,1)}, bf16[1024,2048]{1,0:T(8,128)(2,1)}) custom-call(bf16[1024,1536]{1,0:T(8,128)(2,1)} %fusion.12.q_ref, bf16[1024,2048]{1,0:T(8,128)(2,1)} %convolution_convert_fusion.4.k_ref, bf16[1024,2048]{1,0:T(8,128)(2,1)} %add_convert_fusion.2.v_ref, ...), custom_call_target="tpu_custom_call" | custom-call | flops 64424509440 | bytes 73400320 | tf_op jit(solution)/shard_map/cross_backward/pallas_call | solution.py:303
  534.4 12.1 multiply_reduce_fusion.1
  556.9 124.7 %self_backward.1 = (bf16[1024,1536]{1,0:T(8,128)(2,1)}, bf16[1024,3072]{1,0:T(8,128)(2,1)}, bf16[1024,3072]{1,0:T(8,128)(2,1)}, bf16[512,1536]{1,0:T(8,128)(2,1)}) custom-call(bf16[1024,1536]{1,0:T(8,128)(2,1)} %multiply_convert_fusion.2.q_ref, bf16[1024,3072]{1,0:T(8,128)(2,1)} %convert_bitcast_fusion.k_ref, bf16[1024,3072]{1,0:T(8,128)(2,1)} %fusion.v_ref, ...), custom_call_target="tpu_custom_call" | custom-call | flops 64424509440 | bytes 73400320 | tf_op jit(solution)/shard_map/self_backward/pallas_call | solution.py:336
  721.6 13.2 pad_maximum_fusion.2
  741.6 11.0 convolution_convert_fusion.9
  759.7 13.3 pad_maximum_fusion.1
  773.1 19.6 %convolution_convert_fusion.1 = bf16[1024,4096]{1,0:T(8,128)(2,1)} fusion(bf16[1536,1024]{1,0:T(8,128)(2,1)} %fusion.9.x_ref, bf16[1536,4096]{1,0:T(8,128)(2,1)} %get-tuple-element.92), kind=kOutput, calls=%fused_computation.8 | convolution fusion | flops 12889096192 | bytes 24117248 | tf_op jit(solution)/shard_map/rd,rf->df/dot_general | solution.py:406
  792.7 20.9 %convolution_convert_fusion = bf16[4096,1024]{1,0:T(8,128)(2,1)} fusion(bf16[1536,4096]{1,0:T(8,128)(2,1)} %get-tuple-element.34, f32[1536,1024]{1,0:T(8,128)} %get-tuple-element.60), kind=kOutput, calls=%fused_computation.7 | convolution fusion | flops 12890669056 | bytes 27262976 | tf_op jit(solution)/shard_map/rf,rd->fd/dot_general | solution.py:406
  829.5 50.5 %reduce-scatter.30.cloned.1.call-done = bf16[384,1024]{1,0:T(8,128)(2,1)} async-done(((bf16[3072,1024]{1,0:T(8,128)(2,1)}), bf16[384,1024]{1,0:T(8,128)(2,1)}) %reduce-scatter.30.cloned.1.call-update) | async-done | bytes 786448 | tf_op jit(solution)/shard_map/reduce_scatter | solution.py:1044
  880.1 65.3 %reduce-scatter.22.cloned.1.call-done = bf16[384,1024]{1,0:T(8,128)(2,1)} async-done(((bf16[3072,1024]{1,0:T(8,128)(2,1)}), bf16[384,1024]{1,0:T(8,128)(2,1)}) %reduce-scatter.22.cloned.1.call-update) | async-done | bytes 786448 | tf_op jit(solution)/shard_map/reduce_scatter | solution.py:1044
  945.5 74.7 %reduce-scatter.38.cloned.1.call-done = bf16[128,4096]{1,0:T(8,128)(2,1)} async-done(((bf16[1024,4096]{1,0:T(8,128)(2,1)}), bf16[128,4096]{1,0:T(8,128)(2,1)}) %reduce-scatter.38.cloned.1.call-update) | async-done | bytes 1048592 | tf_op jit(solution)/shard_map/reduce_scatter | solution.py:1044
  1028.9 66.4 %reduce-scatter.42.cloned.1.call-done = bf16[512,1024]{1,0:T(8,128)(2,1)} async-done(((bf16[4096,1024]{1,0:T(8,128)(2,1)}), bf16[512,1024]{1,0:T(8,128)(2,1)}) %reduce-scatter.42.cloned.1.call-update) | async-done | bytes 1048592 | tf_op jit(solution)/shard_map/reduce_scatter | solution.py:1044
  1147.7 17.2 %collective-permute-done.3 = bf16[2,256,1024]{2,1,0:T(8,128)(2,1)S(1)} collective-permute-done((bf16[2,256,1024]{2,1,0:T(8,128)(2,1)S(1)}, bf16[2,256,1024]{2,1,0:T(8,128)(2,1)S(1)}, u32[]{:S(2)}, u32[]{:S(2)}) %collective-permute-start.3) | collective-permute-done | bytes 1048608 | tf_op jit(solution)/shard_map/ppermute | solution.py:1098
  1227.1 16.5 %reduce-scatter.48.cloned.1.call-done = bf16[32,512]{1,0:T(8,128)(2,1)} async-done(((bf16[128,512]{1,0:T(8,128)(2,1)}), bf16[32,512]{1,0:T(8,128)(2,1)}) %reduce-scatter.48.cloned.1.call-update) | async-done | bytes 32784 | tf_op jit(solution)/shard_map/reduce_scatter | solution.py:1048
  1250.9 13.0 reduce-scatter.36.cloned.1.call-done
  1265.4 18.4 %reduce-scatter.28.cloned.1.call-done = bf16[32,1024]{1,0:T(8,128)(2,1)} async-done(((bf16[128,1024]{1,0:T(8,128)(2,1)}), bf16[32,1024]{1,0:T(8,128)(2,1)}) %reduce-scatter.28.cloned.1.call-update) | async-done | bytes 65552 | tf_op jit(solution)/shard_map/reduce_scatter | solution.py:1048
  1285.4 22.5 %reduce-scatter.32.cloned.1.call-done = bf16[96,1024]{1,0:T(8,128)(2,1)} async-done(((bf16[384,1024]{1,0:T(8,128)(2,1)}), bf16[96,1024]{1,0:T(8,128)(2,1)}) %reduce-scatter.32.cloned.1.call-update) | async-done | bytes 196624 | tf_op jit(solution)/shard_map/reduce_scatter | solution.py:1048
  1309.7 23.1 %reduce-scatter.24.cloned.1.call-done = bf16[96,1024]{1,0:T(8,128)(2,1)} async-done(((bf16[384,1024]{1,0:T(8,128)(2,1)}), bf16[96,1024]{1,0:T(8,128)(2,1)}) %reduce-scatter.24.cloned.1.call-update) | async-done | bytes 196624 | tf_op jit(solution)/shard_map/reduce_scatter | solution.py:1048
  1334.5 26.9 %reduce-scatter.40.cloned.1.call-done = bf16[32,4096]{1,0:T(8,128)(2,1)} async-done(((bf16[128,4096]{1,0:T(8,128)(2,1)}), bf16[32,4096]{1,0:T(8,128)(2,1)}) %reduce-scatter.40.cloned.1.call-update) | async-done | bytes 262160 | tf_op jit(solution)/shard_map/reduce_scatter | solution.py:1048
  1363.3 26.1 %reduce-scatter.44.cloned.1.call-done = bf16[128,1024]{1,0:T(8,128)(2,1)} async-done(((bf16[512,1024]{1,0:T(8,128)(2,1)}), bf16[128,1024]{1,0:T(8,128)(2,1)}) %reduce-scatter.44.cloned.1.call-update) | async-done | bytes 262160 | tf_op jit(solution)/shard_map/reduce_scatter | solution.py:1048
  1391.3 76.4 %reduce-scatter.20.cloned.1.call-done = bf16[2,256,1024]{2,1,0:T(8,128)(2,1)} async-done(((bf16[2,1024,1024]{2,1,0:T(8,128)(2,1)}), bf16[2,256,1024]{2,1,0:T(8,128)(2,1)}) %reduce-scatter.20.cloned.1.call-update) | async-done | bytes 1048592 | tf_op jit(solution)/shard_map/reduce_scatter | solution.py:1067
  (290 shorter events, 348.9 us)
Async XLA Ops:
  7.2 321.4 %copy-start = (bf16[1024,1024]{1,0:T(8,128)(2,1)S(1)}, bf16[1024,1024]{1,0:T(8,128)(2,1)}, u32[]{:S(2)}) copy-start(bf16[1024,1024]{1,0:T(8,128)(2,1)} %param.35) | copy-start | bytes 6291460
  7.3 257.7 %all-gather.2.cloned.1.call-start = ((), (), s32[]{:S(2)}) async-start(), calls=%async_computation.15 | async-start | bytes 5242880 | tf_op jit(solution)/shard_map/all_gather | solution.py:1015
  8.0 819.7 %reduce-scatter.46.cloned.1.call-start = ((), (), s32[]{:S(2)}) async-start(), calls=%async_computation.30 | async-start | bytes 1179648
  10.3 45.3 %collective-permute-start = (bf16[2,256,1024]{2,1,0:T(8,128)(2,1)}, bf16[2,256,1024]{2,1,0:T(8,128)(2,1)}, u32[]{:S(2)}, u32[]{:S(2)}) collective-permute-start(bf16[2,256,1024]{2,1,0:T(8,128)(2,1)} %slice_bitcast_fusion.1), channel_id=1, source_target_pairs={{0,1},{1,2},{2,3},{4,5},{5,6},{6,7},{8,9},{9,10},{10,11},{12,13},{... | collective-permute-start | bytes 3145736 | tf_op jit(solution)/shard_map/ppermute | solution.py:993
  21.1 307.4 %copy-start.32 = (f32[1,1024]{1,0:T(1,128)}, f32[1,1024]{1,0:T(1,128)S(1)}, u32[]{:S(2)}) copy-start(f32[1,1024]{1,0:T(1,128)S(1)} %get-tuple-element.73) | copy-start | bytes 12292
  26.1 105.3 %copy-start.38 = (bf16[2,1024]{1,0:T(2,128)(2,1)S(1)}, bf16[2,1024]{1,0:T(2,128)(2,1)}, u32[]{:S(2)}) copy-start(bf16[2,1024]{1,0:T(2,128)(2,1)} %param.34) | copy-start | bytes 12292
  27.3 104.1 %copy-start.10 = (bf16[2,3,256,1024]{3,2,1,0:T(8,128)(2,1)S(1)}, bf16[2,3,256,1024]{3,2,1,0:T(8,128)(2,1)}, u32[]{:S(2)}) copy-start(bf16[2,3,256,1024]{3,2,1,0:T(8,128)(2,1)} %param.22) | copy-start | bytes 9437188
  27.9 300.6 %copy-start.45 = (f32[1,1024]{1,0:T(1,128)}, f32[1,1024]{1,0:T(1,128)S(1)}, u32[]{:S(2)}) copy-start(f32[1,1024]{1,0:T(1,128)S(1)} %get-tuple-element.76) | copy-start | bytes 12292
  55.6 64.0 %collective-permute-start.1 = (bf16[2,256,1024]{2,1,0:T(8,128)(2,1)}, bf16[2,256,1024]{2,1,0:T(8,128)(2,1)S(1)}, u32[]{:S(2)}, u32[]{:S(2)}) collective-permute-start(bf16[2,256,1024]{2,1,0:T(8,128)(2,1)} %collective-permute-done), channel_id=1, source_target_pairs={{0,1},{1,2},{2,3},{4,5},{5,6},{6,7},{8,9},{9,10},{10,11},{12,13},{... | collective-permute-start | bytes 3145736 | tf_op jit(solution)/shard_map/ppermute | solution.py:993
  76.8 83.8 %slice-start.4 = ((s8[6291456]{0:T(1024)(128)(4,1)}), s8[4194304]{0:T(1024)(128)(4,1)S(1)}, s32[]{:S(2)}) async-start(s8[6291456]{0:T(1024)(128)(4,1)} %bitcast.271), calls=%async_computation.36 | async-start | bytes 8388608
  119.7 33.1 %collective-permute-start.2 = (bf16[2,256,1024]{2,1,0:T(8,128)(2,1)S(1)}, bf16[2,256,1024]{2,1,0:T(8,128)(2,1)S(1)}, u32[]{:S(2)}, u32[]{:S(2)}) collective-permute-start(bf16[2,256,1024]{2,1,0:T(8,128)(2,1)S(1)} %collective-permute-done.1), channel_id=1, source_target_pairs={{0,1},{1,2},{2,3},{4,5},{5,6},{6,7},{8,9},{9,10},{10,11},{12,13},{... | collective-permute-start | bytes 3145736 | tf_op jit(solution)/shard_map/ppermute | solution.py:993
  254.4 74.1 %copy-start.18 = (f32[1536]{0:T(1024)}, f32[1536]{0:T(1024)S(1)}, u32[]{:S(2)}) copy-start(f32[1536]{0:T(1024)S(1)} %broadcast_multiply_fusion.8) | copy-start | bytes 18436
  556.9 124.7 %copy-start.11 = (bf16[2,3,256,1024]{3,2,1,0:T(8,128)(2,1)S(1)}, bf16[2,3,256,1024]{3,2,1,0:T(8,128)(2,1)}, u32[]{:S(2)}) copy-start(bf16[2,3,256,1024]{3,2,1,0:T(8,128)(2,1)} %param.22) | copy-start | bytes 9437188
  686.2 142.1 %reduce-scatter.34.cloned.1.call-start = ((), (), s32[]{:S(2)}) async-start(), calls=%async_computation.24 | async-start | bytes 2359296 | tf_op jit(solution)/shard_map/reduce_scatter | solution.py:1044
  694.8 134.2 %reduce-scatter.26.cloned.1.call-start = ((), (), s32[]{:S(2)}) async-start(), calls=%async_computation.20 | async-start | bytes 2359296 | tf_op jit(solution)/shard_map/reduce_scatter | solution.py:1044
  703.6 176.4 %reduce-scatter.30.cloned.1.call-start = ((), (), s32[]{:S(2)}) async-start(), calls=%async_computation.22 | async-start | bytes 7077888 | tf_op jit(solution)/shard_map/reduce_scatter | solution.py:1044
  734.8 210.6 %reduce-scatter.22.cloned.1.call-start = ((), (), s32[]{:S(2)}) async-start(), calls=%async_computation.17 | async-start | bytes 7077888 | tf_op jit(solution)/shard_map/reduce_scatter | solution.py:1044
  773.0 247.1 %reduce-scatter.38.cloned.1.call-start = ((), (), s32[]{:S(2)}) async-start(), calls=%async_computation.26 | async-start | bytes 9437184 | tf_op jit(solution)/shard_map/reduce_scatter | solution.py:1044
  792.7 302.6 %reduce-scatter.42.cloned.1.call-start = ((), (), s32[]{:S(2)}) async-start(), calls=%async_computation.28 | async-start | bytes 9437184 | tf_op jit(solution)/shard_map/reduce_scatter | solution.py:1044
  813.7 406.6 %all-reduce.2.cloned.1.call-start = ((), (), s32[]{:S(2)}) async-start(), calls=%async_computation.19 | async-start | bytes 143360 | tf_op jit(solution)/shard_map/psum | solution.py:1135
  827.6 416.0 %reduce-scatter.48.cloned.1.call-start = ((), (), s32[]{:S(2)}) async-start(), calls=%async_computation.31 | async-start | bytes 163840 | tf_op jit(solution)/shard_map/reduce_scatter | solution.py:1048
  828.2 435.7 %reduce-scatter.36.cloned.1.call-start = ((), (), s32[]{:S(2)}) async-start(), calls=%async_computation.25 | async-start | bytes 327680 | tf_op jit(solution)/shard_map/reduce_scatter | solution.py:1048
  828.9 454.9 %reduce-scatter.28.cloned.1.call-start = ((), (), s32[]{:S(2)}) async-start(), calls=%async_computation.21 | async-start | bytes 327680 | tf_op jit(solution)/shard_map/reduce_scatter | solution.py:1048
  829.5 478.4 %reduce-scatter.32.cloned.1.call-start = ((), (), s32[]{:S(2)}) async-start(), calls=%async_computation.23 | async-start | bytes 983040 | tf_op jit(solution)/shard_map/reduce_scatter | solution.py:1048
  880.0 452.7 %reduce-scatter.24.cloned.1.call-start = ((), (), s32[]{:S(2)}) async-start(), calls=%async_computation.18 | async-start | bytes 983040 | tf_op jit(solution)/shard_map/reduce_scatter | solution.py:1048
  945.4 416.0 %reduce-scatter.40.cloned.1.call-start = ((), (), s32[]{:S(2)}) async-start(), calls=%async_computation.27 | async-start | bytes 1310720 | tf_op jit(solution)/shard_map/reduce_scatter | solution.py:1048
  1020.2 369.2 %reduce-scatter.44.cloned.1.call-start = ((), (), s32[]{:S(2)}) async-start(), calls=%async_computation.29 | async-start | bytes 1310720 | tf_op jit(solution)/shard_map/reduce_scatter | solution.py:1048
  1095.3 372.4 %reduce-scatter.20.cloned.1.call-start = ((), (), s32[]{:S(2)}) async-start(), calls=%async_computation.16 | async-start | bytes 5242880 | tf_op jit(solution)/shard_map/reduce_scatter | solution.py:1067
  1137.5 27.4 %collective-permute-start.3 = (bf16[2,256,1024]{2,1,0:T(8,128)(2,1)S(1)}, bf16[2,256,1024]{2,1,0:T(8,128)(2,1)S(1)}, u32[]{:S(2)}, u32[]{:S(2)}) collective-permute-start(bf16[2,256,1024]{2,1,0:T(8,128)(2,1)S(1)} %slice.203), channel_id=1, source_target_pairs={{1,0},{2,1},{3,2},{5,4},{6,5},{7,6},{9,8},{10,9},{11,10},{13,12},{... | collective-permute-start | bytes 3145736 | tf_op jit(solution)/shard_map/ppermute | solution.py:1098
  1166.5 26.6 %collective-permute-start.4 = (bf16[2,256,1024]{2,1,0:T(8,128)(2,1)S(1)}, bf16[2,256,1024]{2,1,0:T(8,128)(2,1)}, u32[]{:S(2)}, u32[]{:S(2)}) collective-permute-start(bf16[2,256,1024]{2,1,0:T(8,128)(2,1)S(1)} %add_convert_fusion.6), channel_id=1, source_target_pairs={{1,0},{2,1},{3,2},{5,4},{6,5},{7,6},{9,8},{10,9},{11,10},{13,12},{... | collective-permute-start | bytes 3145736 | tf_op jit(solution)/shard_map/ppermute | solution.py:1098
  1195.1 50.0 %collective-permute-start.5 = (bf16[2,256,1024]{2,1,0:T(8,128)(2,1)S(1)}, bf16[2,256,1024]{2,1,0:T(8,128)(2,1)}, u32[]{:S(2)}, u32[]{:S(2)}) collective-permute-start(bf16[2,256,1024]{2,1,0:T(8,128)(2,1)S(1)} %add_convert_fusion.5), channel_id=1, source_target_pairs={{1,0},{2,1},{3,2},{5,4},{6,5},{7,6},{9,8},{10,9},{11,10},{13,12},{... | collective-permute-start | bytes 3145736 | tf_op jit(solution)/shard_map/ppermute | solution.py:1098
  1245.0 222.6 %copy-start.1 = (bf16[1024,1024]{1,0:T(8,128)(2,1)S(1)}, bf16[1024,1024]{1,0:T(8,128)(2,1)}, u32[]{:S(2)}) copy-start(bf16[1024,1024]{1,0:T(8,128)(2,1)} %param.35) | copy-start | bytes 6291460
  (50 other events, 827.2 us)
Sparse Core Ops, SparseCore 0:
  9.7 118.2 all-gather.1
  686.3 38.8 reduce-scatter.45
  728.5 41.1 reduce-scatter.33
  773.7 41.2 reduce-scatter.25
  818.3 61.6 reduce-scatter.29
  883.6 61.7 reduce-scatter.21
  948.8 71.2 reduce-scatter.37
  1024.0 71.2 reduce-scatter.41
  1101.4 118.8 all-reduce.1
  1222.5 21.1 reduce-scatter.47
  1246.0 17.8 reduce-scatter.35
  1266.0 17.7 reduce-scatter.27
  1286.2 21.5 reduce-scatter.31
  1310.1 22.5 reduce-scatter.23
  1335.0 26.3 reduce-scatter.39
  1363.6 25.7 reduce-scatter.43
  1392.2 75.4 reduce-scatter.19

commit v2 on v1

--- a/solution.py
+++ b/solution.py
@@ -118,46 +118,60 @@
     dv_ref[...] = dv_acc[...].astype(low_type)
 
 
-def self_forward_kernel(q_ref, k_ref, v_ref, rel_ref, mark_ref, table_ref, o_ref, total_ref, *, T, S):
-    n, tile = S * T, min(TILE, T)
-    keys = k_ref.shape[1] - n + T
+def near_biases(rel, table):
+    near = near_bias(rel, table)
+    return [
+        pltpu.roll(near[row : row + TILE], 0, 1, stride=1, stride_axis=0)
+        for row in range(0, near.shape[0], TILE)
+    ]
+
+
+def main_and_own(far_ref, near_ref, T):
+    near = near_ref[...]
+    return jnp.concatenate([far_ref[...], near[:, :T]], 1), near[:, T:]
+
+
+def near_window(block, bias, first, main_row):
+    at = lax.broadcasted_iota(jnp.int32, (TILE, TILE), 0)
+    to = lax.broadcasted_iota(jnp.int32, (TILE, TILE), 1)
+    left = block[:, first : first + TILE] + bias[:, :TILE]
+    right = block[:, first + TILE : first + 2 * TILE] + bias[:, TILE:]
+    return left, jnp.where((to <= at) if main_row else (to < at), right, NEGATIVE)
+
+
+def self_forward_kernel(*refs, T, S):
+    q_ref, k_ref, v_ref, k_far_ref, v_far_ref, rel_ref, mark_ref, table_ref = refs[:8]
+    o_ref, total_ref = refs[-2:]
+    n, keys = S * T, k_far_ref.shape[1] + T
     q, rel = q_ref[...], rel_ref[...]
-    k1 = jnp.concatenate([k_ref[:, :keys], mark_ref[...]], 0)
-    v1 = jnp.concatenate([v_ref[:, :keys], jnp.ones((16, keys), low_type)], 0)
+    k, own_k = main_and_own(k_far_ref, k_ref, T)
+    v, own_v = main_and_own(v_far_ref, v_ref, T)
+    biases = near_biases(rel, table_ref[...])
+    k1 = jnp.concatenate([k, mark_ref[...]], 0)
+    v1 = jnp.concatenate([v, jnp.ones((16, keys), low_type)], 0)
     q1 = jnp.concatenate([q, feature_rows(1.0, rel[BUCKETS - 1 :])], 0)
     scores = contract(q1, k1, 0, 0)
-    near = near_bias(rel, table_ref[...])
-    at = lax.broadcasted_iota(jnp.int32, (tile, tile), 0)
-    to = lax.broadcasted_iota(jnp.int32, (tile, tile), 1)
     weights, peaks = [], []
     for s in range(S):
-        for r in range(T // tile):
-            row, first = s * T + r * tile, keys - T + r * tile - TILE
-            bias = pltpu.roll(near[row : row + tile], 0, 1, stride=1, stride_axis=0)
-            block = scores[row : row + tile]
-            left = block[:, first : first + TILE] + bias[:, :TILE]
-            right = block[:, first + TILE : first + TILE + tile] + bias[:, TILE : TILE + tile]
-            right = jnp.where((to <= at) if s == 0 else (to < at), right, NEGATIVE)
+        for r in range(T // TILE):
+            row, first = s * T + r * TILE, keys - T + (r - 1) * TILE
+            block = scores[row : row + TILE]
+            left, right = near_window(block, biases[row // TILE], first, s == 0)
             parts = [left, right]
-            peak = jnp.max(
-                jnp.maximum(left, right) if tile == TILE else jnp.concatenate(parts, 1),
-                1,
-                keepdims=True,
-            )
+            peak = jnp.max(jnp.maximum(left, right), 1, keepdims=True)
             if first > 0:
                 far = block[:, :first]
                 peak = jnp.maximum(peak, jnp.max(far, 1, keepdims=True))
                 parts = [far] + parts
             parts = [jnp.exp(part - peak).astype(low_type) for part in parts]
-            if first + TILE + tile < keys:
-                parts.append(jnp.zeros((tile, keys - first - TILE - tile), low_type))
+            if first + 2 * TILE < keys:
+                parts.append(jnp.zeros((TILE, keys - first - 2 * TILE), low_type))
             weights.append(jnp.concatenate(parts, 1))
-            peaks.append(jnp.broadcast_to(peak, (tile, tile)).T[0:1])
+            peaks.append(jnp.broadcast_to(peak, (TILE, TILE)).T[0:1])
     mixed = contract(v1, jnp.concatenate(weights, 0), 1, 1)
     peak = jnp.concatenate(peaks, 1)
     total, mixed = mixed[SIZE : SIZE + 1], mixed[:SIZE]
-    own_k = k_ref[:, keys:].astype(high_type)
-    own_v = v_ref[:, keys:].astype(high_type)
+    own_k, own_v = own_k.astype(high_type), own_v.astype(high_type)
     own = jnp.sum(q[:, T:].astype(high_type) * own_k, 0, keepdims=True) + rel[0:1, T:]
     top = jnp.maximum(peak[:, T:], own)
     main_part, own_part = jnp.exp(peak[:, T:] - top), jnp.exp(own - top)
@@ -171,77 +185,69 @@
     total_ref[:, T:] = top + jnp.log(joined)
 
 
-def self_backward_kernel(
-    q_ref,
-    k_ref,
-    v_ref,
-    rel_ref,
-    mark_ref,
-    table_ref,
-    o_ref,
-    total_ref,
-    do_ref,
-    dq_ref,
-    dk_ref,
-    dv_ref,
-    drel_ref,
-    *,
-    T,
-    S,
-):
-    n, tile = S * T, min(TILE, T)
-    keys = k_ref.shape[1] - n + T
+def self_backward_kernel(*refs, T, S):
+    q_ref, k_ref, v_ref, k_far_ref, v_far_ref, rel_ref, mark_ref, table_ref = refs[:8]
+    o_ref, total_ref, do_ref = refs[8:11]
+    dq_ref, dkv_ref, drel_ref, far_ref = refs[-4:]
+    n, keys = S * T, k_far_ref.shape[1] + T
+    far = keys - T
     q, rel, do, total = q_ref[...], rel_ref[...], do_ref[...], total_ref[...]
     table = table_ref[...]
-    k1 = jnp.concatenate([k_ref[:, :keys], mark_ref[...]], 0)
-    v1 = jnp.concatenate([v_ref[:, :keys], mark_ref[...]], 0)
+    k, own_k = main_and_own(k_far_ref, k_ref, T)
+    v, own_v = main_and_own(v_far_ref, v_ref, T)
+    biases = near_biases(rel, table)
+    k1 = jnp.concatenate([k, mark_ref[...]], 0)
+    v1 = jnp.concatenate([v, mark_ref[...]], 0)
     do_high = do.astype(high_type)
     delta = jnp.sum(do_high * o_ref[...].astype(high_type), 0, keepdims=True)
     q1 = jnp.concatenate([q, feature_rows(1.0, rel[BUCKETS - 1 :] - total)], 0)
     do1 = jnp.concatenate([do, feature_rows(0.0, -delta)], 0)
     scores = contract(q1, k1, 0, 0)
     slopes = contract(do1, v1, 0, 0)
-    near = near_bias(rel, table)
-    at = lax.broadcasted_iota(jnp.int32, (tile, tile), 0)
-    to = lax.broadcasted_iota(jnp.int32, (tile, tile), 1)
-    mirror = (at + to == tile - 1).astype(high_type).astype(low_type)
-    weights, grads, rels = [], [], []
+    weights, grads, nears = [], [], []
     for s in range(S):
-        for r in range(T // tile):
-            row, first = s * T + r * tile, keys - T + r * tile - TILE
-            bias = pltpu.roll(near[row : row + tile], 0, 1, stride=1, stride_axis=0)
-            block, slope = scores[row : row + tile], slopes[row : row + tile]
-            left = block[:, first : first + TILE] + bias[:, :TILE]
-            right = block[:, first + TILE : first + TILE + tile] + bias[:, TILE : TILE + tile]
-            right = jnp.where((to <= at) if s == 0 else (to < at), right, NEGATIVE)
-            part = jnp.exp(jnp.concatenate([left, right], 1))
-            grad = (part * slope[:, first : first + TILE + tile]).astype(low_type)
-            turned = contract(mirror, grad, 1, 0)
-            if tile < TILE:
-                turned = jnp.concatenate([turned, jnp.zeros((tile, TILE - tile), high_type)], 1)
-            turned = pltpu.roll(turned, 2 * TILE - tile + 1, 1, stride=1, stride_axis=0)
-            turned = turned.astype(low_type)
-            top, rest = split_two(contract(table, turned, 1, 1))
-            both = contract(jnp.concatenate([top, rest], 0), mirror, 1, 0)
-            rels.append(both[:BUCKETS] + both[BUCKETS:])
+        for r in range(T // TILE):
+            row, first = s * T + r * TILE, keys - T + (r - 1) * TILE
+            block, slope = scores[row : row + TILE], slopes[row : row + TILE]
+            part = jnp.exp(
+                jnp.concatenate(near_window(block, biases[row // TILE], first, s == 0), 1)
+            )
+            grad = (part * slope[:, first : first + 2 * TILE]).astype(low_type)
+            nears.append(grad)
             parts, pieces = [part.astype(low_type)], [grad]
             if first > 0:
                 part = jnp.exp(block[:, :first])
                 pieces = [(part * slope[:, :first]).astype(low_type)] + pieces
                 parts = [part.astype(low_type)] + parts
-            if first + TILE + tile < keys:
-                zero = jnp.zeros((tile, keys - first - TILE - tile), low_type)
+            if first + 2 * TILE < keys:
+                zero = jnp.zeros((TILE, keys - first - 2 * TILE), low_type)
                 parts.append(zero)
                 pieces.append(zero)
             weights.append(jnp.concatenate(parts, 1))
             grads.append(jnp.concatenate(pieces, 1))
     weights, grads = jnp.concatenate(weights, 0), jnp.concatenate(grads, 0)
     dq = contract(k1, grads, 1, 1)
-    dk_ref[:, :keys] = contract(q, grads, 1, 0).astype(low_type)
-    dv_ref[:, :keys] = contract(do, weights, 1, 0).astype(low_type)
+    dk = contract(q, grads, 1, 0).astype(low_type)
+    dv = contract(do, weights, 1, 0).astype(low_type)
+    far_ref[0] = dk[:, :far]
+    far_ref[1] = dv[:, :far]
+    at = lax.broadcasted_iota(jnp.int32, (TILE, TILE), 0)
+    to = lax.broadcasted_iota(jnp.int32, (TILE, TILE), 1)
+    mirror = (at + to == TILE - 1).astype(high_type).astype(low_type)
+    flipped = contract(mirror, jnp.concatenate(nears, 1), 1, 0)
+    turned = [
+        pltpu.roll(flipped[:, i : i + 2 * TILE], TILE + 1, 1, stride=1, stride_axis=0).astype(low_type)
+        for i in range(0, 2 * n, 2 * TILE)
+    ]
+    top, rest = split_two(contract(table, jnp.concatenate(turned, 0), 1, 1))
+    stacked = [part[:, i : i + TILE] for i in range(0, n, TILE) for part in (top, rest)]
+    both = contract(jnp.concatenate(stacked, 0), mirror, 1, 0)
+    rels = [
+        both[i : i + BUCKETS] + both[i + BUCKETS : i + 2 * BUCKETS]
+        for i in range(0, both.shape[0], 2 * BUCKETS)
+    ]
     row_sums = dq[SIZE + 1 : SIZE + 2]
-    own_k = k_ref[:, keys:].astype(high_type)
-    own_v = v_ref[:, keys:].astype(high_type)
+    own_k, own_v = own_k.astype(high_type), own_v.astype(high_type)
     own_q, own_do = q[:, T:].astype(high_type), do_high[:, T:]
     own = jnp.sum(own_q * own_k, 0, keepdims=True) + rel[0:1, T:]
     own_part = jnp.exp(own - total[:, T:])
@@ -249,12 +255,73 @@
     own_grad = own_grad.astype(low_type).astype(high_type)
     dq_ref[:, :T] = (dq[:SIZE, :T] * SCALE).astype(low_type)
     dq_ref[:, T:] = ((dq[:SIZE, T:] + own_grad * own_k) * SCALE).astype(low_type)
-    dk_ref[:, keys:] = (own_grad * own_q).astype(low_type)
-    dv_ref[:, keys:] = (own_part.astype(low_type).astype(high_type) * own_do).astype(low_type)
+    dkv_ref[0, :, :T] = dk[:, far:]
+    dkv_ref[1, :, :T] = dv[:, far:]
+    dkv_ref[0, :, T:] = (own_grad * own_q).astype(low_type)
+    dkv_ref[1, :, T:] = (own_part.astype(low_type).astype(high_type) * own_do).astype(low_type)
     bucket = lax.broadcasted_iota(jnp.int32, (BUCKETS, n), 0)
     drel = jnp.concatenate(rels, 1) + jnp.where(bucket == BUCKETS - 1, row_sums, 0.0)
     own_all = jnp.concatenate([jnp.zeros((1, T), high_type), own_grad], 1)
     drel_ref[...] = (drel + jnp.where(bucket == 0, own_all, 0.0)).astype(low_type)
+
+
+def weight_grads_kernel(*refs, sources, terms, parts, sums):
+    xs, rest = refs[: len(sources)], refs[len(sources) :]
+    turned = rest[-1]
+    count = max(place for step in terms for place, _ in step) + 1
+    gs, out_ref = rest[:count], rest[count]
+    e, c = pl.program_id(0), pl.program_id(1)
+
+    @pl.when((e == 0) & (c == 0))
+    def _():
+        start = 0
+        for x_ref, rows in zip(xs, sources, strict=True):
+            turned[:, start : start + rows] = x_ref[...].T
+            start += rows
+
+    for step, term in enumerate(terms):
+
+        @pl.when(c == step)
+        def _():
+            total = None
+            for place, (low_at, high_at) in term:
+                g = gs[place][...]
+                piece = contract(turned[:, low_at:high_at], g, 1, 1)
+                total = piece if total is None else total + piece
+                if sums[step]:
+                    line = contract(jnp.ones((8, high_at - low_at), low_type), g, 1, 1)
+                    held = line if place == term[0][0] else held + line
+            if sums[step]:
+                rest[count + 1][step] = held
+            total = total.astype(low_type)
+            for at, row, rows, halves in parts[step]:
+                if halves:
+                    kept = jnp.where(e < halves, total[row : row + rows], total[row + rows : row + 2 * rows])
+                else:
+                    kept = total[row : row + rows]
+                out_ref[at[0], at[1] : at[1] + rows, :] = kept
+
+
+def back_rows_kernel(*refs, pairs, base, joined):
+    gs, ws, rest = refs[:pairs], refs[pairs : 2 * pairs], refs[2 * pairs :]
+    turned = rest[-pairs:]
+    out_ref = rest[-pairs - 1]
+
+    @pl.when(pl.program_id(1) == 0)
+    def _():
+        for g_ref, t_ref in zip(gs, turned, strict=True):
+            t_ref[...] = g_ref[...].T
+
+    total = rest[0][...] if base else None
+    for t_ref, w_ref in zip(turned, ws, strict=True):
+        piece = contract(t_ref[...], w_ref[...], 1, 1)
+        total = piece if total is None else total + piece
+    if joined:
+        add = rest[1][...]
+        out_ref[: add.shape[0]] = (total[: add.shape[0]] + add).astype(low_type)
+        out_ref[add.shape[0] :] = total[add.shape[0] :].astype(low_type)
+    else:
+        out_ref[...] = total.astype(low_type)
 
 
 def per_head(rows, count):
@@ -313,46 +380,141 @@
     )(q, k, v, mark, o, total, do)
 
 
-def self_forward(q, k, v, rel, mark, table, T, S):
-    B, _, keys = mark.shape
+def self_call(body, b, inputs, more, earlier, T, S, outs, out_specs, products, name):
+    q, far, mark, table = inputs[0], inputs[3].shape[1], inputs[6], inputs[7]
     count = S * T
-    row, key, rels = per_head(SIZE, count), per_head(SIZE, keys + count - T), per_head(BUCKETS, count)
+    row = pl.BlockSpec((SIZE, count), lambda h: (h, b))
+    far_row = pl.BlockSpec((SIZE, far), lambda h: (h, 0))
+    total = pl.BlockSpec((None, None, 1, count), lambda h: (b, h, 0, 0))
+    specs = [row, row, row, far_row, far_row, pl.BlockSpec((BUCKETS, count), lambda h: (h, b))]
+    specs.append(pl.BlockSpec((None, 16, far + T), lambda h: (b, 0, 0)))
+    specs.append(pl.BlockSpec(table.shape, lambda h: (0, 0)))
+    specs += [row, total, row][: len(more)]
+    held = len(specs)
     return pl.pallas_call(
-        functools.partial(self_forward_kernel, T=T, S=S),
-        grid=(B, HEADS),
-        in_specs=[row, key, key, rels, per_sequence(keys), pl.BlockSpec(table.shape, lambda b, h: (0, 0))],
-        out_specs=[row, per_total(count)],
-        out_shape=[like(q), jax.ShapeDtypeStruct((B, HEADS, 1, count), high_type)],
-        cost_estimate=cost(B, count, keys, 2),
+        functools.partial(body, T=T, S=S),
+        grid=(HEADS,),
+        in_specs=specs + [pl.BlockSpec(memory_space=pl.ANY)] * len(earlier),
+        out_specs=out_specs,
+        out_shape=outs,
+        input_output_aliases={held + i: i for i in range(len(earlier))},
+        cost_estimate=cost(1, count, far + T, products),
         compiler_params=pltpu.CompilerParams(vmem_limit_bytes=VMEM_LIMIT),
-        name="self_forward",
-    )(q, k, v, rel, mark, table)
-
-
-def self_backward(q, k, v, rel, mark, table, o, total, do, T, S):
-    B, _, keys = mark.shape
-    count = S * T
-    row, key, rels = per_head(SIZE, count), per_head(SIZE, keys + count - T), per_head(BUCKETS, count)
+        name=name,
+    )(*inputs, *more, *earlier)
+
+
+def self_forward(b, inputs, earlier, T, S):
+    q, mark, count = inputs[0], inputs[6], S * T
+    return self_call(
+        self_forward_kernel,
+        b,
+        inputs,
+        (),
+        earlier,
+        T,
+        S,
+        [like(q), jax.ShapeDtypeStruct((mark.shape[0], HEADS, 1, count), high_type)],
+        [
+            pl.BlockSpec((SIZE, count), lambda h: (h, b)),
+            pl.BlockSpec((None, None, 1, count), lambda h: (b, h, 0, 0)),
+        ],
+        2,
+        "self_forward",
+    )
+
+
+def self_backward(b, inputs, more, earlier, T, S):
+    q, rel, count, far = inputs[0], inputs[5], S * T, inputs[3].shape[1]
+
+    def pair(columns):
+        return jax.ShapeDtypeStruct((2, q.shape[0], columns), low_type)
+
+    return self_call(
+        self_backward_kernel,
+        b,
+        inputs,
+        more,
+        earlier,
+        T,
+        S,
+        [like(q), pair(q.shape[1]), like(rel), pair(far)],
+        [
+            pl.BlockSpec((SIZE, count), lambda h: (h, b)),
+            pl.BlockSpec((2, SIZE, count), lambda h: (0, h, b)),
+            pl.BlockSpec((BUCKETS, count), lambda h: (h, b)),
+            pl.BlockSpec((2, SIZE, far), lambda h: (0, h, 0)),
+        ],
+        5,
+        "self_backward",
+    )
+
+
+def weight_grads(xs, gs, specs, terms, parts, sums, out, name):
+    width = xs[0].shape[1]
+    columns = out[2] // 4
+    sources = [x.shape[0] for x in xs]
+    outs = [jax.ShapeDtypeStruct(out, low_type)]
+    out_specs = [pl.BlockSpec((out[0], out[1], columns), lambda e, c: (0, 0, e))]
+    if any(sums):
+        outs.append(jax.ShapeDtypeStruct((len(terms), 8, out[2]), high_type))
+        out_specs.append(pl.BlockSpec((len(terms), 8, columns), lambda e, c: (0, 0, e)))
+    flops = sum(2 * width * out[2] * (b - a) for term in terms for _, (a, b) in term)
     return pl.pallas_call(
-        functools.partial(self_backward_kernel, T=T, S=S),
-        grid=(B, HEADS),
-        in_specs=[
-            row,
-            key,
-            key,
-            rels,
-            per_sequence(keys),
-            pl.BlockSpec(table.shape, lambda b, h: (0, 0)),
-            row,
-            per_total(count),
-            row,
-        ],
-        out_specs=[row, key, key, rels],
-        out_shape=[like(q), like(k), like(v), like(rel)],
-        cost_estimate=cost(B, count, keys, 5),
+        functools.partial(
+            weight_grads_kernel, sources=sources, terms=terms, parts=parts, sums=sums
+        ),
+        grid=(4, len(terms)),
+        in_specs=[pl.BlockSpec(x.shape, lambda e, c: (0, 0)) for x in xs] + specs,
+        out_specs=out_specs,
+        out_shape=outs,
+        scratch_shapes=[pltpu.VMEM((width, sum(sources)), low_type)],
+        cost_estimate=pl.CostEstimate(
+            flops=flops, bytes_accessed=2 * width * (sum(sources) * 2 + out[2]), transcendentals=0
+        ),
         compiler_params=pltpu.CompilerParams(vmem_limit_bytes=VMEM_LIMIT),
-        name="self_backward",
-    )(q, k, v, rel, mark, table, o, total, do)
+        name=name,
+    )(*xs, *gs)
+
+
+def back_rows(gs, ws, base, joined, tile, name):
+    width, columns = 1024, 256
+
+    def spec(entry, shape, index):
+        if isinstance(entry, tuple):
+            return pl.BlockSpec((None,) + shape, lambda r, d, w=entry[1]: (w,) + index(r, d))
+        return pl.BlockSpec(shape, index)
+
+    arrays = [e[0] if isinstance(e, tuple) else e for e in gs]
+    weights = [e[0] if isinstance(e, tuple) else e for e in ws]
+    rows = arrays[0].shape[-1]
+    sizes = [a.shape[-2] for a in arrays]
+    specs = [spec(e, (f, tile), lambda r, d: (0, r)) for e, f in zip(gs, sizes, strict=True)]
+    specs += [spec(e, (columns, f), lambda r, d: (d, 0)) for e, f in zip(ws, sizes, strict=True)]
+    extra = []
+    if base is not None:
+        specs.append(pl.BlockSpec((tile, columns), lambda r, d: (r, d)))
+        extra.append(base)
+    if joined is not None:
+        specs.append(pl.BlockSpec((joined.shape[0] * tile // rows, columns), lambda r, d: (r, d)))
+        extra.append(joined)
+    return pl.pallas_call(
+        functools.partial(
+            back_rows_kernel, pairs=len(gs), base=base is not None, joined=joined is not None
+        ),
+        grid=(rows // tile, width // columns),
+        in_specs=specs,
+        out_specs=pl.BlockSpec((tile, columns), lambda r, d: (r, d)),
+        out_shape=jax.ShapeDtypeStruct((rows, width), low_type),
+        scratch_shapes=[pltpu.VMEM((tile, f), low_type) for f in sizes],
+        cost_estimate=pl.CostEstimate(
+            flops=2 * rows * width * sum(sizes),
+            bytes_accessed=2 * (rows + width) * sum(sizes) + 6 * rows * width,
+            transcendentals=0,
+        ),
+        compiler_params=pltpu.CompilerParams(vmem_limit_bytes=VMEM_LIMIT),
+        name=name,
+    )(*arrays, *weights, *extra)
 
 
 def ffn_kernel(x_ref, w_ref, b_ref, g_ref, slope_ref):
@@ -952,7 +1114,7 @@
     norm_bias,
 ):
     B, S, T, width = hidden.shape
-    if T % TILE:
+    if T % TILE or lax.axis_size("dp") != 8 or width % (32 * 8 * lax.axis_size("seq")):
         return plain_on_device(
             hidden,
             encoder_out,
@@ -986,23 +1148,38 @@
     self_bias, cross_bias = self_qv_bias.astype(high_type), cross_qv_bias.astype(high_type)
     table = jnp.asarray(bucket_table(), low_type)
 
+    after = lax.optimization_barrier
     x = hidden.reshape(B * S * T, width)
     rows = B * S * T
-    moving, pieces = hidden[:, 0], []
-    for _ in range(seq_parts - 1):
-        moving = lax.ppermute(moving, "seq", up)
-        pieces.append(moving)
-    x_all = jnp.concatenate(pieces[::-1] + [hidden.reshape(B, S * T, width)], 1)
-    x_keys = x_all.reshape(-1, width)
+    far_rows, held = [], None
+    for b in range(B):
+        moving, pieces = hidden[b, 0], []
+        if held is not None:
+            moving, held = after((moving, held))
+        for _ in range(seq_parts - 1):
+            moving = lax.ppermute(moving, "seq", up)
+            pieces.append(moving)
+        held = moving
+        far_rows.append(jnp.concatenate(pieces[::-1], 0))
+    e_own, far_rows[0] = after((encoder_out, far_rows[0]))
+    e_all = lax.all_gather(e_own, "seq", axis=1, tiled=True).reshape(-1, width)
     key_at = place * T - far + jnp.arange(keys, dtype=jnp.int32)
     self_mark = key_features((key_at >= 0) & (key_at < dec_lengths[:, None]))
     cross_mark = key_features(jnp.arange(keys, dtype=jnp.int32) < enc_lengths[:, None])
 
     q = ((dot("de,rd->er", self_qkv[0], x) + self_bias[0][:, None]) * SCALE).astype(low_type)
     rel = dot("db,rd->br", rel_weight, x) + rel_bias.astype(high_type)[:, None]
-    k = dot("de,rd->er", self_qkv[1], x_keys).astype(low_type)
-    v = (dot("de,rd->er", self_qkv[2], x_keys) + self_bias[1][:, None]).astype(low_type)
-    attended, self_total = self_forward(q, k, v, rel, self_mark, table, T, S)
+    k = dot("de,rd->er", self_qkv[1], x).astype(low_type)
+    v = (dot("de,rd->er", self_qkv[2], x) + self_bias[1][:, None]).astype(low_type)
+    self_inputs, results = [], ()
+    for b in range(B):
+        k_far = dot("de,rd->er", self_qkv[1], far_rows[b]).astype(low_type)
+        v_far = (dot("de,rd->er", self_qkv[2], far_rows[b]) + self_bias[1][:, None]).astype(
+            low_type
+        )
+        self_inputs.append((q, k, v, k_far, v_far, rel, self_mark, table))
+        results = self_forward(b, self_inputs[b], results, T, S)
+    attended, self_total = results
     first_sum = (
         x.astype(high_type)
         + dot("er,ed->rd", attended, self_out)
@@ -1012,7 +1189,6 @@
     first_norm = first_unit * gains[0] + shifts[0]
     first_low = first_norm.astype(low_type)
 
-    e_all = lax.all_gather(encoder_out, "seq", axis=1, tiled=True).reshape(-1, width)
     qc = ((dot("de,rd->er", cross_qkv[0], first_low) + cross_bias[0][:, None]) * SCALE).astype(
         low_type
     )
@@ -1041,88 +1217,190 @@
     grad_ffn = grad_third.astype(low_type)
 
     def over_dp(piece):
-        return lax.psum_scatter(piece.astype(low_type), "dp", scatter_dimension=0, tiled=True)
-
-    def over_seq(piece):
-        return (
-            lax.psum_scatter(piece, "seq", scatter_dimension=0, tiled=True)
-            .astype(high_type)
-            .reshape(-1)
-        )
-
+        return lax.psum_scatter(piece, "dp", scatter_dimension=0, tiled=True)
+
+    def over_dp_by_steps(piece, meanwhile):
+        me = lax.axis_index("dp")
+
+        def swap(pair, bit):
+            mine = (me >> bit) & 1
+            sent = lax.dynamic_index_in_dim(pair, 1 - mine, 0, keepdims=False)
+            kept = lax.dynamic_index_in_dim(pair, mine, 0, keepdims=False)
+            came = lax.ppermute(sent, "dp", [(i, i ^ (1 << bit)) for i in range(8)])
+            return low(came.astype(high_type) + kept.astype(high_type))
+
+        count = piece.shape[0] // 8
+        chip = swap(jnp.swapaxes(piece.reshape(4, 2, count, width), 0, 1), 0)
+        chip, meanwhile = after((chip, meanwhile))
+        first, second = chip[:, : count // 2], chip[:, count // 2 :]
+        first = swap(jnp.swapaxes(first.reshape(2, 2, count // 2, width), 0, 1), 1)
+        second = swap(second.reshape(2, 2, count // 2, width), 2)
+        return jnp.concatenate([swap(first, 2), swap(second, 1)], 0), meanwhile
+
+    def over_seq(*pieces):
+        cut = [piece.reshape(seq_parts, -1, width) for piece in pieces]
+        joined = jnp.concatenate(cut, 1)
+
+        def block(hop):
+            return lax.dynamic_index_in_dim(
+                joined, (place - hop) % seq_parts, 0, keepdims=False
+            ).astype(high_type)
+
+        ring = [(i, (i + 1) % seq_parts) for i in range(seq_parts)]
+        held = block(1)
+        for hop in range(2, seq_parts + 1):
+            held = lax.ppermute(held.astype(low_type), "seq", ring).astype(high_type) + block(hop)
+        ends = np.cumsum([piece.shape[1] for piece in cut])
+        return [
+            held[end - piece.shape[1] : end].reshape(-1)
+            for piece, end in zip(cut, ends, strict=True)
+        ]
+
+    def low(value):
+        return value.astype(low_type)
+
+    part_ffn_out, grad_ffn = after((low(dot("rf,rd->fd", activated, grad_ffn)), grad_ffn))
+    mat_ffn_out = over_dp(part_ffn_out)
     grad_pre = (dot("rd,fd->rf", grad_ffn, ffn_out) * slope.astype(high_type)).astype(low_type)
-    mat_ffn_out = over_dp(dot("rf,rd->fd", activated, grad_ffn))
-    mat_ffn_in = over_dp(dot("rd,rf->df", second_low, grad_pre))
+    part_ffn_in, grad_pre = after((low(dot("rd,rf->df", second_low, grad_pre)), grad_pre))
+    mat_ffn_in = over_dp(part_ffn_in)
     grad_second = grad_third + dot("rf,df->rd", grad_pre, ffn_in)
     grad_second_sum, grad_gain_cross, grad_shift_cross = norm_back(
         second_sum, grad_second, gains[1]
     )
     grad_cross = grad_second_sum.astype(low_type)
-    mat_cross_out = over_dp(dot("er,rd->ed", cross_mixed, grad_cross))
+    part_cross_out, grad_cross = after((low(dot("er,rd->ed", cross_mixed, grad_cross)), grad_cross))
+    mat_cross_out = over_dp(part_cross_out)
     grad_cross_mixed = dot("ed,rd->er", cross_out, grad_cross).astype(low_type)
     dqc, dkc, dvc = cross_backward(
         qc, kc, vc, cross_mark, cross_mixed, cross_total, grad_cross_mixed
     )
-    grad_encoder = dot("er,de->rd", dkc, cross_qkv[1]) + dot("er,de->rd", dvc, cross_qkv[2])
-    grad_encoder = lax.psum_scatter(
-        grad_encoder.astype(low_type).reshape(B, keys, width),
-        "seq",
-        scatter_dimension=1,
-        tiled=True,
-    )
-    mat_cross_qkv = over_dp(
-        jnp.concatenate(
-            [
-                dot("rd,er->de", first_low, dqc),
-                dot("rd,er->de", e_all, dkc),
-                dot("rd,er->de", e_all, dvc),
-            ]
-        )
-    )
+    dqc, dkc, dvc, mat_ffn_out, mat_ffn_in = after((dqc, dkc, dvc, mat_ffn_out, mat_ffn_in))
+    done_ffn_in, done_ffn_out = over_seq(mat_ffn_in, mat_ffn_out)
+    part_encoder = back_rows(
+        (dkc, dvc), ((cross_qkv, 1), (cross_qkv, 2)), None, None, keys, "encoder_rows"
+    ).reshape(B, keys, width)
+    third = 3 * width // 8
+
+    def cut(step, size, blocks):
+        found = []
+        for block in range(blocks):
+            low_at, high_at = max(size * block, width * step), min(size * (block + 1), width * (step + 1))
+            if low_at < high_at:
+                found.append(((block, low_at - size * block), low_at - width * step, high_at - low_at, 0))
+        return found
+
+    quarter = width // 4
+    (part_cross_qkv,) = weight_grads(
+        (first_low, e_all),
+        (dqc, dkc, dvc),
+        [
+            pl.BlockSpec((quarter, rows), lambda e, c: (e, 0)),
+            pl.BlockSpec((quarter, B * keys), lambda e, c: (e, 0)),
+            pl.BlockSpec((quarter, B * keys), lambda e, c: (e, 0)),
+        ],
+        [[(0, (0, rows))], [(1, (rows, rows + B * keys))], [(2, (rows, rows + B * keys))]],
+        [cut(step, third, 8) for step in range(3)],
+        [False] * 3,
+        (8, third, width),
+        "cross_weights",
+    )
+    part_cross_qkv = part_cross_qkv.reshape(3 * width, width)
+    part_encoder, part_cross_qkv, dqc = after((part_encoder, part_cross_qkv, dqc))
+    mat_cross_qkv = over_dp(part_cross_qkv)
+
+    def positions(hop):
+        at = (place + hop) % seq_parts
+        return lax.dynamic_slice_in_dim(part_encoder, at * T, T, 1)
+
+    encoder_parts = [positions(0)] + [
+        lax.ppermute(positions(hop), "seq", [(i, (i + hop) % seq_parts) for i in range(seq_parts)])
+        for hop in range(1, seq_parts)
+    ]
     grad_first = grad_second_sum + dot("er,de->rd", dqc, cross_qkv[0])
     grad_first_sum, grad_gain_self, grad_shift_self = norm_back(first_sum, grad_first, gains[0])
     grad_self = grad_first_sum.astype(low_type)
-    mat_self_out = over_dp(dot("er,rd->ed", attended, grad_self))
+    part_self_out, grad_self = after((low(dot("er,rd->ed", attended, grad_self)), grad_self))
+    mat_self_out = over_dp(part_self_out)
     grad_attended = dot("ed,rd->er", self_out, grad_self).astype(low_type)
-    dq, dk, dv, drel = self_backward(
-        q, k, v, rel, self_mark, table, attended, self_total, grad_attended, T, S
-    )
-    count = far + S * T
-    dk_parts, dv_parts = dk.reshape(width, B, count), dv.reshape(width, B, count)
-    away = dot("ebr,de->brd", dk_parts[:, :, :far], self_qkv[1]) + dot(
-        "ebr,de->brd", dv_parts[:, :, :far], self_qkv[2]
-    )
-    away = away.astype(low_type)
-    moving = away[:, :T]
-    for hop in range(1, seq_parts):
-        moving = lax.ppermute(moving, "seq", down).astype(high_type)
-        if hop < seq_parts - 1:
-            moving = (moving + away[:, hop * T : (hop + 1) * T].astype(high_type)).astype(low_type)
-    home = (
-        grad_first_sum.reshape(B, S * T, width)
-        + dot("ebr,de->brd", dq.reshape(width, B, S * T), self_qkv[0])
-        + dot("ebr,de->brd", dk_parts[:, :, far:], self_qkv[1])
-        + dot("ebr,de->brd", dv_parts[:, :, far:], self_qkv[2])
-        + dot("jbr,dj->brd", drel.reshape(-1, B, S * T), rel_weight)
-    ).reshape(B, S, T, width)
-    mat_self_qkv = over_dp(
-        jnp.concatenate(
+    grad_attended, done_ffn_in, done_ffn_out = after((grad_attended, done_ffn_in, done_ffn_out))
+    results, came = (), []
+    for b in range(B):
+        *results, far_grads = self_backward(
+            b, self_inputs[b], (attended, self_total, grad_attended), tuple(results), T, S
+        )
+        if b:
+            far_grads, came[b - 1] = after((far_grads, came[b - 1]))
+        away = back_rows(
+            ((far_grads, 0), (far_grads, 1)), ((self_qkv, 1), (self_qkv, 2)), None, None, far, "far_rows"
+        )
+        if b == 0:
+            far_columns = [far_grads]
+        else:
+            far_columns.append(far_grads)
+        came.append(
             [
-                dot("rd,er->de", x, dq),
-                dot("rd,er->de", x_keys, dk),
-                dot("rd,er->de", x_keys, dv),
+                lax.ppermute(
+                    away[(seq_parts - 1 - hop) * T : (seq_parts - hop) * T],
+                    "seq",
+                    [(i + hop, i) for i in range(seq_parts - hop)],
+                )
+                for hop in range(1, seq_parts)
             ]
         )
-    )
-    mat_rel = over_dp(dot("rd,jr->dj", x, drel))
-    grad_hidden = jnp.concatenate(
-        [(home[:, :1] + moving[:, None]).astype(low_type), home[:, 1:].astype(low_type)], 1
-    )
-
+        if b + 1 < B:
+            results[0], self_inputs[b + 1], away, encoder_parts = after(
+                (results[0], self_inputs[b + 1], away, encoder_parts)
+            )
+            grad_encoder = functools.reduce(
+                jnp.add, [piece.astype(high_type) for piece in encoder_parts]
+            ).astype(low_type)
+    results[0], away = after((results[0], away))
+    dq, dkv, drel = results
+    blocks, size, rel_size = 8 * seq_parts, 3 * width // (8 * seq_parts), width // (16 * seq_parts)
+    near_at, far_at = (0, rows), [(rows + b * far, rows + (b + 1) * far) for b in range(B)]
+    part_self, part_sums = weight_grads(
+        (x, *far_rows),
+        (dq, dkv, dkv, drel) + tuple(far_columns) * 2,
+        [
+            pl.BlockSpec((quarter, rows), lambda e, c: (e, 0)),
+            pl.BlockSpec((None, quarter, rows), lambda e, c: (0, e, 0)),
+            pl.BlockSpec((None, quarter, rows), lambda e, c: (1, e, 0)),
+            pl.BlockSpec((quarter, rows), lambda e, c: (e % 2, 0)),
+        ]
+        + [pl.BlockSpec((None, quarter, far), lambda e, c: (0, e, 0))] * B
+        + [pl.BlockSpec((None, quarter, far), lambda e, c: (1, e, 0))] * B,
+        [
+            [(0, near_at)],
+            [(1, near_at)] + [(4 + b, far_at[b]) for b in range(B)],
+            [(2, near_at)] + [(4 + B + b, far_at[b]) for b in range(B)],
+            [(3, near_at)],
+        ],
+        [cut(step, size, blocks) for step in range(3)]
+        + [[((block, size), 2 * rel_size * block, rel_size, 2) for block in range(blocks)]],
+        [True, False, True, True],
+        (blocks, size + rel_size, width),
+        "self_weights",
+    )
+    part_self, came[-1] = after((part_self, came[-1]))
+    mat_self, (dq, mat_cross_out, mat_cross_qkv, mat_self_out, part_sums) = over_dp_by_steps(
+        part_self.reshape(-1, width), (dq, mat_cross_out, mat_cross_qkv, mat_self_out, part_sums)
+    )
+    moved = jnp.concatenate(
+        [functools.reduce(jnp.add, [piece.astype(high_type) for piece in came[b]]) for b in range(B)], 0
+    )
+    grad_hidden = back_rows(
+        (dq, (dkv, 0), (dkv, 1), drel),
+        ((self_qkv, 0), (self_qkv, 1), (self_qkv, 2), rel_weight),
+        grad_first_sum,
+        moved,
+        S * T,
+        "near_rows",
+    ).reshape(hidden.shape)
     vectors = [
-        jnp.stack([row_sum(dq), row_sum(dv)]),
+        jnp.stack([part_sums[0, 0], part_sums[2, 0]]),
         column_sum(grad_self),
-        row_sum(drel),
+        part_sums[3, 0, : width // 2],
         jnp.stack([row_sum(dqc), row_sum(dvc)]),
         column_sum(grad_cross),
         column_sum(grad_pre),
@@ -1132,26 +1410,39 @@
     ]
     blocks = [piece.reshape(seq_parts, -1) for piece in vectors]
     ends = np.cumsum([piece.shape[1] for piece in blocks])
-    summed = lax.psum(jnp.concatenate(blocks, 1), ("dp", "seq"))
+    summed = jnp.concatenate(blocks, 1)
+    for axis, size_of in (("dp", 8), ("seq", seq_parts)):
+        for bit in range(size_of.bit_length() - 1):
+            summed = summed + lax.ppermute(summed, axis, [(i, i ^ (1 << bit)) for i in range(size_of)])
     mine = lax.dynamic_index_in_dim(summed, place, 0, keepdims=False)
+    done_cross_out, done_cross_qkv, done_self_out = over_seq(
+        mat_cross_out, mat_cross_qkv, mat_self_out
+    )
+    mat_self, mine, done_cross_out, grad_hidden = after((mat_self, mine, done_cross_out, grad_hidden))
+    (done_self,) = over_seq(mat_self)
+    done_self = done_self.reshape(size + rel_size, width)
+    done_self_qkv = done_self[:size].reshape(-1)
+    half = width // 2
+    done_rel = jnp.concatenate([done_self[size:, :half], done_self[size:, half:]], 0).reshape(-1)
+
     vecs = [mine[end - piece.shape[1] : end] for piece, end in zip(blocks, ends, strict=True)]
     return (
         output,
         grad_hidden,
         grad_encoder,
-        over_seq(mat_self_qkv),
+        done_self_qkv,
         vecs[0],
-        over_seq(mat_self_out),
+        done_self_out,
         vecs[1],
-        over_seq(mat_rel),
+        done_rel,
         vecs[2],
-        over_seq(mat_cross_qkv),
+        done_cross_qkv,
         vecs[3],
-        over_seq(mat_cross_out),
+        done_cross_out,
         vecs[4],
-        over_seq(mat_ffn_in),
+        done_ffn_in,
         vecs[5],
-        over_seq(mat_ffn_out),
+        done_ffn_out,
         vecs[6],
         vecs[7],
         vecs[8],

time: 1480 us -> 1010 us (0.68)
  waiting for transfers between devices: 593 us -> 102 us
  matrix products: 328 us -> 223 us
  starting transfers between devices: 42.9 us -> 130 us
  Pallas kernels: 345 us -> 409 us
  other arithmetic: 97.2 us -> 75.3 us
    reduce_scatter x14 -> x5, waiting for transfers between devices: 480 us -> 1.35 us  [over_dp(): return lax.psum_scatter(piece, 'dp', scatter_dimension=0, tiled=True)]
    dot_general x34 -> x23, matrix products: 328 us -> 223 us  [dot(): return jnp.einsum(spec, left, right, preferred_element_type=high_type)]
    ppermute x3 -> x28, starting transfers between devices: 4.34 us -> 91.7 us  [the longest x9 59.4 us: over_seq(): lax.ppermute(held.astype(low_type), 'seq', ring).astype(high_type)]
    pallas_call x2 -> x10, Pallas kernels: 194 us -> 258 us  [the longest x4 137 us: self_call(): pl.pallas_call(functools.partial(body, T=T, S=S), grid=(HEADS,), in_specs...]
    ppermute x3 -> x6, waiting for transfers between devices: 79.3 us -> 26.7 us  [on_device(): moving = lax.ppermute(moving, 'seq', up)]
    ppermute x3 -> x28, waiting for transfers between devices: 21.3 us -> 73.6 us  [the longest x9 59.7 us: over_seq(): lax.ppermute(held.astype(low_type), 'seq', ring).astype(high_type)]
    concatenate x4, other arithmetic: 37.9 us -> 5.65 us  [the longest x1 2.66 us: on_device(): far_rows.append(jnp.concatenate(pieces[::-1], 0))]
    convert_element_type x3 -> x16, other arithmetic: 5.93 us -> 33.7 us  [the longest x5 9.03 us: low(): return value.astype(low_type)]
  transfers between devices with their start and end apart: 23 -> 40, of which waited for: 18 -> 17; matrix products, arithmetic and copies ran while one was open for 22% -> 25% of each run, Pallas kernels for 5% -> 32%
where the time goes in v2:
time: 1010 us; the launch traced here: 996 us
  Pallas kernels  409 us (40%)
  matrix products  223 us (22%)
  starting transfers between devices  130 us (13%)
  waiting for transfers between devices  102 us (10%)
  other arithmetic  75.3 us (7%)
  local copies, waits for them, and re-layouts  42.3 us (4%)
  between operations  15.5 us (2%)
    dot_general x23, matrix products, dot(): return jnp.einsum(spec, left, right, preferred_element_type=high_type)  223 us
    pallas_call x4, Pallas kernels, self_call(): pl.pallas_call(functools.partial(body, T=T, S=S), grid=(HEADS,), in_specs...  137 us
    pallas_call x1, Pallas kernels, cross_backward(): pl.pallas_call(functools.partial(cross_backward_kernel, step=count // 2),...  65.3 us
    pallas_call x2, Pallas kernels, weight_grads(): pl.pallas_call(functools.partial(weight_grads_kernel, sources=sources, te...  62.5 us
    ppermute x9, waiting for transfers between devices, over_seq(): lax.ppermute(held.astype(low_type), 'seq', ring).astype(high_type)  59.7 us
    ppermute x9, starting transfers between devices, over_seq(): lax.ppermute(held.astype(low_type), 'seq', ring).astype(high_type)  59.4 us
    pallas_call x4, Pallas kernels, back_rows(): pl.pallas_call(functools.partial(back_rows_kernel, pairs=len(gs), base=ba...  58.4 us
    pallas_call x1, Pallas kernels, cross_forward(): pl.pallas_call(cross_forward_kernel, grid=(B, HEADS), in_specs=[per_head(...  46.1 us
  transfers between devices with their start and end apart: 40, of which 17 were waited for; matrix products, arithmetic and copies ran while one was open for 25% of the time, Pallas kernels for 32%

profile of v2, /device:TPU:0, one launch (start us, length us, event | category | flops | bytes accessed | tf_op | source)
XLA Modules:
  0.0 996.5 jit_solution(16845009349162036986)
XLA Ops:
  17.6 8.1 add_convert_fusion.2.refs_2_
  92.3 11.6 %collective-permute-done.4 = bf16[256,1024]{1,0:T(8,128)(2,1)S(1)} collective-permute-done((bf16[256,1024]{1,0:T(8,128)(2,1)S(1)}, bf16[256,1024]{1,0:T(8,128)(2,1)S(1)}, u32[]{:S(2)}, u32[]{:S(2)}) %collective-permute-start.4) | collective-permute-done | bytes 524320 | tf_op jit(solution)/shard_map/ppermute | solution.py:1160
  104.0 14.7 %collective-permute-start.5 = (bf16[256,1024]{1,0:T(8,128)(2,1)S(1)}, bf16[256,1024]{1,0:T(8,128)(2,1)S(1)}, u32[]{:S(2)}, u32[]{:S(2)}) collective-permute-start(bf16[256,1024]{1,0:T(8,128)(2,1)S(1)} %collective-permute-done.4), channel_id=1, source_target_pairs={{0,1},{1,2},{2,3},{4,5},{5,6},{6,7},{8,9},{9,10},{10,11},{12,13},{... | collective-permute-start | bytes 1572872 | tf_op jit(solution)/shard_map/ppermute | solution.py:1160
  118.7 26.8 %self_forward.2 = (bf16[1024,1536]{1,0:T(8,128)(2,1)}, f32[2,16,1,768]{3,2,1,0:T(1,128)}) custom-call(bf16[1024,1536]{1,0:T(8,128)(2,1)} %multiply_convert_fusion.2.refs_0_, bf16[1024,1536]{1,0:T(8,128)(2,1)} %convolution_convert_fusion.4.refs_1_, bf16[1024,1536]{1,0:T(8,128)(2,1)} %add_convert_fusion.2.refs_2_, bf16[1024,768]{1,0:T(8,128)(2,1)} %fusion.54.refs_3_, ...), custom_call_target="tpu_custom_call" | custom-call | flops 12884901888 | bytes 14680064 | tf_op jit(solution)/shard_map/self_forward/pallas_call | solution.py:394
  155.5 27.0 %self_forward.3 = (bf16[1024,1536]{1,0:T(8,128)(2,1)}, f32[2,16,1,768]{3,2,1,0:T(1,128)}) custom-call(bf16[1024,1536]{1,0:T(8,128)(2,1)} %multiply_convert_fusion.2.refs_0_, bf16[1024,1536]{1,0:T(8,128)(2,1)} %convolution_convert_fusion.4.refs_1_, bf16[1024,1536]{1,0:T(8,128)(2,1)} %add_convert_fusion.2.refs_2_, ...), custom_call_target="tpu_custom_call", output_to_operand_aliasing={{0}: (8, {}), {1}: (9, {})} | custom-call | flops 12884901888 | bytes 14680064 | tf_op jit(solution)/shard_map/self_forward/pallas_call | solution.py:394
  199.5 9.5 convert_bitcast_fusion.k_ref
  209.1 7.8 fusion.10.v_ref
  216.9 46.1 %cross_forward.1 = (bf16[1024,1536]{1,0:T(8,128)(2,1)}, f32[2,16,1,768]{3,2,1,0:T(1,128)}) custom-call(bf16[1024,1536]{1,0:T(8,128)(2,1)} %fusion.13.q_ref, bf16[1024,2048]{1,0:T(8,128)(2,1)} %convert_bitcast_fusion.k_ref, bf16[1024,2048]{1,0:T(8,128)(2,1)} %fusion.10.v_ref, bf16[2,16,1024]{2,1,0:T(8,128)(2,1)} %get-tuple-element.227.mark_ref), custom_call_target="tpu_custom_call" | custom-call | flops 25769803776 | bytes 29360128 | tf_op jit(solution)/shard_map/cross_forward/pallas_call | solution.py:354
  263.1 8.6 fusion.95
  275.3 39.7 %ffn_first.1 = (bf16[1536,4096]{1,0:T(8,128)(2,1)}, bf16[1536,4096]{1,0:T(8,128)(2,1)}) custom-call(bf16[1536,1024]{1,0:T(8,128)(2,1)} %fusion.9.x_ref, bf16[1024,4096]{1,0:T(8,128)(2,1)} %w_ref.1, f32[1,4096]{1,0:T(1,128)} %bitcast.296), custom_call_target="tpu_custom_call" | custom-call | flops 12884901888 | bytes 25165824 | tf_op jit(solution)/shard_map/ffn_first/pallas_call | solution.py:541
  315.0 19.9 %fusion.96 = (f32[1536]{0:T(1024)S(1)}, f32[1536,1024]{1,0:T(8,128)S(1)}) fusion(f32[1024]{0:T(1024)S(1)} %copy-done.40, bf16[1536,4096]{1,0:T(8,128)(2,1)} %get-tuple-element.101, bf16[4096,1024]{1,0:T(8,128)(2,1)} %param.39, f32[1024]{0:T(1024)S(1)} %bitcast.291, f32[1024]{0:T(1024)S(1)} %bitcast.284, f32[1536]{0:T(1024)S(1)} %add_rsqrt_fusion.1, ...), kind=kOutput, calls=%fused_computation.217 | convolution fusion | flops 12895909888 | bytes 33585152 | tf_op jit(solution)/shard_map/rf,fd->rd/dot_general | solution.py:568
  347.7 15.3 %convolution_convert_fusion.1 = bf16[4096,1024]{1,0:T(8,128)(2,1)} fusion(bf16[1536,4096]{1,0:T(8,128)(2,1)S(1)} %bitcast.312, bf16[1536,1024]{1,0:T(8,128)(2,1)S(1)} %get-tuple-element.103), kind=kOutput, calls=%fused_computation.5 | convolution fusion | flops 12889096192 | bytes 24117248 | tf_op jit(solution)/shard_map/rf,rd->fd/dot_general | solution.py:568
  363.1 22.1 %multiply_convert_fusion = bf16[1536,4096]{1,0:T(8,128)(2,1)} fusion(bf16[1536,4096]{1,0:T(8,128)(2,1)} %get-tuple-element.104, bf16[1536,1024]{1,0:T(8,128)(2,1)} %copy-done.8, bf16[4096,1024]{1,0:T(8,128)(2,1)} %param.39), kind=kOutput, calls=%fused_computation.1 | convolution fusion | flops 12903776256 | bytes 36700160 | tf_op jit(solution)/shard_map/rd,fd->rf/dot_general | solution.py:568
  385.2 20.7 %convolution_convert_fusion = bf16[1024,4096]{1,0:T(8,128)(2,1)} fusion(bf16[1536,1024]{1,0:T(8,128)(2,1)} %fusion.9.x_ref, bf16[1536,4096]{1,0:T(8,128)(2,1)} %multiply_convert_fusion), kind=kOutput, calls=%fused_computation.4 | convolution fusion | flops 12889096192 | bytes 24117248 | tf_op jit(solution)/shard_map/rd,rf->df/dot_general | solution.py:568
  405.9 26.4 %multiply_reduce_fusion = (f32[1024]{0:T(1024)}, f32[1536]{0:T(1024)S(1)}, f32[1536]{0:T(1024)S(1)}, f32[1024]{0:T(1024)}, f32[1536,1024]{1,0:T(8,128)}) fusion(f32[1536,1024]{1,0:T(8,128)} %copy-done.4, f32[1536]{0:T(1024)S(1)} %add_rsqrt_fusion.1, f32[1536]{0:T(1024)S(1)} %broadcast_multiply_fusion.7, f32[1024]{0:T(1024)S(1)} %bitcast.285, ...), kind=kOutput, calls=%fused_computation.19 | convolution fusion | flops 12900625408 | bytes 39882752 | tf_op jit(solution)/shard_map/rf,df->rd/dot_general | solution.py:568
  453.0 65.3 %cross_backward.1 = (bf16[1024,1536]{1,0:T(8,128)(2,1)}, bf16[1024,2048]{1,0:T(8,128)(2,1)}, bf16[1024,2048]{1,0:T(8,128)(2,1)}) custom-call(bf16[1024,1536]{1,0:T(8,128)(2,1)} %fusion.13.q_ref, bf16[1024,2048]{1,0:T(8,128)(2,1)} %convert_bitcast_fusion.k_ref, bf16[1024,2048]{1,0:T(8,128)(2,1)} %fusion.10.v_ref, ...), custom_call_target="tpu_custom_call" | custom-call | flops 64424509440 | bytes 73400320 | tf_op jit(solution)/shard_map/cross_backward/pallas_call | solution.py:370
  519.7 18.1 %encoder_rows.1 = bf16[2048,1024]{1,0:T(8,128)(2,1)} custom-call(bf16[1024,2048]{1,0:T(8,128)(2,1)} %get-tuple-element.113.refs_0_.refs_3_, bf16[1024,2048]{1,0:T(8,128)(2,1)} %get-tuple-element.114.refs_1_.refs_4_, bf16[3,1024,1024]{2,1,0:T(8,128)(2,1)} %refs_3_.3, bf16[3,1024,1024]{2,1,0:T(8,128)(2,1)} %refs_3_.3), custom_call_target="tpu_custom_call" | custom-call | flops 8589934592 | bytes 25165824 | tf_op jit(solution)/shard_map/encoder_rows/pallas_call | solution.py:501
  537.9 23.5 %cross_weights.1 = bf16[8,384,1024]{2,1,0:T(8,128)(2,1)} custom-call(bf16[1536,1024]{1,0:T(8,128)(2,1)} %copy-done.12, bf16[2048,1024]{1,0:T(8,128)(2,1)} %bitcast.309, bf16[1024,1536]{1,0:T(8,128)(2,1)} %get-tuple-element.116.refs_2_, bf16[1024,2048]{1,0:T(8,128)(2,1)} %get-tuple-element.113.refs_0_.refs_3_, ...), custom_call_target="tpu_custom_call" | custom-call | flops 11811160064 | bytes 16777216 | tf_op jit(solution)/shard_map/cross_weights/pallas_call | solution.py:463
  561.4 11.4 %multiply_reduce_fusion.1 = (f32[1024]{0:T(1024)S(1)}, f32[1536]{0:T(1024)S(1)}, f32[1536]{0:T(1024)S(1)}, f32[1024]{0:T(1024)S(1)}, f32[1536,1024]{1,0:T(8,128)S(1)}) fusion(f32[1536,1024]{1,0:T(8,128)} %copy-done.3, f32[1536]{0:T(1024)S(1)} %copy-done.25, f32[1536]{0:T(1024)S(1)} %copy-done.23, f32[1024]{0:T(1024)S(1)} %bitcast.281, ...), kind=kOutput, calls=%fused_computation.20 | convolution fusion | flops 3236948992 | bytes 24154112 | tf_op jit(solution)/shard_map/er,de->rd/dot_general | solution.py:568
  589.5 12.3 %collective-permute-done.6 = bf16[256,1024]{1,0:T(8,128)(2,1)S(1)} collective-permute-done((bf16[256,1024]{1,0:T(8,128)(2,1)S(1)}, bf16[256,1024]{1,0:T(8,128)(2,1)S(1)}, u32[]{:S(2)}, u32[]{:S(2)}) %collective-permute-start.6) | collective-permute-done | bytes 524320 | tf_op jit(solution)/shard_map/ppermute | solution.py:1252
  621.5 42.1 %collective-permute-start.8 = (bf16[256,1024]{1,0:T(8,128)(2,1)S(1)}, bf16[256,1024]{1,0:T(8,128)(2,1)S(1)}, u32[]{:S(2)}, u32[]{:S(2)}) collective-permute-start(bf16[256,1024]{1,0:T(8,128)(2,1)S(1)} %fusion.60), channel_id=1, source_target_pairs={{0,1},{1,2},{2,3},{3,0},{4,5},{5,6},{6,7},{7,4},{8,9},{9,10},{10,1... | collective-permute-start | bytes 1572872 | tf_op jit(solution)/shard_map/ppermute | solution.py:1252
  663.7 8.6 fusion.12.refs_10_
  672.2 18.7 %collective-permute-done.8 = bf16[256,1024]{1,0:T(8,128)(2,1)S(1)} collective-permute-done((bf16[256,1024]{1,0:T(8,128)(2,1)S(1)}, bf16[256,1024]{1,0:T(8,128)(2,1)S(1)}, u32[]{:S(2)}, u32[]{:S(2)}) %collective-permute-start.8) | collective-permute-done | bytes 524320 | tf_op jit(solution)/shard_map/ppermute | solution.py:1252
  693.0 41.3 %self_backward.2 = (bf16[1024,1536]{1,0:T(8,128)(2,1)}, bf16[2,1024,1536]{2,1,0:T(8,128)(2,1)}, bf16[512,1536]{1,0:T(8,128)(2,1)}, bf16[2,1024,768]{2,1,0:T(8,128)(2,1)}) custom-call(bf16[1024,1536]{1,0:T(8,128)(2,1)} %multiply_convert_fusion.2.refs_0_, bf16[1024,1536]{1,0:T(8,128)(2,1)} %convolution_convert_fusion.4.refs_1_, ...), custom_call_target="tpu_custom_call" | custom-call | flops 32212254720 | bytes 36700160 | tf_op jit(solution)/shard_map/self_backward/pallas_call | solution.py:394
  734.4 8.4 far_rows.2
  748.2 41.7 %self_backward.3 = (bf16[1024,1536]{1,0:T(8,128)(2,1)}, bf16[2,1024,1536]{2,1,0:T(8,128)(2,1)}, bf16[512,1536]{1,0:T(8,128)(2,1)}, bf16[2,1024,768]{2,1,0:T(8,128)(2,1)}) custom-call(bf16[1024,1536]{1,0:T(8,128)(2,1)} %multiply_convert_fusion.2.refs_0_, ...), custom_call_target="tpu_custom_call", output_to_operand_aliasing={{0}: (11, {}), {1}: (12, {}), {2}: (13, {})} | custom-call | flops 32212254720 | bytes 36700160 | tf_op jit(solution)/shard_map/self_backward/pallas_call | solution.py:394
  790.0 8.6 far_rows.3
  803.9 39.0 %self_weights.1 = (bf16[32,112,1024]{2,1,0:T(8,128)(2,1)}, f32[4,8,1024]{2,1,0:T(8,128)}) custom-call(bf16[1536,1024]{1,0:T(8,128)(2,1)} %bitcast.267, bf16[768,1024]{1,0:T(8,128)(2,1)} %pad_maximum_fusion.1.refs_1_, bf16[768,1024]{1,0:T(8,128)(2,1)} %copy-done.21, bf16[1024,1536]{1,0:T(8,128)(2,1)} %get-tuple-element.152.refs_3_.refs_0_, ...), custom_call_target="tpu_custom_call" | custom-call | flops 19327352832 | bytes 14680064 | tf_op jit(solution)/shard_map/self_weights/pallas_call | solution.py:463
  843.0 9.6 collective-permute-done.16
  891.8 11.1 %collective-permute-start.28 = (bf16[160,1024]{1,0:T(8,128)(2,1)S(1)}, bf16[160,1024]{1,0:T(8,128)(2,1)S(1)}, u32[]{:S(2)}, u32[]{:S(2)}) collective-permute-start(bf16[160,1024]{1,0:T(8,128)(2,1)S(1)} %dynamic-slice_bitcast_fusion.5), channel_id=1, source_target_pairs={{0,1},{1,2},{2,3},{3,0},{4,5},{5,6},{6,7},{7,4},{8,9},{9,10},{10,1... | collective-permute-start | bytes 983048 | tf_op jit(solution)/shard_map/ppermute | solution.py:1252
  924.6 23.3 %near_rows.1 = bf16[1536,1024]{1,0:T(8,128)(2,1)} custom-call(bf16[1024,1536]{1,0:T(8,128)(2,1)} %get-tuple-element.152.refs_3_.refs_0_, bf16[2,1024,1536]{2,1,0:T(8,128)(2,1)} %get-tuple-element.139.refs_4_.refs_5_.refs_1_.refs_2_, bf16[2,1024,1536]{2,1,0:T(8,128)(2,1)} %get-tuple-element.139.refs_4_.refs_5_.refs_1_.refs_2_, ...), custom_call_target="tpu_custom_call" | custom-call | flops 11274289152 | bytes 27787264 | tf_op jit(solution)/shard_map/near_rows/pallas_call | solution.py:501
  971.8 8.1 collective-permute-done.32
  (334 shorter events, 285.3 us)
Async XLA Ops:
  7.2 192.3 %all-gather.2.cloned.1.call-start = ((), (), s32[]{:S(2)}) async-start(), calls=%async_computation.5 | async-start | bytes 5242880 | tf_op jit(solution)/shard_map/all_gather | solution.py:1165
  9.6 26.4 %collective-permute-start = (bf16[256,1024]{1,0:T(8,128)(2,1)}, bf16[256,1024]{1,0:T(8,128)(2,1)}, u32[]{:S(2)}, u32[]{:S(2)}) collective-permute-start(bf16[256,1024]{1,0:T(8,128)(2,1)} %get-tuple-element.194), channel_id=1, source_target_pairs={{0,1},{1,2},{2,3},{4,5},{5,6},{6,7},{8,9},{9,10},{10,11},{12,13},{... | collective-permute-start | bytes 1572872 | tf_op jit(solution)/shard_map/ppermute | solution.py:1160
  36.0 13.8 %collective-permute-start.1 = (bf16[256,1024]{1,0:T(8,128)(2,1)}, bf16[256,1024]{1,0:T(8,128)(2,1)}, u32[]{:S(2)}, u32[]{:S(2)}) collective-permute-start(bf16[256,1024]{1,0:T(8,128)(2,1)} %collective-permute-done), channel_id=1, source_target_pairs={{0,1},{1,2},{2,3},{4,5},{5,6},{6,7},{8,9},{9,10},{10,11},{12,13},{... | collective-permute-start | bytes 1572872 | tf_op jit(solution)/shard_map/ppermute | solution.py:1160
  49.9 14.7 %collective-permute-start.2 = (bf16[256,1024]{1,0:T(8,128)(2,1)}, bf16[256,1024]{1,0:T(8,128)(2,1)}, u32[]{:S(2)}, u32[]{:S(2)}) collective-permute-start(bf16[256,1024]{1,0:T(8,128)(2,1)} %collective-permute-done.1), channel_id=1, source_target_pairs={{0,1},{1,2},{2,3},{4,5},{5,6},{6,7},{8,9},{9,10},{10,11},{12,13},{... | collective-permute-start | bytes 1572872 | tf_op jit(solution)/shard_map/ppermute | solution.py:1160
  64.6 13.8 %collective-permute-start.3 = (bf16[256,1024]{1,0:T(8,128)(2,1)}, bf16[256,1024]{1,0:T(8,128)(2,1)S(1)}, u32[]{:S(2)}, u32[]{:S(2)}) collective-permute-start(bf16[256,1024]{1,0:T(8,128)(2,1)} %get-tuple-element.94), channel_id=1, source_target_pairs={{0,1},{1,2},{2,3},{4,5},{5,6},{6,7},{8,9},{9,10},{10,11},{12,13},{... | collective-permute-start | bytes 1572872 | tf_op jit(solution)/shard_map/ppermute | solution.py:1160
  72.4 446.0 %reduce-scatter.6.cloned.1.call-start = ((), (), s32[]{:S(2)}) async-start(), calls=%async_computation.6 | async-start | bytes 9437184 | tf_op jit(solution)/shard_map/reduce_scatter | solution.py:1220
  78.3 25.6 %collective-permute-start.4 = (bf16[256,1024]{1,0:T(8,128)(2,1)S(1)}, bf16[256,1024]{1,0:T(8,128)(2,1)S(1)}, u32[]{:S(2)}, u32[]{:S(2)}) collective-permute-start(bf16[256,1024]{1,0:T(8,128)(2,1)S(1)} %collective-permute-done.3), channel_id=1, source_target_pairs={{0,1},{1,2},{2,3},{4,5},{5,6},{6,7},{8,9},{9,10},{10,11},{12,13},{... | collective-permute-start | bytes 1572872 | tf_op jit(solution)/shard_map/ppermute | solution.py:1160
  104.0 41.6 %collective-permute-start.5 = (bf16[256,1024]{1,0:T(8,128)(2,1)S(1)}, bf16[256,1024]{1,0:T(8,128)(2,1)S(1)}, u32[]{:S(2)}, u32[]{:S(2)}) collective-permute-start(bf16[256,1024]{1,0:T(8,128)(2,1)S(1)} %collective-permute-done.4), channel_id=1, source_target_pairs={{0,1},{1,2},{2,3},{4,5},{5,6},{6,7},{8,9},{9,10},{10,11},{12,13},{... | collective-permute-start | bytes 1572872 | tf_op jit(solution)/shard_map/ppermute | solution.py:1160
  363.1 156.7 %reduce-scatter.8.cloned.1.call-start = ((), (), s32[]{:S(2)}) async-start(), calls=%async_computation.7 | async-start | bytes 9437184 | tf_op jit(solution)/shard_map/reduce_scatter | solution.py:1220
  405.9 482.3 %reduce-scatter.10.cloned.1.call-start = ((), (), s32[]{:S(2)}) async-start(), calls=%async_computation.8 | async-start | bytes 2359296 | tf_op jit(solution)/shard_map/reduce_scatter | solution.py:1220
  453.0 435.2 %reduce-scatter.14.cloned.1.call-start = ((), (), s32[]{:S(2)}) async-start(), calls=%async_computation.10 | async-start | bytes 2359296 | tf_op jit(solution)/shard_map/reduce_scatter | solution.py:1220
  583.4 304.8 %reduce-scatter.12.cloned.1.call-start = ((), (), s32[]{:S(2)}) async-start(), calls=%async_computation.9 | async-start | bytes 7077888 | tf_op jit(solution)/shard_map/reduce_scatter | solution.py:1220
  584.6 17.2 %collective-permute-start.6 = (bf16[256,1024]{1,0:T(8,128)(2,1)S(1)}, bf16[256,1024]{1,0:T(8,128)(2,1)S(1)}, u32[]{:S(2)}, u32[]{:S(2)}) collective-permute-start(bf16[256,1024]{1,0:T(8,128)(2,1)S(1)} %fusion.69), channel_id=1, source_target_pairs={{0,1},{1,2},{2,3},{3,0},{4,5},{5,6},{6,7},{7,4},{8,9},{9,10},{10,1... | collective-permute-start | bytes 1572872 | tf_op jit(solution)/shard_map/ppermute | solution.py:1252
  602.8 17.5 %collective-permute-start.7 = (bf16[256,1024]{1,0:T(8,128)(2,1)}, bf16[256,1024]{1,0:T(8,128)(2,1)}, u32[]{:S(2)}, u32[]{:S(2)}) collective-permute-start(bf16[256,1024]{1,0:T(8,128)(2,1)} %fusion.61), channel_id=1, source_target_pairs={{0,1},{1,2},{2,3},{3,0},{4,5},{5,6},{6,7},{7,4},{8,9},{9,10},{10,1... | collective-permute-start | bytes 1572872 | tf_op jit(solution)/shard_map/ppermute | solution.py:1252
  607.4 136.9 %collective-permute-start.11 = (bf16[2,256,1024]{2,1,0:T(8,128)(2,1)}, bf16[2,256,1024]{2,1,0:T(8,128)(2,1)S(1)}, u32[]{:S(2)}, u32[]{:S(2)}) collective-permute-start(bf16[2,256,1024]{2,1,0:T(8,128)(2,1)} %get-tuple-element.188), channel_id=1, source_target_pairs={{0,3},{1,0},{2,1},{3,2},{4,7},{5,4},{6,5},{7,6},{8,11},{9,8},{10,9... | collective-permute-start | bytes 3145736 | tf_op jit(solution)/shard_map/ppermute | solution.py:1317
  611.8 132.6 %collective-permute-start.10 = (bf16[2,256,1024]{2,1,0:T(8,128)(2,1)}, bf16[2,256,1024]{2,1,0:T(8,128)(2,1)}, u32[]{:S(2)}, u32[]{:S(2)}) collective-permute-start(bf16[2,256,1024]{2,1,0:T(8,128)(2,1)} %get-tuple-element.189), channel_id=1, source_target_pairs={{0,2},{1,3},{2,0},{3,1},{4,6},{5,7},{6,4},{7,5},{8,10},{9,11},{10,... | collective-permute-start | bytes 3145736 | tf_op jit(solution)/shard_map/ppermute | solution.py:1317
  612.2 132.1 %collective-permute-start.9 = (bf16[2,256,1024]{2,1,0:T(8,128)(2,1)}, bf16[2,256,1024]{2,1,0:T(8,128)(2,1)}, u32[]{:S(2)}, u32[]{:S(2)}) collective-permute-start(bf16[2,256,1024]{2,1,0:T(8,128)(2,1)} %get-tuple-element.190), channel_id=1, source_target_pairs={{0,1},{1,2},{2,3},{3,0},{4,5},{5,6},{6,7},{7,4},{8,9},{9,10},{10,1... | collective-permute-start | bytes 3145736 | tf_op jit(solution)/shard_map/ppermute | solution.py:1317
  621.5 69.4 %collective-permute-start.8 = (bf16[256,1024]{1,0:T(8,128)(2,1)S(1)}, bf16[256,1024]{1,0:T(8,128)(2,1)S(1)}, u32[]{:S(2)}, u32[]{:S(2)}) collective-permute-start(bf16[256,1024]{1,0:T(8,128)(2,1)S(1)} %fusion.60), channel_id=1, source_target_pairs={{0,1},{1,2},{2,3},{3,0},{4,5},{5,6},{6,7},{7,4},{8,9},{9,10},{10,1... | collective-permute-start | bytes 1572872 | tf_op jit(solution)/shard_map/ppermute | solution.py:1252
  744.3 45.6 %collective-permute-start.14 = (bf16[256,1024]{1,0:T(8,128)(2,1)S(1)}, bf16[256,1024]{1,0:T(8,128)(2,1)S(1)}, u32[]{:S(2)}, u32[]{:S(2)}) collective-permute-start(bf16[256,1024]{1,0:T(8,128)(2,1)S(1)} %get-tuple-element.199), channel_id=1, source_target_pairs={{3,0},{7,4},{11,8},{15,12},{19,16},{23,20},{27,24},{31,28}} | collective-permute-start | bytes 1572872 | tf_op jit(solution)/shard_map/ppermute | solution.py:1343
  745.6 44.3 %collective-permute-start.13 = (bf16[256,1024]{1,0:T(8,128)(2,1)S(1)}, bf16[256,1024]{1,0:T(8,128)(2,1)S(1)}, u32[]{:S(2)}, u32[]{:S(2)}) collective-permute-start(bf16[256,1024]{1,0:T(8,128)(2,1)S(1)} %get-tuple-element.200), channel_id=1, source_target_pairs={{2,0},{3,1},{6,4},{7,5},{10,8},{11,9},{14,12},{15,13},{18,16},{19,... | collective-permute-start | bytes 1572872 | tf_op jit(solution)/shard_map/ppermute | solution.py:1343
  746.9 43.0 %collective-permute-start.12 = (bf16[256,1024]{1,0:T(8,128)(2,1)S(1)}, bf16[256,1024]{1,0:T(8,128)(2,1)S(1)}, u32[]{:S(2)}, u32[]{:S(2)}) collective-permute-start(bf16[256,1024]{1,0:T(8,128)(2,1)S(1)} %get-tuple-element.201), channel_id=1, source_target_pairs={{1,0},{2,1},{3,2},{5,4},{6,5},{7,6},{9,8},{10,9},{11,10},{13,12},{... | collective-permute-start | bytes 1572872 | tf_op jit(solution)/shard_map/ppermute | solution.py:1343
  800.0 42.9 %collective-permute-start.17 = (bf16[256,1024]{1,0:T(8,128)(2,1)S(1)}, bf16[256,1024]{1,0:T(8,128)(2,1)S(1)}, u32[]{:S(2)}, u32[]{:S(2)}) collective-permute-start(bf16[256,1024]{1,0:T(8,128)(2,1)S(1)} %get-tuple-element.196), channel_id=1, source_target_pairs={{3,0},{7,4},{11,8},{15,12},{19,16},{23,20},{27,24},{31,28}} | collective-permute-start | bytes 1572872 | tf_op jit(solution)/shard_map/ppermute | solution.py:1343
  801.3 51.2 %collective-permute-start.16 = (bf16[256,1024]{1,0:T(8,128)(2,1)S(1)}, bf16[256,1024]{1,0:T(8,128)(2,1)S(1)}, u32[]{:S(2)}, u32[]{:S(2)}) collective-permute-start(bf16[256,1024]{1,0:T(8,128)(2,1)S(1)} %get-tuple-element.197), channel_id=1, source_target_pairs={{2,0},{3,1},{6,4},{7,5},{10,8},{11,9},{14,12},{15,13},{18,16},{19,... | collective-permute-start | bytes 1572872 | tf_op jit(solution)/shard_map/ppermute | solution.py:1343
  802.6 49.9 %collective-permute-start.15 = (bf16[256,1024]{1,0:T(8,128)(2,1)S(1)}, bf16[256,1024]{1,0:T(8,128)(2,1)}, u32[]{:S(2)}, u32[]{:S(2)}) collective-permute-start(bf16[256,1024]{1,0:T(8,128)(2,1)S(1)} %get-tuple-element.198), channel_id=1, source_target_pairs={{1,0},{2,1},{3,2},{5,4},{6,5},{7,6},{9,8},{10,9},{11,10},{13,12},{... | collective-permute-start | bytes 1572872 | tf_op jit(solution)/shard_map/ppermute | solution.py:1343
  857.0 24.3 %collective-permute-start.18 = (bf16[4,448,1024]{2,1,0:T(8,128)(2,1)}, bf16[4,448,1024]{2,1,0:T(8,128)(2,1)}, u32[]{:S(2)}, u32[]{:S(2)}) collective-permute-start(bf16[4,448,1024]{2,1,0:T(8,128)(2,1)} %dynamic-slice_bitcast_fusion), channel_id=1, source_target_pairs={{0,4},{4,0},{8,12},{12,8},{16,20},{20,16},{24,28},{28,24},{1,5},{5... | collective-permute-start | bytes 11010056 | tf_op jit(solution)/shard_map/ppermute | solution.py:1229
  889.8 13.1 %collective-permute-start.23 = (f32[4,4480]{1,0:T(4,128)S(1)}, f32[4,4480]{1,0:T(4,128)S(1)}, u32[]{:S(2)}, u32[]{:S(2)}) collective-permute-start(f32[4,4480]{1,0:T(4,128)S(1)} %constant_dynamic-update-slice_fusion.3), channel_id=1, source_target_pairs={{0,4},{4,0},{8,12},{12,8},{16,20},{20,16},{24,28},{28,24},{1,5},{5... | collective-permute-start | bytes 215048 | tf_op jit(solution)/shard_map/ppermute | solution.py:1416
  891.8 32.6 %collective-permute-start.28 = (bf16[160,1024]{1,0:T(8,128)(2,1)S(1)}, bf16[160,1024]{1,0:T(8,128)(2,1)S(1)}, u32[]{:S(2)}, u32[]{:S(2)}) collective-permute-start(bf16[160,1024]{1,0:T(8,128)(2,1)S(1)} %dynamic-slice_bitcast_fusion.5), channel_id=1, source_target_pairs={{0,1},{1,2},{2,3},{3,0},{4,5},{5,6},{6,7},{7,4},{8,9},{9,10},{10,1... | collective-permute-start | bytes 983048 | tf_op jit(solution)/shard_map/ppermute | solution.py:1252
  911.4 37.3 %collective-permute-start.19 = (bf16[2,224,1024]{2,1,0:T(8,128)(2,1)}, bf16[2,224,1024]{2,1,0:T(8,128)(2,1)S(1)}, u32[]{:S(2)}, u32[]{:S(2)}) collective-permute-start(bf16[2,224,1024]{2,1,0:T(8,128)(2,1)} %dynamic-slice_bitcast_fusion.2), channel_id=1, source_target_pairs={{0,8},{4,12},{8,0},{12,4},{16,24},{20,28},{24,16},{28,20},{1,9},{5... | collective-permute-start | bytes 2752520 | tf_op jit(solution)/shard_map/ppermute | solution.py:1229
  918.4 31.4 %collective-permute-start.21 = (bf16[2,224,1024]{2,1,0:T(8,128)(2,1)}, bf16[2,224,1024]{2,1,0:T(8,128)(2,1)}, u32[]{:S(2)}, u32[]{:S(2)}) collective-permute-start(bf16[2,224,1024]{2,1,0:T(8,128)(2,1)} %dynamic-slice_bitcast_fusion.1), channel_id=1, source_target_pairs={{0,16},{4,20},{8,24},{12,28},{16,0},{20,4},{24,8},{28,12},{1,17},{... | collective-permute-start | bytes 2752520 | tf_op jit(solution)/shard_map/ppermute | solution.py:1229
  919.8 28.1 %collective-permute-start.27 = (f32[4,4480]{1,0:T(4,128)S(1)}, f32[4,4480]{1,0:T(4,128)S(1)}, u32[]{:S(2)}, u32[]{:S(2)}) collective-permute-start(f32[4,4480]{1,0:T(4,128)S(1)} %add.455), channel_id=1, source_target_pairs={{0,2},{1,3},{2,0},{3,1},{4,6},{5,7},{6,4},{7,5},{8,10},{9,11},{10,... | collective-permute-start | bytes 215048 | tf_op jit(solution)/shard_map/ppermute | solution.py:1416
  924.5 23.5 %collective-permute-start.29 = (bf16[160,1024]{1,0:T(8,128)(2,1)S(1)}, bf16[160,1024]{1,0:T(8,128)(2,1)S(1)}, u32[]{:S(2)}, u32[]{:S(2)}) collective-permute-start(bf16[160,1024]{1,0:T(8,128)(2,1)S(1)} %fusion.65), channel_id=1, source_target_pairs={{0,1},{1,2},{2,3},{3,0},{4,5},{5,6},{6,7},{7,4},{8,9},{9,10},{10,1... | collective-permute-start | bytes 983048 | tf_op jit(solution)/shard_map/ppermute | solution.py:1252
  969.6 10.3 %collective-permute-start.32 = (bf16[112,1024]{1,0:T(8,128)(2,1)S(1)}, bf16[112,1024]{1,0:T(8,128)(2,1)S(1)}, u32[]{:S(2)}, u32[]{:S(2)}) collective-permute-start(bf16[112,1024]{1,0:T(8,128)(2,1)S(1)} %fusion.75), channel_id=1, source_target_pairs={{0,1},{1,2},{2,3},{3,0},{4,5},{5,6},{6,7},{7,4},{8,9},{9,10},{10,1... | collective-permute-start | bytes 688136 | tf_op jit(solution)/shard_map/ppermute | solution.py:1252
  (64 other events, 1318.1 us)
Sparse Core Ops, SparseCore 0:
  72.5 97.1 all-gather.1
  363.2 81.3 reduce-scatter.5
  448.5 71.2 reduce-scatter.7
  522.9 41.2 reduce-scatter.9
  583.5 49.2 reduce-scatter.13
  636.0 67.1 reduce-scatter.11

commit v3 on v2

--- a/solution.py
+++ b/solution.py
@@ -17,7 +17,12 @@
 TILE = 128
 NEGATIVE = -1e30
 EPSILON = 1e-05
-VMEM_LIMIT = 56 * 2**20
+VMEM_LIMIT = 60 * 2**20
+SPLIT = 2
+FFN_COLS = 1024
+FFN_ROWS = 768
+FFN_STEP = 512
+BACK_COLUMNS = 512
 
 low_type = jnp.bfloat16
 high_type = jnp.float32
@@ -265,34 +270,22 @@
     drel_ref[...] = (drel + jnp.where(bucket == 0, own_all, 0.0)).astype(low_type)
 
 
-def weight_grads_kernel(*refs, sources, terms, parts, sums):
-    xs, rest = refs[: len(sources)], refs[len(sources) :]
-    turned = rest[-1]
-    count = max(place for step in terms for place, _ in step) + 1
-    gs, out_ref = rest[:count], rest[count]
+def weight_grads_kernel(*refs, xs, terms, parts, sums):
+    x_refs, rest = refs[:xs], refs[xs:]
+    count = max(place for step in terms for _, place in step) + 1
+    g_refs, out_ref = rest[:count], rest[count]
     e, c = pl.program_id(0), pl.program_id(1)
-
-    @pl.when((e == 0) & (c == 0))
-    def _():
-        start = 0
-        for x_ref, rows in zip(xs, sources, strict=True):
-            turned[:, start : start + rows] = x_ref[...].T
-            start += rows
 
     for step, term in enumerate(terms):
 
         @pl.when(c == step)
         def _():
-            total = None
-            for place, (low_at, high_at) in term:
-                g = gs[place][...]
-                piece = contract(turned[:, low_at:high_at], g, 1, 1)
-                total = piece if total is None else total + piece
-                if sums[step]:
-                    line = contract(jnp.ones((8, high_at - low_at), low_type), g, 1, 1)
-                    held = line if place == term[0][0] else held + line
+            x = jnp.concatenate([x_refs[x_at][...] for x_at, _ in term], 0)
+            g = jnp.concatenate([g_refs[g_at][...] for _, g_at in term], 1)
+            total = contract(x, g, 0, 1)
             if sums[step]:
-                rest[count + 1][step] = held
+                line = jnp.sum(g.astype(high_type), 1, keepdims=True)
+                rest[count + 1][step] = jnp.broadcast_to(line, (line.shape[0], TILE))
             total = total.astype(low_type)
             for at, row, rows, halves in parts[step]:
                 if halves:
@@ -303,18 +296,10 @@
 
 
 def back_rows_kernel(*refs, pairs, base, joined):
-    gs, ws, rest = refs[:pairs], refs[pairs : 2 * pairs], refs[2 * pairs :]
-    turned = rest[-pairs:]
-    out_ref = rest[-pairs - 1]
-
-    @pl.when(pl.program_id(1) == 0)
-    def _():
-        for g_ref, t_ref in zip(gs, turned, strict=True):
-            t_ref[...] = g_ref[...].T
-
+    gs, ws, rest, out_ref = refs[:pairs], refs[pairs : 2 * pairs], refs[2 * pairs : -1], refs[-1]
     total = rest[0][...] if base else None
-    for t_ref, w_ref in zip(turned, ws, strict=True):
-        piece = contract(t_ref[...], w_ref[...], 1, 1)
+    for g_ref, w_ref in zip(gs, ws, strict=True):
+        piece = contract(g_ref[...], w_ref[...], 0, 1)
         total = piece if total is None else total + piece
     if joined:
         add = rest[1][...]
@@ -452,25 +437,22 @@
 
 def weight_grads(xs, gs, specs, terms, parts, sums, out, name):
     width = xs[0].shape[1]
-    columns = out[2] // 4
-    sources = [x.shape[0] for x in xs]
-    outs = [jax.ShapeDtypeStruct(out, low_type)]
-    out_specs = [pl.BlockSpec((out[0], out[1], columns), lambda e, c: (0, 0, e))]
-    if any(sums):
-        outs.append(jax.ShapeDtypeStruct((len(terms), 8, out[2]), high_type))
-        out_specs.append(pl.BlockSpec((len(terms), 8, columns), lambda e, c: (0, 0, e)))
-    flops = sum(2 * width * out[2] * (b - a) for term in terms for _, (a, b) in term)
+    columns = out[2] // SPLIT
+    flops = sum(2 * width * out[2] * xs[x_at].shape[0] for term in terms for x_at, _ in term)
     return pl.pallas_call(
-        functools.partial(
-            weight_grads_kernel, sources=sources, terms=terms, parts=parts, sums=sums
-        ),
-        grid=(4, len(terms)),
+        functools.partial(weight_grads_kernel, xs=len(xs), terms=terms, parts=parts, sums=sums),
+        grid=(SPLIT, len(terms)),
         in_specs=[pl.BlockSpec(x.shape, lambda e, c: (0, 0)) for x in xs] + specs,
-        out_specs=out_specs,
-        out_shape=outs,
-        scratch_shapes=[pltpu.VMEM((width, sum(sources)), low_type)],
+        out_specs=[
+            pl.BlockSpec((out[0], out[1], columns), lambda e, c: (0, 0, e)),
+            pl.BlockSpec((len(terms), columns, TILE), lambda e, c: (0, e, 0)),
+        ],
+        out_shape=[
+            jax.ShapeDtypeStruct(out, low_type),
+            jax.ShapeDtypeStruct((len(terms), out[2], TILE), high_type),
+        ],
         cost_estimate=pl.CostEstimate(
-            flops=flops, bytes_accessed=2 * width * (sum(sources) * 2 + out[2]), transcendentals=0
+            flops=flops, bytes_accessed=flops // 256, transcendentals=0
         ),
         compiler_params=pltpu.CompilerParams(vmem_limit_bytes=VMEM_LIMIT),
         name=name,
@@ -478,7 +460,7 @@
 
 
 def back_rows(gs, ws, base, joined, tile, name):
-    width, columns = 1024, 256
+    width, columns = 1024, BACK_COLUMNS
 
     def spec(entry, shape, index):
         if isinstance(entry, tuple):
@@ -506,7 +488,6 @@
         in_specs=specs,
         out_specs=pl.BlockSpec((tile, columns), lambda r, d: (r, d)),
         out_shape=jax.ShapeDtypeStruct((rows, width), low_type),
-        scratch_shapes=[pltpu.VMEM((tile, f), low_type) for f in sizes],
         cost_estimate=pl.CostEstimate(
             flops=2 * rows * width * sum(sizes),
             bytes_accessed=2 * (rows + width) * sum(sizes) + 6 * rows * width,
@@ -517,29 +498,27 @@
     )(*arrays, *weights, *extra)
 
 
-def ffn_kernel(x_ref, w_ref, b_ref, g_ref, slope_ref):
-    u = contract(x_ref[...], w_ref[...], 1, 0) + b_ref[...]
-    z = jnp.abs(u) * (0.5**0.5)
-    t = 1.0 / (1.0 + 0.3275911 * z)
-    bell = jnp.exp(-z * z)
-    poly = t * (
-        0.254829592
-        + t * (-0.284496736 + t * (1.421413741 + t * (-1.453152027 + t * 1.061405429)))
-    )
-    tail = 0.5 * poly * bell
-    phi = jnp.where(u < 0.0, tail, 1.0 - tail)
-    g_ref[...] = (u * phi).astype(low_type)
-    slope_ref[...] = (phi + u * (bell * (2.0 * math.pi) ** -0.5)).astype(low_type)
+def ffn_kernel(x_ref, w_ref, b_ref, g_ref, slope_ref, *, step):
+    x = x_ref[...]
+    for at in range(0, w_ref.shape[1], step):
+        u = contract(x, w_ref[:, at : at + step], 1, 0) + b_ref[:, at : at + step]
+        t = 1.0 / (1.0 + (0.3275911 * 0.5**0.5) * jnp.abs(u))
+        bell = jnp.exp2(u * u * (-0.5 / math.log(2.0)))
+        poly = 0.7107068705 + t * (-0.7265760135 + t * 0.5307027145)
+        tail = bell * (t * (0.127414796 + t * (-0.142248368 + t * poly)))
+        phi = jnp.where(u < 0.0, tail, 1.0 - tail)
+        g_ref[:, at : at + step] = (u * phi).astype(low_type)
+        slope_ref[:, at : at + step] = (phi + u * (bell * (2.0 * math.pi) ** -0.5)).astype(low_type)
 
 
 def ffn_first(x, w, b):
     rows, width = x.shape
     hidden = w.shape[1]
-    tm, tn = math.gcd(rows, 512), math.gcd(hidden, 1024)
+    tm, tn = math.gcd(rows, FFN_ROWS), math.gcd(hidden, FFN_COLS)
     block = pl.BlockSpec((tm, tn), lambda j, i: (i, j))
     out = jax.ShapeDtypeStruct((rows, hidden), low_type)
     return pl.pallas_call(
-        ffn_kernel,
+        functools.partial(ffn_kernel, step=FFN_STEP),
         grid=(hidden // tn, rows // tm),
         in_specs=[
             pl.BlockSpec((tm, width), lambda j, i: (i, 0)),
@@ -1142,8 +1121,6 @@
     keys = T * seq_parts
     far = keys - T
     place = lax.axis_index("seq")
-    up = [(i, i + 1) for i in range(seq_parts - 1)]
-    down = [(i + 1, i) for i in range(seq_parts - 1)]
     gains, shifts = norm_gain.astype(high_type), norm_bias.astype(high_type)
     self_bias, cross_bias = self_qv_bias.astype(high_type), cross_qv_bias.astype(high_type)
     table = jnp.asarray(bucket_table(), low_type)
@@ -1151,17 +1128,18 @@
     after = lax.optimization_barrier
     x = hidden.reshape(B * S * T, width)
     rows = B * S * T
-    far_rows, held = [], None
+    far_rows = []
     for b in range(B):
-        moving, pieces = hidden[b, 0], []
-        if held is not None:
-            moving, held = after((moving, held))
-        for _ in range(seq_parts - 1):
-            moving = lax.ppermute(moving, "seq", up)
-            pieces.append(moving)
-        held = moving
-        far_rows.append(jnp.concatenate(pieces[::-1], 0))
-    e_own, far_rows[0] = after((encoder_out, far_rows[0]))
+        sent = hidden[b, 0]
+        if b:
+            sent, far_rows[b - 1] = after((sent, far_rows[b - 1]))
+        pieces = [
+            lax.ppermute(sent, "seq", [(i, i + hop) for i in range(seq_parts - hop)])
+            for hop in range(seq_parts - 1, 0, -1)
+        ]
+        far_rows.append(jnp.concatenate(pieces, 0))
+        if b == 0:
+            e_own, far_rows[0] = after((encoder_out, far_rows[0]))
     e_all = lax.all_gather(e_own, "seq", axis=1, tiled=True).reshape(-1, width)
     key_at = place * T - far + jnp.arange(keys, dtype=jnp.int32)
     self_mark = key_features((key_at >= 0) & (key_at < dec_lengths[:, None]))
@@ -1179,6 +1157,8 @@
         )
         self_inputs.append((q, k, v, k_far, v_far, rel, self_mark, table))
         results = self_forward(b, self_inputs[b], results, T, S)
+        if b + 1 < B:
+            far_rows[b + 1], results = after((far_rows[b + 1], results))
     attended, self_total = results
     first_sum = (
         x.astype(high_type)
@@ -1219,7 +1199,7 @@
     def over_dp(piece):
         return lax.psum_scatter(piece, "dp", scatter_dimension=0, tiled=True)
 
-    def over_dp_by_steps(piece, meanwhile):
+    def over_dp_by_steps(piece, meanwhile, beside, later):
         me = lax.axis_index("dp")
 
         def swap(pair, bit):
@@ -1235,7 +1215,8 @@
         first, second = chip[:, : count // 2], chip[:, count // 2 :]
         first = swap(jnp.swapaxes(first.reshape(2, 2, count // 2, width), 0, 1), 1)
         second = swap(second.reshape(2, 2, count // 2, width), 2)
-        return jnp.concatenate([swap(first, 2), swap(second, 1)], 0), meanwhile
+        first, second, done, later = after((first, second, beside(meanwhile), later))
+        return jnp.concatenate([swap(first, 2), swap(second, 1)], 0), done, later
 
     def over_seq(*pieces):
         cut = [piece.reshape(seq_parts, -1, width) for piece in pieces]
@@ -1249,12 +1230,18 @@
         ring = [(i, (i + 1) % seq_parts) for i in range(seq_parts)]
         held = block(1)
         for hop in range(2, seq_parts + 1):
-            held = lax.ppermute(held.astype(low_type), "seq", ring).astype(high_type) + block(hop)
+            came = yield lax.ppermute(held.astype(low_type), "seq", ring)
+            held = came.astype(high_type) + block(hop)
         ends = np.cumsum([piece.shape[1] for piece in cut])
-        return [
+        yield [
             held[end - piece.shape[1] : end].reshape(-1)
             for piece, end in zip(cut, ends, strict=True)
         ]
+
+    def finish(steps, item):
+        for _ in range(seq_parts - 2):
+            item = steps.send(item)
+        return steps.send(item)
 
     def low(value):
         return value.astype(low_type)
@@ -1270,16 +1257,19 @@
     )
     grad_cross = grad_second_sum.astype(low_type)
     part_cross_out, grad_cross = after((low(dot("er,rd->ed", cross_mixed, grad_cross)), grad_cross))
-    mat_cross_out = over_dp(part_cross_out)
     grad_cross_mixed = dot("ed,rd->er", cross_out, grad_cross).astype(low_type)
     dqc, dkc, dvc = cross_backward(
         qc, kc, vc, cross_mark, cross_mixed, cross_total, grad_cross_mixed
     )
     dqc, dkc, dvc, mat_ffn_out, mat_ffn_in = after((dqc, dkc, dvc, mat_ffn_out, mat_ffn_in))
-    done_ffn_in, done_ffn_out = over_seq(mat_ffn_in, mat_ffn_out)
+    ffn_steps = over_seq(mat_ffn_in, mat_ffn_out)
+    ffn_item = next(ffn_steps)
     part_encoder = back_rows(
         (dkc, dvc), ((cross_qkv, 1), (cross_qkv, 2)), None, None, keys, "encoder_rows"
     ).reshape(B, keys, width)
+    grad_encoder = lax.psum_scatter(part_encoder, "seq", scatter_dimension=1, tiled=True)
+    e_all, part_encoder, part_cross_out = after((e_all, part_encoder, part_cross_out))
+    mat_cross_out = over_dp(part_cross_out)
     third = 3 * width // 8
 
     def cut(step, size, blocks):
@@ -1290,118 +1280,122 @@
                 found.append(((block, low_at - size * block), low_at - width * step, high_at - low_at, 0))
         return found
 
-    quarter = width // 4
-    (part_cross_qkv,) = weight_grads(
+    columns = width // SPLIT
+    part_cross_qkv, cross_sums = weight_grads(
         (first_low, e_all),
         (dqc, dkc, dvc),
         [
-            pl.BlockSpec((quarter, rows), lambda e, c: (e, 0)),
-            pl.BlockSpec((quarter, B * keys), lambda e, c: (e, 0)),
-            pl.BlockSpec((quarter, B * keys), lambda e, c: (e, 0)),
+            pl.BlockSpec((columns, rows), lambda e, c: (e, 0)),
+            pl.BlockSpec((columns, B * keys), lambda e, c: (e, 0)),
+            pl.BlockSpec((columns, B * keys), lambda e, c: (e, 0)),
         ],
-        [[(0, (0, rows))], [(1, (rows, rows + B * keys))], [(2, (rows, rows + B * keys))]],
+        [[(0, 0)], [(1, 1)], [(1, 2)]],
         [cut(step, third, 8) for step in range(3)],
-        [False] * 3,
+        [True, False, True],
         (8, third, width),
         "cross_weights",
     )
     part_cross_qkv = part_cross_qkv.reshape(3 * width, width)
-    part_encoder, part_cross_qkv, dqc = after((part_encoder, part_cross_qkv, dqc))
+    part_encoder, part_cross_qkv, dqc, ffn_item = after(
+        (part_encoder, part_cross_qkv, dqc, ffn_item)
+    )
+    ffn_item = ffn_steps.send(ffn_item)
     mat_cross_qkv = over_dp(part_cross_qkv)
 
-    def positions(hop):
-        at = (place + hop) % seq_parts
-        return lax.dynamic_slice_in_dim(part_encoder, at * T, T, 1)
-
-    encoder_parts = [positions(0)] + [
-        lax.ppermute(positions(hop), "seq", [(i, (i + hop) % seq_parts) for i in range(seq_parts)])
-        for hop in range(1, seq_parts)
-    ]
     grad_first = grad_second_sum + dot("er,de->rd", dqc, cross_qkv[0])
     grad_first_sum, grad_gain_self, grad_shift_self = norm_back(first_sum, grad_first, gains[0])
     grad_self = grad_first_sum.astype(low_type)
     part_self_out, grad_self = after((low(dot("er,rd->ed", attended, grad_self)), grad_self))
     mat_self_out = over_dp(part_self_out)
     grad_attended = dot("ed,rd->er", self_out, grad_self).astype(low_type)
-    grad_attended, done_ffn_in, done_ffn_out = after((grad_attended, done_ffn_in, done_ffn_out))
-    results, came = (), []
+    def give_back(far_grads):
+        away = back_rows(
+            ((far_grads, 0), (far_grads, 1)), ((self_qkv, 1), (self_qkv, 2)), None, None, far, "far_rows"
+        )
+        return away, [
+            lax.ppermute(
+                away[(seq_parts - 1 - hop) * T : (seq_parts - hop) * T],
+                "seq",
+                [(i + hop, i) for i in range(seq_parts - hop)],
+            )
+            for hop in range(1, seq_parts)
+        ]
+
+    results, came, far_columns = (), [], []
     for b in range(B):
         *results, far_grads = self_backward(
             b, self_inputs[b], (attended, self_total, grad_attended), tuple(results), T, S
         )
         if b:
-            far_grads, came[b - 1] = after((far_grads, came[b - 1]))
-        away = back_rows(
-            ((far_grads, 0), (far_grads, 1)), ((self_qkv, 1), (self_qkv, 2)), None, None, far, "far_rows"
-        )
-        if b == 0:
-            far_columns = [far_grads]
-        else:
-            far_columns.append(far_grads)
-        came.append(
-            [
-                lax.ppermute(
-                    away[(seq_parts - 1 - hop) * T : (seq_parts - hop) * T],
-                    "seq",
-                    [(i + hop, i) for i in range(seq_parts - hop)],
-                )
-                for hop in range(1, seq_parts)
-            ]
-        )
+            far_grads, came[b - 1], grad_encoder, ffn_item = after(
+                (far_grads, came[b - 1], grad_encoder, ffn_item)
+            )
+        far_columns.append(far_grads)
+        away, pieces = give_back(far_grads)
+        came.append(pieces)
         if b + 1 < B:
-            results[0], self_inputs[b + 1], away, encoder_parts = after(
-                (results[0], self_inputs[b + 1], away, encoder_parts)
+            results[0], self_inputs[b + 1], away, ffn_item = after(
+                (results[0], self_inputs[b + 1], away, ffn_item)
             )
-            grad_encoder = functools.reduce(
-                jnp.add, [piece.astype(high_type) for piece in encoder_parts]
-            ).astype(low_type)
+            for _ in range(seq_parts - 3):
+                ffn_item = ffn_steps.send(ffn_item)
     results[0], away = after((results[0], away))
+    done_ffn_in, done_ffn_out = ffn_steps.send(ffn_item)
     dq, dkv, drel = results
     blocks, size, rel_size = 8 * seq_parts, 3 * width // (8 * seq_parts), width // (16 * seq_parts)
-    near_at, far_at = (0, rows), [(rows + b * far, rows + (b + 1) * far) for b in range(B)]
     part_self, part_sums = weight_grads(
         (x, *far_rows),
         (dq, dkv, dkv, drel) + tuple(far_columns) * 2,
         [
-            pl.BlockSpec((quarter, rows), lambda e, c: (e, 0)),
-            pl.BlockSpec((None, quarter, rows), lambda e, c: (0, e, 0)),
-            pl.BlockSpec((None, quarter, rows), lambda e, c: (1, e, 0)),
-            pl.BlockSpec((quarter, rows), lambda e, c: (e % 2, 0)),
+            pl.BlockSpec((columns, rows), lambda e, c: (e, 0)),
+            pl.BlockSpec((None, columns, rows), lambda e, c: (0, e, 0)),
+            pl.BlockSpec((None, columns, rows), lambda e, c: (1, e, 0)),
+            pl.BlockSpec((width // 2, rows), lambda e, c: (0, 0)),
         ]
-        + [pl.BlockSpec((None, quarter, far), lambda e, c: (0, e, 0))] * B
-        + [pl.BlockSpec((None, quarter, far), lambda e, c: (1, e, 0))] * B,
+        + [pl.BlockSpec((None, columns, far), lambda e, c: (0, e, 0))] * B
+        + [pl.BlockSpec((None, columns, far), lambda e, c: (1, e, 0))] * B,
         [
-            [(0, near_at)],
-            [(1, near_at)] + [(4 + b, far_at[b]) for b in range(B)],
-            [(2, near_at)] + [(4 + B + b, far_at[b]) for b in range(B)],
-            [(3, near_at)],
+            [(0, 0)],
+            [(0, 1)] + [(1 + b, 4 + b) for b in range(B)],
+            [(0, 2)] + [(1 + b, 4 + B + b) for b in range(B)],
+            [(0, 3)],
         ],
         [cut(step, size, blocks) for step in range(3)]
-        + [[((block, size), 2 * rel_size * block, rel_size, 2) for block in range(blocks)]],
+        + [[((block, size), 2 * rel_size * block, rel_size, 1) for block in range(blocks)]],
         [True, False, True, True],
         (blocks, size + rel_size, width),
         "self_weights",
     )
     part_self, came[-1] = after((part_self, came[-1]))
-    mat_self, (dq, mat_cross_out, mat_cross_qkv, mat_self_out, part_sums) = over_dp_by_steps(
-        part_self.reshape(-1, width), (dq, mat_cross_out, mat_cross_qkv, mat_self_out, part_sums)
-    )
-    moved = jnp.concatenate(
-        [functools.reduce(jnp.add, [piece.astype(high_type) for piece in came[b]]) for b in range(B)], 0
-    )
-    grad_hidden = back_rows(
-        (dq, (dkv, 0), (dkv, 1), drel),
-        ((self_qkv, 0), (self_qkv, 1), (self_qkv, 2), rel_weight),
-        grad_first_sum,
-        moved,
-        S * T,
-        "near_rows",
-    ).reshape(hidden.shape)
+    summands = (grad_self, grad_cross, grad_pre, grad_ffn, part_sums, cross_sums)
+
+    def near_rows(arrays):
+        dq, came = arrays
+        moved = jnp.concatenate(
+            [functools.reduce(jnp.add, [piece.astype(high_type) for piece in came[b]]) for b in range(B)], 0
+        )
+        return back_rows(
+            (dq, (dkv, 0), (dkv, 1), drel),
+            ((self_qkv, 0), (self_qkv, 1), (self_qkv, 2), rel_weight),
+            grad_first_sum,
+            moved,
+            S * T,
+            "near_rows",
+        )
+
+    mat_self, grad_hidden, (mat_cross_out, mat_cross_qkv, mat_self_out, summands) = over_dp_by_steps(
+        part_self.reshape(-1, width),
+        (dq, came),
+        near_rows,
+        (mat_cross_out, mat_cross_qkv, mat_self_out, summands),
+    )
+    grad_hidden = grad_hidden.reshape(hidden.shape)
+    grad_self, grad_cross, grad_pre, grad_ffn, part_sums, cross_sums = summands
     vectors = [
-        jnp.stack([part_sums[0, 0], part_sums[2, 0]]),
+        jnp.stack([part_sums[0, :, 0], part_sums[2, :, 0]]),
         column_sum(grad_self),
-        part_sums[3, 0, : width // 2],
-        jnp.stack([row_sum(dqc), row_sum(dvc)]),
+        part_sums[3, : width // 2, 0],
+        jnp.stack([cross_sums[0, :, 0], cross_sums[2, :, 0]]),
         column_sum(grad_cross),
         column_sum(grad_pre),
         column_sum(grad_ffn),
@@ -1415,11 +1409,10 @@
         for bit in range(size_of.bit_length() - 1):
             summed = summed + lax.ppermute(summed, axis, [(i, i ^ (1 << bit)) for i in range(size_of)])
     mine = lax.dynamic_index_in_dim(summed, place, 0, keepdims=False)
-    done_cross_out, done_cross_qkv, done_self_out = over_seq(
-        mat_cross_out, mat_cross_qkv, mat_self_out
-    )
-    mat_self, mine, done_cross_out, grad_hidden = after((mat_self, mine, done_cross_out, grad_hidden))
-    (done_self,) = over_seq(mat_self)
+    cross_steps = over_seq(mat_cross_out, mat_cross_qkv, mat_self_out)
+    done_cross_out, done_cross_qkv, done_self_out = finish(cross_steps, next(cross_steps))
+    self_steps = over_seq(mat_self)
+    (done_self,) = finish(self_steps, next(self_steps))
     done_self = done_self.reshape(size + rel_size, width)
     done_self_qkv = done_self[:size].reshape(-1)
     half = width // 2

time: 1010 us -> 886 us (0.88)
  starting transfers between devices: 130 us -> 68.5 us
  waiting for transfers between devices: 102 us -> 75.1 us
  Pallas kernels: 409 us -> 385 us
    ppermute x24 -> x21, waiting for transfers between devices: 96 us -> 21.2 us  [the longest x9 21.1 us: over_seq(): came = (yield lax.ppermute(held.astype(low_type), 'seq', ring))]
    ppermute x24 -> x21, starting transfers between devices: 112 us -> 52.1 us  [the longest x6 27 us: on_device(): lax.ppermute(sent, 'seq', [(i, i + hop) for i in range(seq_parts - hop)])]
    reduce_scatter x5, waiting for transfers between devices: 1.35 us -> 25.7 us  [over_dp(): return lax.psum_scatter(piece, 'dp', scatter_dimension=0, tiled=True)]
    ppermute x5, waiting for transfers between devices: 2.11 us -> 15.7 us  [on_device(): lax.ppermute(summed, axis, [(i, i ^ 1 << bit) for i in range(size_of)])]
    pallas_call x3, Pallas kernels: 102 us -> 88.9 us  [the longest x2 52.8 us: weight_grads(): pl.pallas_call(functools.partial(weight_grads_kernel, xs=len(xs), terms=t...]
    pallas_call x4, Pallas kernels: 58.4 us -> 48.3 us  [back_rows(): pl.pallas_call(functools.partial(back_rows_kernel, pairs=len(gs), base=ba...]
  transfers between devices with their start and end apart: 40 -> 38, of which waited for: 17 -> 12; matrix products, arithmetic and copies ran while one was open for 25% -> 26% of each run, Pallas kernels for 32% -> 33%
where the time goes in v3:
time: 886 us; the launch traced here: 878 us
  Pallas kernels  385 us (43%)
  matrix products  223 us (25%)
  waiting for transfers between devices  75.1 us (8%)
  other arithmetic  70.9 us (8%)
  starting transfers between devices  68.5 us (8%)
  local copies, waits for them, and re-layouts  40 us (5%)
  between operations  15.7 us (2%)
    dot_general x23, matrix products, dot(): return jnp.einsum(spec, left, right, preferred_element_type=high_type)  223 us
    pallas_call x4, Pallas kernels, self_call(): pl.pallas_call(functools.partial(body, T=T, S=S), grid=(HEADS,), in_specs...  136 us
    pallas_call x1, Pallas kernels, cross_backward(): pl.pallas_call(functools.partial(cross_backward_kernel, step=count // 2),...  65.1 us
    pallas_call x2, Pallas kernels, weight_grads(): pl.pallas_call(functools.partial(weight_grads_kernel, xs=len(xs), terms=t...  52.8 us
    pallas_call x4, Pallas kernels, back_rows(): pl.pallas_call(functools.partial(back_rows_kernel, pairs=len(gs), base=ba...  48.3 us
    pallas_call x1, Pallas kernels, cross_forward(): pl.pallas_call(cross_forward_kernel, grid=(B, HEADS), in_specs=[per_head(...  46.1 us
    pallas_call x1, Pallas kernels, ffn_first(): pl.pallas_call(functools.partial(ffn_kernel, step=FFN_STEP), grid=(hidden...  36.1 us
    ppermute x6, starting transfers between devices, on_device(): lax.ppermute(sent, 'seq', [(i, i + hop) for i in range(seq_parts - hop)])  27 us
  transfers between devices with their start and end apart: 38, of which 12 were waited for; matrix products, arithmetic and copies ran while one was open for 26% of the time, Pallas kernels for 33%

profile of v3, /device:TPU:0, one launch (start us, length us, event | category | flops | bytes accessed | tf_op | source)
XLA Modules:
  0.0 878.1 jit_solution(14570403059832620736)
XLA Ops:
  30.1 7.8 convolution_convert_fusion.4.refs_1_
  81.8 26.8 %self_forward.2 = (bf16[1024,1536]{1,0:T(8,128)(2,1)}, f32[2,16,1,768]{3,2,1,0:T(1,128)}) custom-call(bf16[1024,1536]{1,0:T(8,128)(2,1)} %multiply_convert_fusion.2.refs_0_, bf16[1024,1536]{1,0:T(8,128)(2,1)} %convolution_convert_fusion.4.refs_1_, bf16[1024,1536]{1,0:T(8,128)(2,1)} %add_convert_fusion.2.refs_2_, bf16[1024,768]{1,0:T(8,128)(2,1)} %fusion.57.refs_3_, ...), custom_call_target="tpu_custom_call" | custom-call | flops 12884901888 | bytes 14680064 | tf_op jit(solution)/shard_map/self_forward/pallas_call | solution.py:379
  119.6 26.8 %self_forward.3 = (bf16[1024,1536]{1,0:T(8,128)(2,1)}, f32[2,16,1,768]{3,2,1,0:T(1,128)}) custom-call(bf16[1024,1536]{1,0:T(8,128)(2,1)} %multiply_convert_fusion.2.refs_0_, bf16[1024,1536]{1,0:T(8,128)(2,1)} %convolution_convert_fusion.4.refs_1_, bf16[1024,1536]{1,0:T(8,128)(2,1)} %add_convert_fusion.2.refs_2_, ...), custom_call_target="tpu_custom_call", output_to_operand_aliasing={{0}: (8, {}), {1}: (9, {})} | custom-call | flops 12884901888 | bytes 14680064 | tf_op jit(solution)/shard_map/self_forward/pallas_call | solution.py:379
  146.5 7.6 fusion.92
  165.7 9.5 %convert_bitcast_fusion.k_ref = bf16[1024,2048]{1,0:T(8,128)(2,1)} fusion(bf16[2048,1024]{1,0:T(8,128)(2,1)} %bitcast.324, bf16[3,1024,1024]{2,1,0:T(8,128)(2,1)} %refs_3_.3), kind=kOutput, calls=%fused_computation.49 | convolution fusion | flops 4297064448 | bytes 10485760 | tf_op jit(solution)/shard_map/de,rd->er/dot_general | solution.py:547
  175.2 7.9 fusion.10.v_ref
  183.2 46.1 %cross_forward.1 = (bf16[1024,1536]{1,0:T(8,128)(2,1)}, f32[2,16,1,768]{3,2,1,0:T(1,128)}) custom-call(bf16[1024,1536]{1,0:T(8,128)(2,1)} %fusion.13.q_ref, bf16[1024,2048]{1,0:T(8,128)(2,1)} %convert_bitcast_fusion.k_ref, bf16[1024,2048]{1,0:T(8,128)(2,1)} %fusion.10.v_ref, bf16[2,16,1024]{2,1,0:T(8,128)(2,1)} %get-tuple-element.253.mark_ref), custom_call_target="tpu_custom_call" | custom-call | flops 25769803776 | bytes 29360128 | tf_op jit(solution)/shard_map/cross_forward/pallas_call | solution.py:339
  229.3 8.6 fusion.93
  241.5 36.1 %ffn_first.1 = (bf16[1536,4096]{1,0:T(8,128)(2,1)}, bf16[1536,4096]{1,0:T(8,128)(2,1)}) custom-call(bf16[1536,1024]{1,0:T(8,128)(2,1)} %fusion.9.x_ref, bf16[1024,4096]{1,0:T(8,128)(2,1)} %w_ref.1, f32[1,4096]{1,0:T(1,128)} %bitcast.307), custom_call_target="tpu_custom_call" | custom-call | flops 12884901888 | bytes 25165824 | tf_op jit(solution)/shard_map/ffn_first/pallas_call | solution.py:520
  277.6 19.9 %fusion.94 = (f32[1536]{0:T(1024)S(1)}, f32[1536,1024]{1,0:T(8,128)S(1)}) fusion(f32[1024]{0:T(1024)S(1)} %copy-done.43, bf16[1536,4096]{1,0:T(8,128)(2,1)} %get-tuple-element.119, bf16[4096,1024]{1,0:T(8,128)(2,1)} %param.39, f32[1024]{0:T(1024)S(1)} %bitcast.300, f32[1024]{0:T(1024)S(1)} %bitcast.293, f32[1536]{0:T(1024)S(1)} %add_rsqrt_fusion.1, ...), kind=kOutput, calls=%fused_computation.212 | convolution fusion | flops 12895909888 | bytes 33585152 | tf_op jit(solution)/shard_map/rf,fd->rd/dot_general | solution.py:547
  310.2 15.3 %convolution_convert_fusion.1 = bf16[4096,1024]{1,0:T(8,128)(2,1)} fusion(bf16[1536,4096]{1,0:T(8,128)(2,1)S(1)} %bitcast.328, bf16[1536,1024]{1,0:T(8,128)(2,1)S(1)} %get-tuple-element.192), kind=kOutput, calls=%fused_computation.4 | convolution fusion | flops 12889096192 | bytes 24117248 | tf_op jit(solution)/shard_map/rf,rd->fd/dot_general | solution.py:547
  325.7 21.3 %multiply_convert_fusion = bf16[1536,4096]{1,0:T(8,128)(2,1)} fusion(bf16[1536,4096]{1,0:T(8,128)(2,1)} %get-tuple-element.122, bf16[1536,1024]{1,0:T(8,128)(2,1)} %copy-done.6, bf16[4096,1024]{1,0:T(8,128)(2,1)} %param.39), kind=kOutput, calls=%fused_computation.1 | convolution fusion | flops 12903776256 | bytes 36700160 | tf_op jit(solution)/shard_map/rd,fd->rf/dot_general | solution.py:547
  347.0 19.3 %convolution_convert_fusion = bf16[1024,4096]{1,0:T(8,128)(2,1)} fusion(bf16[1536,1024]{1,0:T(8,128)(2,1)} %fusion.9.x_ref, bf16[1536,4096]{1,0:T(8,128)(2,1)} %multiply_convert_fusion), kind=kOutput, calls=%fused_computation.3 | convolution fusion | flops 12889096192 | bytes 24117248 | tf_op jit(solution)/shard_map/rd,rf->df/dot_general | solution.py:547
  366.4 29.3 %multiply_reduce_fusion = (f32[1024]{0:T(1024)}, f32[1536]{0:T(1024)S(1)}, f32[1536]{0:T(1024)S(1)}, f32[1024]{0:T(1024)}, f32[1536,1024]{1,0:T(8,128)}) fusion(f32[1536,1024]{1,0:T(8,128)} %copy-done.3, f32[1536]{0:T(1024)S(1)} %add_rsqrt_fusion.1, f32[1536]{0:T(1024)S(1)} %broadcast_multiply_fusion.7, f32[1024]{0:T(1024)S(1)} %bitcast.294, ...), kind=kOutput, calls=%fused_computation.18 | convolution fusion | flops 12900625408 | bytes 39882752 | tf_op jit(solution)/shard_map/rf,df->rd/dot_general | solution.py:547
  395.7 7.7 fusion.79
  416.3 65.1 %cross_backward.1 = (bf16[1024,1536]{1,0:T(8,128)(2,1)}, bf16[1024,2048]{1,0:T(8,128)(2,1)}, bf16[1024,2048]{1,0:T(8,128)(2,1)}) custom-call(bf16[1024,1536]{1,0:T(8,128)(2,1)} %fusion.13.q_ref, bf16[1024,2048]{1,0:T(8,128)(2,1)} %convert_bitcast_fusion.k_ref, bf16[1024,2048]{1,0:T(8,128)(2,1)} %fusion.10.v_ref, ...), custom_call_target="tpu_custom_call" | custom-call | flops 64424509440 | bytes 73400320 | tf_op jit(solution)/shard_map/cross_backward/pallas_call | solution.py:355
  481.4 25.7 %reduce-scatter.9.cloned.1.call-done = bf16[128,4096]{1,0:T(8,128)(2,1)} async-done(((bf16[1024,4096]{1,0:T(8,128)(2,1)}), bf16[128,4096]{1,0:T(8,128)(2,1)}) %reduce-scatter.9.cloned.1.call-update) | async-done | bytes 1048592 | tf_op jit(solution)/shard_map/reduce_scatter | solution.py:1200
  507.1 14.1 %encoder_rows.1 = bf16[2048,1024]{1,0:T(8,128)(2,1)} custom-call(bf16[1024,2048]{1,0:T(8,128)(2,1)} %get-tuple-element.131.refs_0_.refs_3_, bf16[1024,2048]{1,0:T(8,128)(2,1)} %get-tuple-element.132.refs_1_.refs_4_, bf16[3,1024,1024]{2,1,0:T(8,128)(2,1)} %refs_3_.3, bf16[3,1024,1024]{2,1,0:T(8,128)(2,1)} %refs_3_.3), custom_call_target="tpu_custom_call" | custom-call | flops 8589934592 | bytes 25165824 | tf_op jit(solution)/shard_map/encoder_rows/pallas_call | solution.py:483
  528.8 20.5 %cross_weights.1 = (bf16[8,384,1024]{2,1,0:T(8,128)(2,1)}, f32[3,1024,128]{2,1,0:T(8,128)}) custom-call(bf16[1536,1024]{1,0:T(8,128)(2,1)} %copy-done.11, bf16[2048,1024]{1,0:T(8,128)(2,1)} %bitcast.325, bf16[1024,1536]{1,0:T(8,128)(2,1)} %get-tuple-element.139.refs_2_, bf16[1024,2048]{1,0:T(8,128)(2,1)} %get-tuple-element.131.refs_0_.refs_3_, ...), custom_call_target="tpu_custom_call" | custom-call | flops 11811160064 | bytes 46137344 | tf_op jit(solution)/shard_map/cross_weights/pallas_call | solution.py:442
  550.5 11.5 %multiply_reduce_fusion.1 = (f32[1024]{0:T(1024)S(1)}, f32[1536]{0:T(1024)S(1)}, f32[1536]{0:T(1024)S(1)}, f32[1024]{0:T(1024)S(1)}, f32[1536,1024]{1,0:T(8,128)S(1)}) fusion(f32[1536,1024]{1,0:T(8,128)} %copy-done.2, f32[1536]{0:T(1024)S(1)} %copy-done.27, f32[1536]{0:T(1024)S(1)} %copy-done.25, f32[1024]{0:T(1024)S(1)} %bitcast.290, ...), kind=kOutput, calls=%fused_computation.19 | convolution fusion | flops 3236948992 | bytes 24154112 | tf_op jit(solution)/shard_map/er,de->rd/dot_general | solution.py:547
  572.4 7.6 fusion.12.refs_10_
  580.1 41.3 %self_backward.2 = (bf16[1024,1536]{1,0:T(8,128)(2,1)}, bf16[2,1024,1536]{2,1,0:T(8,128)(2,1)}, bf16[512,1536]{1,0:T(8,128)(2,1)}, bf16[2,1024,768]{2,1,0:T(8,128)(2,1)}) custom-call(bf16[1024,1536]{1,0:T(8,128)(2,1)} %multiply_convert_fusion.2.refs_0_, bf16[1024,1536]{1,0:T(8,128)(2,1)} %convolution_convert_fusion.4.refs_1_, ...), custom_call_target="tpu_custom_call" | custom-call | flops 32212254720 | bytes 36700160 | tf_op jit(solution)/shard_map/self_backward/pallas_call | solution.py:379
  621.3 7.2 far_rows.2
  640.9 41.4 %self_backward.3 = (bf16[1024,1536]{1,0:T(8,128)(2,1)}, bf16[2,1024,1536]{2,1,0:T(8,128)(2,1)}, bf16[512,1536]{1,0:T(8,128)(2,1)}, bf16[2,1024,768]{2,1,0:T(8,128)(2,1)}) custom-call(bf16[1024,1536]{1,0:T(8,128)(2,1)} %multiply_convert_fusion.2.refs_0_, ...), custom_call_target="tpu_custom_call", output_to_operand_aliasing={{0}: (11, {}), {1}: (12, {}), {2}: (13, {})} | custom-call | flops 32212254720 | bytes 36700160 | tf_op jit(solution)/shard_map/self_backward/pallas_call | solution.py:379
  682.5 7.4 far_rows.3
  695.2 32.3 %self_weights.1 = (bf16[32,112,1024]{2,1,0:T(8,128)(2,1)}, f32[4,1024,128]{2,1,0:T(8,128)}) custom-call(bf16[1536,1024]{1,0:T(8,128)(2,1)} %bitcast.277, bf16[768,1024]{1,0:T(8,128)(2,1)} %copy-done.12, bf16[768,1024]{1,0:T(8,128)(2,1)} %copy-done.13, bf16[1024,1536]{1,0:T(8,128)(2,1)} %get-tuple-element.171.refs_3_.refs_0_, ...), custom_call_target="tpu_custom_call" | custom-call | flops 19327352832 | bytes 75497472 | tf_op jit(solution)/shard_map/self_weights/pallas_call | solution.py:442
  754.2 19.6 %near_rows.1 = bf16[1536,1024]{1,0:T(8,128)(2,1)} custom-call(bf16[1024,1536]{1,0:T(8,128)(2,1)} %get-tuple-element.171.refs_3_.refs_0_, bf16[2,1024,1536]{2,1,0:T(8,128)(2,1)} %get-tuple-element.160.refs_4_.refs_5_.refs_1_.refs_2_, bf16[2,1024,1536]{2,1,0:T(8,128)(2,1)} %get-tuple-element.160.refs_4_.refs_5_.refs_1_.refs_2_, ...), custom_call_target="tpu_custom_call" | custom-call | flops 11274289152 | bytes 27787264 | tf_op jit(solution)/shard_map/near_rows/pallas_call | solution.py:483
  773.8 7.9 collective-permute-done.17
  796.5 7.1 convert_reduce_fusion
  830.1 12.1 %collective-permute-done.27 = f32[4,4480]{1,0:T(4,128)S(1)} collective-permute-done((f32[4,4480]{1,0:T(4,128)S(1)}, f32[4,4480]{1,0:T(4,128)S(1)}, u32[]{:S(2)}, u32[]{:S(2)}) %collective-permute-start.27) | collective-permute-done | bytes 71712 | tf_op jit(solution)/shard_map/ppermute | solution.py:1410
  845.0 8.6 collective-permute-done.20
  854.5 7.0 collective-permute-done.21
  (335 shorter events, 235.8 us)
Async XLA Ops:
  7.2 158.5 %all-gather.2.cloned.1.call-start = ((), (), s32[]{:S(2)}) async-start(), calls=%async_computation.6 | async-start | bytes 5242880 | tf_op jit(solution)/shard_map/all_gather | solution.py:1143
  9.6 46.7 %collective-permute-start.2 = (bf16[256,1024]{1,0:T(8,128)(2,1)}, bf16[256,1024]{1,0:T(8,128)(2,1)}, u32[]{:S(2)}, u32[]{:S(2)}) collective-permute-start(bf16[256,1024]{1,0:T(8,128)(2,1)} %get-tuple-element.224), channel_id=1, source_target_pairs={{0,1},{1,2},{2,3},{4,5},{5,6},{6,7},{8,9},{9,10},{10,11},{12,13},{... | collective-permute-start | bytes 1572872 | tf_op jit(solution)/shard_map/ppermute | solution.py:1137
  15.3 41.0 %collective-permute-start.1 = (bf16[256,1024]{1,0:T(8,128)(2,1)}, bf16[256,1024]{1,0:T(8,128)(2,1)}, u32[]{:S(2)}, u32[]{:S(2)}) collective-permute-start(bf16[256,1024]{1,0:T(8,128)(2,1)} %get-tuple-element.224), channel_id=1, source_target_pairs={{0,2},{1,3},{4,6},{5,7},{8,10},{9,11},{12,14},{13,15},{16,18},{17,... | collective-permute-start | bytes 1572872 | tf_op jit(solution)/shard_map/ppermute | solution.py:1137
  19.9 36.5 %collective-permute-start = (bf16[256,1024]{1,0:T(8,128)(2,1)}, bf16[256,1024]{1,0:T(8,128)(2,1)}, u32[]{:S(2)}, u32[]{:S(2)}) collective-permute-start(bf16[256,1024]{1,0:T(8,128)(2,1)} %get-tuple-element.224), channel_id=1, source_target_pairs={{0,3},{4,7},{8,11},{12,15},{16,19},{20,23},{24,27},{28,31}} | collective-permute-start | bytes 1572872 | tf_op jit(solution)/shard_map/ppermute | solution.py:1137
  57.8 50.8 %collective-permute-start.5 = (bf16[256,1024]{1,0:T(8,128)(2,1)}, bf16[256,1024]{1,0:T(8,128)(2,1)S(1)}, u32[]{:S(2)}, u32[]{:S(2)}) collective-permute-start(bf16[256,1024]{1,0:T(8,128)(2,1)} %get-tuple-element.109), channel_id=1, source_target_pairs={{0,1},{1,2},{2,3},{4,5},{5,6},{6,7},{8,9},{9,10},{10,11},{12,13},{... | collective-permute-start | bytes 1572872 | tf_op jit(solution)/shard_map/ppermute | solution.py:1137
  64.8 43.9 %collective-permute-start.4 = (bf16[256,1024]{1,0:T(8,128)(2,1)}, bf16[256,1024]{1,0:T(8,128)(2,1)S(1)}, u32[]{:S(2)}, u32[]{:S(2)}) collective-permute-start(bf16[256,1024]{1,0:T(8,128)(2,1)} %get-tuple-element.109), channel_id=1, source_target_pairs={{0,2},{1,3},{4,6},{5,7},{8,10},{9,11},{12,14},{13,15},{16,18},{17,... | collective-permute-start | bytes 1572872 | tf_op jit(solution)/shard_map/ppermute | solution.py:1137
  70.0 38.6 %collective-permute-start.3 = (bf16[256,1024]{1,0:T(8,128)(2,1)}, bf16[256,1024]{1,0:T(8,128)(2,1)}, u32[]{:S(2)}, u32[]{:S(2)}) collective-permute-start(bf16[256,1024]{1,0:T(8,128)(2,1)} %get-tuple-element.109), channel_id=1, source_target_pairs={{0,3},{4,7},{8,11},{12,15},{16,19},{20,23},{24,27},{28,31}} | collective-permute-start | bytes 1572872 | tf_op jit(solution)/shard_map/ppermute | solution.py:1137
  81.7 399.7 %reduce-scatter.7.cloned.1.call-start = ((), (), s32[]{:S(2)}) async-start(), calls=%async_computation.7 | async-start | bytes 9437184 | tf_op jit(solution)/shard_map/reduce_scatter | solution.py:1200
  325.6 181.5 %reduce-scatter.9.cloned.1.call-start = ((), (), s32[]{:S(2)}) async-start(), calls=%async_computation.8 | async-start | bytes 9437184 | tf_op jit(solution)/shard_map/reduce_scatter | solution.py:1200
  366.3 316.1 %reduce-scatter.11.cloned.1.call-start = ((), (), s32[]{:S(2)}) async-start(), calls=%async_computation.9 | async-start | bytes 5242880 | tf_op jit(solution)/shard_map/reduce_scatter | solution.py:1270
  521.2 264.5 %reduce-scatter.13.cloned.1.call-start = ((), (), s32[]{:S(2)}) async-start(), calls=%async_computation.10 | async-start | bytes 2359296 | tf_op jit(solution)/shard_map/reduce_scatter | solution.py:1200
  523.2 26.3 %collective-permute-start.6 = (bf16[256,1024]{1,0:T(8,128)(2,1)S(1)}, bf16[256,1024]{1,0:T(8,128)(2,1)S(1)}, u32[]{:S(2)}, u32[]{:S(2)}) collective-permute-start(bf16[256,1024]{1,0:T(8,128)(2,1)S(1)} %fusion.69), channel_id=1, source_target_pairs={{0,1},{1,2},{2,3},{3,0},{4,5},{5,6},{6,7},{7,4},{8,9},{9,10},{10,1... | collective-permute-start | bytes 1572872 | tf_op jit(solution)/shard_map/ppermute | solution.py:1233
  549.4 236.4 %reduce-scatter.17.cloned.1.call-start = ((), (), s32[]{:S(2)}) async-start(), calls=%async_computation.12 | async-start | bytes 2359296 | tf_op jit(solution)/shard_map/reduce_scatter | solution.py:1200
  550.5 84.8 %collective-permute-start.7 = (bf16[256,1024]{1,0:T(8,128)(2,1)}, bf16[256,1024]{1,0:T(8,128)(2,1)}, u32[]{:S(2)}, u32[]{:S(2)}) collective-permute-start(bf16[256,1024]{1,0:T(8,128)(2,1)} %fusion.61), channel_id=1, source_target_pairs={{0,1},{1,2},{2,3},{3,0},{4,5},{5,6},{6,7},{7,4},{8,9},{9,10},{10,1... | collective-permute-start | bytes 1572872 | tf_op jit(solution)/shard_map/ppermute | solution.py:1233
  580.0 205.8 %reduce-scatter.15.cloned.1.call-start = ((), (), s32[]{:S(2)}) async-start(), calls=%async_computation.11 | async-start | bytes 7077888 | tf_op jit(solution)/shard_map/reduce_scatter | solution.py:1200
  631.1 51.3 %collective-permute-start.10 = (bf16[256,1024]{1,0:T(8,128)(2,1)}, bf16[256,1024]{1,0:T(8,128)(2,1)S(1)}, u32[]{:S(2)}, u32[]{:S(2)}) collective-permute-start(bf16[256,1024]{1,0:T(8,128)(2,1)} %get-tuple-element.229), channel_id=1, source_target_pairs={{3,0},{7,4},{11,8},{15,12},{19,16},{23,20},{27,24},{31,28}} | collective-permute-start | bytes 1572872 | tf_op jit(solution)/shard_map/ppermute | solution.py:1316
  632.4 50.0 %collective-permute-start.9 = (bf16[256,1024]{1,0:T(8,128)(2,1)}, bf16[256,1024]{1,0:T(8,128)(2,1)S(1)}, u32[]{:S(2)}, u32[]{:S(2)}) collective-permute-start(bf16[256,1024]{1,0:T(8,128)(2,1)} %get-tuple-element.230), channel_id=1, source_target_pairs={{2,0},{3,1},{6,4},{7,5},{10,8},{11,9},{14,12},{15,13},{18,16},{19,... | collective-permute-start | bytes 1572872 | tf_op jit(solution)/shard_map/ppermute | solution.py:1316
  633.7 48.7 %collective-permute-start.8 = (bf16[256,1024]{1,0:T(8,128)(2,1)}, bf16[256,1024]{1,0:T(8,128)(2,1)}, u32[]{:S(2)}, u32[]{:S(2)}) collective-permute-start(bf16[256,1024]{1,0:T(8,128)(2,1)} %get-tuple-element.231), channel_id=1, source_target_pairs={{1,0},{2,1},{3,2},{5,4},{6,5},{7,6},{9,8},{10,9},{11,10},{13,12},{... | collective-permute-start | bytes 1572872 | tf_op jit(solution)/shard_map/ppermute | solution.py:1316
  636.5 45.9 %collective-permute-start.11 = (bf16[256,1024]{1,0:T(8,128)(2,1)S(1)}, bf16[256,1024]{1,0:T(8,128)(2,1)}, u32[]{:S(2)}, u32[]{:S(2)}) collective-permute-start(bf16[256,1024]{1,0:T(8,128)(2,1)S(1)} %fusion.60), channel_id=1, source_target_pairs={{0,1},{1,2},{2,3},{3,0},{4,5},{5,6},{6,7},{7,4},{8,9},{9,10},{10,1... | collective-permute-start | bytes 1572872 | tf_op jit(solution)/shard_map/ppermute | solution.py:1233
  691.3 36.2 %collective-permute-start.14 = (bf16[256,1024]{1,0:T(8,128)(2,1)S(1)}, bf16[256,1024]{1,0:T(8,128)(2,1)}, u32[]{:S(2)}, u32[]{:S(2)}) collective-permute-start(bf16[256,1024]{1,0:T(8,128)(2,1)S(1)} %get-tuple-element.226), channel_id=1, source_target_pairs={{3,0},{7,4},{11,8},{15,12},{19,16},{23,20},{27,24},{31,28}} | collective-permute-start | bytes 1572872 | tf_op jit(solution)/shard_map/ppermute | solution.py:1316
  692.6 34.9 %collective-permute-start.13 = (bf16[256,1024]{1,0:T(8,128)(2,1)S(1)}, bf16[256,1024]{1,0:T(8,128)(2,1)}, u32[]{:S(2)}, u32[]{:S(2)}) collective-permute-start(bf16[256,1024]{1,0:T(8,128)(2,1)S(1)} %get-tuple-element.227), channel_id=1, source_target_pairs={{2,0},{3,1},{6,4},{7,5},{10,8},{11,9},{14,12},{15,13},{18,16},{19,... | collective-permute-start | bytes 1572872 | tf_op jit(solution)/shard_map/ppermute | solution.py:1316
  693.9 33.7 %collective-permute-start.12 = (bf16[256,1024]{1,0:T(8,128)(2,1)S(1)}, bf16[256,1024]{1,0:T(8,128)(2,1)}, u32[]{:S(2)}, u32[]{:S(2)}) collective-permute-start(bf16[256,1024]{1,0:T(8,128)(2,1)S(1)} %get-tuple-element.228), channel_id=1, source_target_pairs={{1,0},{2,1},{3,2},{5,4},{6,5},{7,6},{9,8},{10,9},{11,10},{13,12},{... | collective-permute-start | bytes 1572872 | tf_op jit(solution)/shard_map/ppermute | solution.py:1316
  745.1 36.7 %collective-permute-start.17 = (bf16[2,224,1024]{2,1,0:T(8,128)(2,1)}, bf16[2,224,1024]{2,1,0:T(8,128)(2,1)}, u32[]{:S(2)}, u32[]{:S(2)}) collective-permute-start(bf16[2,224,1024]{2,1,0:T(8,128)(2,1)} %dynamic-slice_bitcast_fusion.1), channel_id=1, source_target_pairs={{0,16},{4,20},{8,24},{12,28},{16,0},{20,4},{24,8},{28,12},{1,17},{... | collective-permute-start | bytes 2752520 | tf_op jit(solution)/shard_map/ppermute | solution.py:1209
  747.6 36.6 %collective-permute-start.16 = (bf16[2,224,1024]{2,1,0:T(8,128)(2,1)}, bf16[2,224,1024]{2,1,0:T(8,128)(2,1)}, u32[]{:S(2)}, u32[]{:S(2)}) collective-permute-start(bf16[2,224,1024]{2,1,0:T(8,128)(2,1)} %dynamic-slice_bitcast_fusion.2), channel_id=1, source_target_pairs={{0,8},{4,12},{8,0},{12,4},{16,24},{20,28},{24,16},{28,20},{1,9},{5... | collective-permute-start | bytes 2752520 | tf_op jit(solution)/shard_map/ppermute | solution.py:1209
  803.7 8.2 collective-permute-start.23
  805.2 24.7 %collective-permute-start.28 = (bf16[160,1024]{1,0:T(8,128)(2,1)S(1)}, bf16[160,1024]{1,0:T(8,128)(2,1)S(1)}, u32[]{:S(2)}, u32[]{:S(2)}) collective-permute-start(bf16[160,1024]{1,0:T(8,128)(2,1)S(1)} %dynamic-slice_bitcast_fusion.5), channel_id=1, source_target_pairs={{0,1},{1,2},{2,3},{3,0},{4,5},{5,6},{6,7},{7,4},{8,9},{9,10},{10,1... | collective-permute-start | bytes 983048 | tf_op jit(solution)/shard_map/ppermute | solution.py:1233
  817.9 24.8 %collective-permute-start.19 = (bf16[224,1024]{1,0:T(8,128)(2,1)S(1)}, bf16[224,1024]{1,0:T(8,128)(2,1)S(1)}, u32[]{:S(2)}, u32[]{:S(2)}) collective-permute-start(bf16[224,1024]{1,0:T(8,128)(2,1)S(1)} %dynamic-slice_bitcast_fusion.3), channel_id=1, source_target_pairs={{0,8},{4,12},{8,0},{12,4},{16,24},{20,28},{24,16},{28,20},{1,9},{5... | collective-permute-start | bytes 1376264 | tf_op jit(solution)/shard_map/ppermute | solution.py:1209
  822.8 20.1 %collective-permute-start.18 = (bf16[224,1024]{1,0:T(8,128)(2,1)S(1)}, bf16[224,1024]{1,0:T(8,128)(2,1)S(1)}, u32[]{:S(2)}, u32[]{:S(2)}) collective-permute-start(bf16[224,1024]{1,0:T(8,128)(2,1)S(1)} %dynamic-slice_bitcast_fusion.4), channel_id=1, source_target_pairs={{0,16},{4,20},{8,24},{12,28},{16,0},{20,4},{24,8},{28,12},{1,17},{... | collective-permute-start | bytes 1376264 | tf_op jit(solution)/shard_map/ppermute | solution.py:1209
  825.3 16.9 %collective-permute-start.27 = (f32[4,4480]{1,0:T(4,128)S(1)}, f32[4,4480]{1,0:T(4,128)S(1)}, u32[]{:S(2)}, u32[]{:S(2)}) collective-permute-start(f32[4,4480]{1,0:T(4,128)S(1)} %add.410), channel_id=1, source_target_pairs={{0,2},{1,3},{2,0},{3,1},{4,6},{5,7},{6,4},{7,5},{8,10},{9,11},{10,... | collective-permute-start | bytes 215048 | tf_op jit(solution)/shard_map/ppermute | solution.py:1410
  830.0 23.7 %collective-permute-start.29 = (bf16[160,1024]{1,0:T(8,128)(2,1)S(1)}, bf16[160,1024]{1,0:T(8,128)(2,1)S(1)}, u32[]{:S(2)}, u32[]{:S(2)}) collective-permute-start(bf16[160,1024]{1,0:T(8,128)(2,1)S(1)} %fusion.65), channel_id=1, source_target_pairs={{0,1},{1,2},{2,3},{3,0},{4,5},{5,6},{6,7},{7,4},{8,9},{9,10},{10,1... | collective-permute-start | bytes 983048 | tf_op jit(solution)/shard_map/ppermute | solution.py:1233
  843.2 10.4 %collective-permute-start.20 = (bf16[112,1024]{1,0:T(8,128)(2,1)S(1)}, bf16[112,1024]{1,0:T(8,128)(2,1)S(1)}, u32[]{:S(2)}, u32[]{:S(2)}) collective-permute-start(bf16[112,1024]{1,0:T(8,128)(2,1)S(1)} %dynamic-slice_bitcast_fusion.6), channel_id=1, source_target_pairs={{0,1},{1,2},{2,3},{3,0},{4,5},{5,6},{6,7},{7,4},{8,9},{9,10},{10,1... | collective-permute-start | bytes 688136 | tf_op jit(solution)/shard_map/ppermute | solution.py:1233
  853.9 11.2 %collective-permute-start.30 = (bf16[160,1024]{1,0:T(8,128)(2,1)S(1)}, bf16[160,1024]{1,0:T(8,128)(2,1)S(1)}, u32[]{:S(2)}, u32[]{:S(2)}) collective-permute-start(bf16[160,1024]{1,0:T(8,128)(2,1)S(1)} %fusion.64), channel_id=1, source_target_pairs={{0,1},{1,2},{2,3},{3,0},{4,5},{5,6},{6,7},{7,4},{8,9},{9,10},{10,1... | collective-permute-start | bytes 983048 | tf_op jit(solution)/shard_map/ppermute | solution.py:1233
  (66 other events, 982.0 us)
Sparse Core Ops, SparseCore 0:
  81.9 83.8 all-gather.1
  325.7 106.1 reduce-scatter.6
  435.8 71.2 reduce-scatter.8
  521.4 97.4 reduce-scatter.10
  622.3 41.2 reduce-scatter.12
  666.8 41.1 reduce-scatter.16
  711.8 72.1 reduce-scatter.14

commit v4 on v3

--- a/solution.py
+++ b/solution.py
@@ -18,6 +18,7 @@
 NEGATIVE = -1e30
 EPSILON = 1e-05
 VMEM_LIMIT = 60 * 2**20
+GROUPS = {"cross_forward": 4, "cross_backward": 2, "self_forward": 1, "self_backward": 2}
 SPLIT = 2
 FFN_COLS = 1024
 FFN_ROWS = 768
@@ -309,6 +310,24 @@
         out_ref[...] = total.astype(low_type)
 
 
+def by_head(body, group, split, **static):
+    def kernel(*refs):
+        for head in range(group):
+            views = []
+            for ref, how in zip(refs, split, strict=True):
+                if how is None:
+                    views.append(ref)
+                elif how == 0:
+                    views.append(ref.at[head])
+                elif isinstance(how, tuple):
+                    views.append(ref.at[:, pl.ds(head * how[1], how[1]), :])
+                else:
+                    views.append(ref.at[pl.ds(head * how, how), :])
+            body(*views, **static)
+
+    return kernel
+
+
 def per_head(rows, count):
     return pl.BlockSpec((rows, count), lambda b, h: (h, b))
 
@@ -317,8 +336,8 @@
     return pl.BlockSpec((None, 16, keys), lambda b, h: (b, 0, 0))
 
 
-def per_total(count):
-    return pl.BlockSpec((None, None, 1, count), lambda b, h: (b, h, 0, 0))
+def per_total(group, count):
+    return pl.BlockSpec((None, group, 1, count), lambda b, h: (b, h, 0, 0))
 
 
 def like(array):
@@ -335,12 +354,13 @@
 
 def cross_forward(q, k, v, mark):
     B, _, keys = mark.shape
-    count = q.shape[1] // B
+    count, group = q.shape[1] // B, GROUPS["cross_forward"]
+    size = group * SIZE
     return pl.pallas_call(
-        cross_forward_kernel,
-        grid=(B, HEADS),
-        in_specs=[per_head(SIZE, count), per_head(SIZE, keys), per_head(SIZE, keys), per_sequence(keys)],
-        out_specs=[per_head(SIZE, count), per_total(count)],
+        by_head(cross_forward_kernel, group, [SIZE, SIZE, SIZE, None, SIZE, 0]),
+        grid=(B, HEADS // group),
+        in_specs=[per_head(size, count), per_head(size, keys), per_head(size, keys), per_sequence(keys)],
+        out_specs=[per_head(size, count), per_total(group, count)],
         out_shape=[like(q), jax.ShapeDtypeStruct((B, HEADS, 1, count), high_type)],
         cost_estimate=cost(B, count, keys, 2),
         compiler_params=pltpu.CompilerParams(vmem_limit_bytes=VMEM_LIMIT),
@@ -350,12 +370,18 @@
 
 def cross_backward(q, k, v, mark, o, total, do):
     B, _, keys = mark.shape
-    count = q.shape[1] // B
-    row, key = per_head(SIZE, count), per_head(SIZE, keys)
+    count, group = q.shape[1] // B, GROUPS["cross_backward"]
+    size = group * SIZE
+    row, key = per_head(size, count), per_head(size, keys)
     return pl.pallas_call(
-        functools.partial(cross_backward_kernel, step=count // 2),
-        grid=(B, HEADS),
-        in_specs=[row, key, key, per_sequence(keys), row, per_total(count), row],
+        by_head(
+            cross_backward_kernel,
+            group,
+            [SIZE, SIZE, SIZE, None, SIZE, 0, SIZE, SIZE, SIZE, SIZE, None, None],
+            step=count // 2,
+        ),
+        grid=(B, HEADS // group),
+        in_specs=[row, key, key, per_sequence(keys), row, per_total(group, count), row],
         out_specs=[row, key, key],
         out_shape=[like(q), like(k), like(v)],
         scratch_shapes=[pltpu.VMEM((SIZE, keys), high_type)] * 2,
@@ -365,20 +391,30 @@
     )(q, k, v, mark, o, total, do)
 
 
-def self_call(body, b, inputs, more, earlier, T, S, outs, out_specs, products, name):
+def self_call(body, b, inputs, more, earlier, T, S, outs, out_specs, out_split, products, name):
     q, far, mark, table = inputs[0], inputs[3].shape[1], inputs[6], inputs[7]
-    count = S * T
-    row = pl.BlockSpec((SIZE, count), lambda h: (h, b))
-    far_row = pl.BlockSpec((SIZE, far), lambda h: (h, 0))
-    total = pl.BlockSpec((None, None, 1, count), lambda h: (b, h, 0, 0))
-    specs = [row, row, row, far_row, far_row, pl.BlockSpec((BUCKETS, count), lambda h: (h, b))]
+    count, group = S * T, GROUPS[name]
+    row = pl.BlockSpec((group * SIZE, count), lambda h: (h, b))
+    far_row = pl.BlockSpec((group * SIZE, far), lambda h: (h, 0))
+    total = pl.BlockSpec((None, group, 1, count), lambda h: (b, h, 0, 0))
+    specs = [row, row, row, far_row, far_row, pl.BlockSpec((group * BUCKETS, count), lambda h: (h, b))]
     specs.append(pl.BlockSpec((None, 16, far + T), lambda h: (b, 0, 0)))
     specs.append(pl.BlockSpec(table.shape, lambda h: (0, 0)))
     specs += [row, total, row][: len(more)]
     held = len(specs)
     return pl.pallas_call(
-        functools.partial(body, T=T, S=S),
-        grid=(HEADS,),
+        by_head(
+            body,
+            group,
+            [SIZE] * 5
+            + [BUCKETS, None, None]
+            + [SIZE, 0, SIZE][: len(more)]
+            + [None] * len(earlier)
+            + out_split,
+            T=T,
+            S=S,
+        ),
+        grid=(HEADS // group,),
         in_specs=specs + [pl.BlockSpec(memory_space=pl.ANY)] * len(earlier),
         out_specs=out_specs,
         out_shape=outs,
@@ -390,7 +426,7 @@
 
 
 def self_forward(b, inputs, earlier, T, S):
-    q, mark, count = inputs[0], inputs[6], S * T
+    q, mark, count, group = inputs[0], inputs[6], S * T, GROUPS["self_forward"]
     return self_call(
         self_forward_kernel,
         b,
@@ -401,9 +437,10 @@
         S,
         [like(q), jax.ShapeDtypeStruct((mark.shape[0], HEADS, 1, count), high_type)],
         [
-            pl.BlockSpec((SIZE, count), lambda h: (h, b)),
-            pl.BlockSpec((None, None, 1, count), lambda h: (b, h, 0, 0)),
+            pl.BlockSpec((group * SIZE, count), lambda h: (h, b)),
+            pl.BlockSpec((None, group, 1, count), lambda h: (b, h, 0, 0)),
         ],
+        [SIZE, 0],
         2,
         "self_forward",
     )
@@ -411,6 +448,7 @@
 
 def self_backward(b, inputs, more, earlier, T, S):
     q, rel, count, far = inputs[0], inputs[5], S * T, inputs[3].shape[1]
+    group = GROUPS["self_backward"]
 
     def pair(columns):
         return jax.ShapeDtypeStruct((2, q.shape[0], columns), low_type)
@@ -425,11 +463,12 @@
         S,
         [like(q), pair(q.shape[1]), like(rel), pair(far)],
         [
-            pl.BlockSpec((SIZE, count), lambda h: (h, b)),
-            pl.BlockSpec((2, SIZE, count), lambda h: (0, h, b)),
-            pl.BlockSpec((BUCKETS, count), lambda h: (h, b)),
-            pl.BlockSpec((2, SIZE, far), lambda h: (0, h, 0)),
+            pl.BlockSpec((group * SIZE, count), lambda h: (h, b)),
+            pl.BlockSpec((2, group * SIZE, count), lambda h: (0, h, b)),
+            pl.BlockSpec((group * BUCKETS, count), lambda h: (h, b)),
+            pl.BlockSpec((2, group * SIZE, far), lambda h: (0, h, 0)),
         ],
+        [SIZE, (2, SIZE), BUCKETS, (2, SIZE)],
         5,
         "self_backward",
     )
@@ -496,6 +535,37 @@
         compiler_params=pltpu.CompilerParams(vmem_limit_bytes=VMEM_LIMIT),
         name=name,
     )(*arrays, *weights, *extra)
+
+
+def keys_and_values_kernel(x_ref, wk_ref, wv_ref, b_ref, k_ref, v_ref):
+    x = x_ref[...]
+    k_ref[...] = contract(wk_ref[...], x, 0, 1).astype(low_type)
+    v_ref[...] = (contract(wv_ref[...], x, 0, 1) + b_ref[...]).astype(low_type)
+
+
+def keys_and_values(x, weights, bias):
+    rows, width = x.shape
+    columns = width // SPLIT
+    out = jax.ShapeDtypeStruct((width, rows), low_type)
+    return pl.pallas_call(
+        keys_and_values_kernel,
+        grid=(SPLIT,),
+        in_specs=[
+            pl.BlockSpec((rows, width), lambda e: (0, 0)),
+            pl.BlockSpec((None, width, columns), lambda e: (1, 0, e)),
+            pl.BlockSpec((None, width, columns), lambda e: (2, 0, e)),
+            pl.BlockSpec((columns, 1), lambda e: (e, 0)),
+        ],
+        out_specs=[pl.BlockSpec((columns, rows), lambda e: (e, 0))] * 2,
+        out_shape=[out, out],
+        cost_estimate=pl.CostEstimate(
+            flops=4 * rows * width * width,
+            bytes_accessed=2 * (3 * rows * width + 2 * width * width),
+            transcendentals=0,
+        ),
+        compiler_params=pltpu.CompilerParams(vmem_limit_bytes=VMEM_LIMIT),
+        name="keys_and_values",
+    )(x, weights, weights, bias[:, None])
 
 
 def ffn_kernel(x_ref, w_ref, b_ref, g_ref, slope_ref, *, step):
@@ -1138,9 +1208,6 @@
             for hop in range(seq_parts - 1, 0, -1)
         ]
         far_rows.append(jnp.concatenate(pieces, 0))
-        if b == 0:
-            e_own, far_rows[0] = after((encoder_out, far_rows[0]))
-    e_all = lax.all_gather(e_own, "seq", axis=1, tiled=True).reshape(-1, width)
     key_at = place * T - far + jnp.arange(keys, dtype=jnp.int32)
     self_mark = key_features((key_at >= 0) & (key_at < dec_lengths[:, None]))
     cross_mark = key_features(jnp.arange(keys, dtype=jnp.int32) < enc_lengths[:, None])
@@ -1151,10 +1218,10 @@
     v = (dot("de,rd->er", self_qkv[2], x) + self_bias[1][:, None]).astype(low_type)
     self_inputs, results = [], ()
     for b in range(B):
-        k_far = dot("de,rd->er", self_qkv[1], far_rows[b]).astype(low_type)
-        v_far = (dot("de,rd->er", self_qkv[2], far_rows[b]) + self_bias[1][:, None]).astype(
-            low_type
-        )
+        k_far, v_far = keys_and_values(far_rows[b], self_qkv, self_bias[1])
+        if b == 0:
+            e_own, k_far = after((encoder_out, k_far))
+            e_all = lax.all_gather(e_own, "seq", axis=1, tiled=True).reshape(-1, width)
         self_inputs.append((q, k, v, k_far, v_far, rel, self_mark, table))
         results = self_forward(b, self_inputs[b], results, T, S)
         if b + 1 < B:
@@ -1172,8 +1239,7 @@
     qc = ((dot("de,rd->er", cross_qkv[0], first_low) + cross_bias[0][:, None]) * SCALE).astype(
         low_type
     )
-    kc = dot("de,rd->er", cross_qkv[1], e_all).astype(low_type)
-    vc = (dot("de,rd->er", cross_qkv[2], e_all) + cross_bias[1][:, None]).astype(low_type)
+    kc, vc = keys_and_values(e_all, cross_qkv, cross_bias[1])
     cross_mixed, cross_total = cross_forward(qc, kc, vc, cross_mark)
     second_sum = (
         first_norm
@@ -1199,7 +1265,7 @@
     def over_dp(piece):
         return lax.psum_scatter(piece, "dp", scatter_dimension=0, tiled=True)
 
-    def over_dp_by_steps(piece, meanwhile, beside, later):
+    def over_dp_by_steps(piece, beside_first, first_inputs, beside_second, second_inputs):
         me = lax.axis_index("dp")
 
         def swap(pair, bit):
@@ -1211,12 +1277,17 @@
 
         count = piece.shape[0] // 8
         chip = swap(jnp.swapaxes(piece.reshape(4, 2, count, width), 0, 1), 0)
-        chip, meanwhile = after((chip, meanwhile))
+        chip, first_inputs = after((chip, first_inputs))
         first, second = chip[:, : count // 2], chip[:, count // 2 :]
         first = swap(jnp.swapaxes(first.reshape(2, 2, count // 2, width), 0, 1), 1)
         second = swap(second.reshape(2, 2, count // 2, width), 2)
-        first, second, done, later = after((first, second, beside(meanwhile), later))
-        return jnp.concatenate([swap(first, 2), swap(second, 1)], 0), done, later
+        first, second, done_first, second_inputs = after(
+            (first, second, beside_first(first_inputs), second_inputs)
+        )
+        first, second, done_second = after(
+            (swap(first, 2), swap(second, 1), beside_second((done_first[1], *second_inputs)))
+        )
+        return jnp.concatenate([first, second], 0), done_first, done_second
 
     def over_seq(*pieces):
         cut = [piece.reshape(seq_parts, -1, width) for piece in pieces]
@@ -1330,6 +1401,7 @@
             far_grads, came[b - 1], grad_encoder, ffn_item = after(
                 (far_grads, came[b - 1], grad_encoder, ffn_item)
             )
+            done_ffn_in, done_ffn_out = ffn_steps.send(ffn_item)
         far_columns.append(far_grads)
         away, pieces = give_back(far_grads)
         came.append(pieces)
@@ -1340,7 +1412,6 @@
             for _ in range(seq_parts - 3):
                 ffn_item = ffn_steps.send(ffn_item)
     results[0], away = after((results[0], away))
-    done_ffn_in, done_ffn_out = ffn_steps.send(ffn_item)
     dq, dkv, drel = results
     blocks, size, rel_size = 8 * seq_parts, 3 * width // (8 * seq_parts), width // (16 * seq_parts)
     part_self, part_sums = weight_grads(
@@ -1367,10 +1438,9 @@
         "self_weights",
     )
     part_self, came[-1] = after((part_self, came[-1]))
-    summands = (grad_self, grad_cross, grad_pre, grad_ffn, part_sums, cross_sums)
 
     def near_rows(arrays):
-        dq, came = arrays
+        dq, came, sums = arrays
         moved = jnp.concatenate(
             [functools.reduce(jnp.add, [piece.astype(high_type) for piece in came[b]]) for b in range(B)], 0
         )
@@ -1381,44 +1451,59 @@
             moved,
             S * T,
             "near_rows",
-        )
-
-    mat_self, grad_hidden, (mat_cross_out, mat_cross_qkv, mat_self_out, summands) = over_dp_by_steps(
+        ), sums
+
+    def vector_sums(arrays):
+        sums, part_sums, cross_sums = arrays
+        vectors = [
+            jnp.stack([part_sums[0, :, 0], part_sums[2, :, 0]]),
+            sums[0],
+            part_sums[3, : width // 2, 0],
+            jnp.stack([cross_sums[0, :, 0], cross_sums[2, :, 0]]),
+            sums[1],
+            sums[2],
+            sums[3],
+            jnp.stack([grad_gain_self, grad_gain_cross, grad_gain_ffn]),
+            jnp.stack([grad_shift_self, grad_shift_cross, grad_shift_ffn]),
+        ]
+        blocks = [piece.reshape(seq_parts, -1) for piece in vectors]
+        summed = jnp.concatenate(blocks, 1)
+        for bit in range(3):
+            summed = summed + lax.ppermute(summed, "dp", [(i, i ^ (1 << bit)) for i in range(8)])
+        return summed, [piece.shape[1] for piece in blocks]
+
+    lengths = []
+
+    cross_steps = None
+
+    def second_window(arrays):
+        nonlocal cross_steps
+        cross_steps = over_seq(*arrays[3:])
+        summed, found = vector_sums(arrays[:3])
+        lengths.extend(found)
+        return summed, next(cross_steps)
+
+    part_self, summands = after((part_self, (grad_self, grad_cross, grad_pre, grad_ffn)))
+    sums = [column_sum(summand) for summand in summands]
+    mat_self, (grad_hidden, sums), (summed, cross_item) = over_dp_by_steps(
         part_self.reshape(-1, width),
-        (dq, came),
         near_rows,
-        (mat_cross_out, mat_cross_qkv, mat_self_out, summands),
+        (dq, came, sums),
+        second_window,
+        (part_sums, cross_sums, mat_cross_out, mat_cross_qkv, mat_self_out),
     )
     grad_hidden = grad_hidden.reshape(hidden.shape)
-    grad_self, grad_cross, grad_pre, grad_ffn, part_sums, cross_sums = summands
-    vectors = [
-        jnp.stack([part_sums[0, :, 0], part_sums[2, :, 0]]),
-        column_sum(grad_self),
-        part_sums[3, : width // 2, 0],
-        jnp.stack([cross_sums[0, :, 0], cross_sums[2, :, 0]]),
-        column_sum(grad_cross),
-        column_sum(grad_pre),
-        column_sum(grad_ffn),
-        jnp.stack([grad_gain_self, grad_gain_cross, grad_gain_ffn]),
-        jnp.stack([grad_shift_self, grad_shift_cross, grad_shift_ffn]),
-    ]
-    blocks = [piece.reshape(seq_parts, -1) for piece in vectors]
-    ends = np.cumsum([piece.shape[1] for piece in blocks])
-    summed = jnp.concatenate(blocks, 1)
-    for axis, size_of in (("dp", 8), ("seq", seq_parts)):
-        for bit in range(size_of.bit_length() - 1):
-            summed = summed + lax.ppermute(summed, axis, [(i, i ^ (1 << bit)) for i in range(size_of)])
-    mine = lax.dynamic_index_in_dim(summed, place, 0, keepdims=False)
-    cross_steps = over_seq(mat_cross_out, mat_cross_qkv, mat_self_out)
-    done_cross_out, done_cross_qkv, done_self_out = finish(cross_steps, next(cross_steps))
-    self_steps = over_seq(mat_self)
-    (done_self,) = finish(self_steps, next(self_steps))
+    done_cross_out, done_cross_qkv, done_self_out = finish(cross_steps, cross_item)
+    ends = np.cumsum(lengths)
+    lines = -(-int(ends[-1]) // (16 * width)) * 16
+    summed = jnp.pad(summed, ((0, 0), (0, lines * width - int(ends[-1]))))
+    self_steps = over_seq(mat_self, low(summed))
+    done_self, mine = finish(self_steps, next(self_steps))
     done_self = done_self.reshape(size + rel_size, width)
     done_self_qkv = done_self[:size].reshape(-1)
     half = width // 2
     done_rel = jnp.concatenate([done_self[size:, :half], done_self[size:, half:]], 0).reshape(-1)
-
-    vecs = [mine[end - piece.shape[1] : end] for piece, end in zip(blocks, ends, strict=True)]
+    vecs = [mine[end - count : end] for count, end in zip(lengths, ends, strict=True)]
     return (
         output,
         grad_hidden,

time: 886 us -> 872 us (0.984)
  matrix products: 223 us -> 186 us
  Pallas kernels: 385 us -> 401 us
  starting transfers between devices: 68.5 us -> 57 us
    dot_general x23 -> x17, matrix products: 223 us -> 186 us  [dot(): return jnp.einsum(spec, left, right, preferred_element_type=high_type)]
    pallas_call x6 -> x9, Pallas kernels: 248 us -> 263 us  [the longest x4 134 us: self_call(): pl.pallas_call(by_head(body, group, [SIZE] * 5 + [BUCKETS, None, None] +...]
    ppermute x9, waiting for transfers between devices: 21.1 us -> 35.6 us  [over_seq(): came = (yield lax.ppermute(held.astype(low_type), 'seq', ring))]
  transfers between devices with their start and end apart: 38 -> 36, of which waited for: 12 -> 12; matrix products, arithmetic and copies ran while one was open for 26% -> 26% of each run, Pallas kernels for 33% -> 34%
where the time goes in v4:
time: 872 us; the launch traced here: 862 us
  Pallas kernels  401 us (46%)
  matrix products  186 us (21%)
  waiting for transfers between devices  82.2 us (9%)
  other arithmetic  76.7 us (9%)
  starting transfers between devices  57 us (7%)
  local copies, waits for them, and re-layouts  43.5 us (5%)
  between operations  15.9 us (2%)
    dot_general x17, matrix products, dot(): return jnp.einsum(spec, left, right, preferred_element_type=high_type)  186 us
    pallas_call x4, Pallas kernels, self_call(): pl.pallas_call(by_head(body, group, [SIZE] * 5 + [BUCKETS, None, None] +...  134 us
    pallas_call x1, Pallas kernels, cross_backward(): pl.pallas_call(by_head(cross_backward_kernel, group, [SIZE, SIZE, SIZE, N...  60.6 us
    pallas_call x2, Pallas kernels, weight_grads(): pl.pallas_call(functools.partial(weight_grads_kernel, xs=len(xs), terms=t...  53 us
    pallas_call x4, Pallas kernels, back_rows(): pl.pallas_call(functools.partial(back_rows_kernel, pairs=len(gs), base=ba...  48.9 us
    pallas_call x1, Pallas kernels, cross_forward(): pl.pallas_call(by_head(cross_forward_kernel, group, [SIZE, SIZE, SIZE, No...  39.9 us
    pallas_call x1, Pallas kernels, ffn_first(): pl.pallas_call(functools.partial(ffn_kernel, step=FFN_STEP), grid=(hidden...  36.1 us
    ppermute x9, waiting for transfers between devices, over_seq(): came = (yield lax.ppermute(held.astype(low_type), 'seq', ring))  35.6 us
  transfers between devices with their start and end apart: 36, of which 12 were waited for; matrix products, arithmetic and copies ran while one was open for 26% of the time, Pallas kernels for 34%

profile of v4, /device:TPU:0, one launch (start us, length us, event | category | flops | bytes accessed | tf_op | source)
XLA Modules:
  0.0 862.0 jit_solution(13737298367026056528)
XLA Ops:
  30.9 7.8 convolution_convert_fusion.4.refs_1_
  73.5 7.0 keys_and_values.3
  80.6 26.8 %self_forward.2 = (bf16[1024,1536]{1,0:T(8,128)(2,1)}, f32[2,16,1,768]{3,2,1,0:T(1,128)}) custom-call(bf16[1024,1536]{1,0:T(8,128)(2,1)} %multiply_convert_fusion.2.refs_0_, bf16[1024,1536]{1,0:T(8,128)(2,1)} %convolution_convert_fusion.4.refs_1_, bf16[1024,1536]{1,0:T(8,128)(2,1)} %add_convert_fusion.1.refs_2_, ...), custom_call_target="tpu_custom_call" | custom-call | flops 12884901888 | bytes 14680064 | tf_op jit(solution)/shard_map/self_forward/pallas_call | solution.py:405
  114.4 7.1 keys_and_values.4
  121.5 26.9 %self_forward.3 = (bf16[1024,1536]{1,0:T(8,128)(2,1)}, f32[2,16,1,768]{3,2,1,0:T(1,128)}) custom-call(bf16[1024,1536]{1,0:T(8,128)(2,1)} %multiply_convert_fusion.2.refs_0_, bf16[1024,1536]{1,0:T(8,128)(2,1)} %convolution_convert_fusion.4.refs_1_, bf16[1024,1536]{1,0:T(8,128)(2,1)} %add_convert_fusion.1.refs_2_, ...), custom_call_target="tpu_custom_call", output_to_operand_aliasing={{0}: (8, {}), {1}: (9, {})} | custom-call | flops 12884901888 | bytes 14680064 | tf_op jit(solution)/shard_map/self_forward/pallas_call | solution.py:405
  148.3 7.6 fusion.65
  166.8 14.1 %keys_and_values.5 = (bf16[1024,2048]{1,0:T(8,128)(2,1)}, bf16[1024,2048]{1,0:T(8,128)(2,1)}) custom-call(bf16[2048,1024]{1,0:T(8,128)(2,1)} %bitcast.287, bf16[3,1024,1024]{2,1,0:T(8,128)(2,1)} %refs_3_.3, bf16[3,1024,1024]{2,1,0:T(8,128)(2,1)} %refs_3_.3, f32[1024,1]{1,0:T(8,128)} %copy.53.b_ref), custom_call_target="tpu_custom_call" | custom-call | flops 8589934592 | bytes 16777216 | tf_op jit(solution)/shard_map/keys_and_values/pallas_call | solution.py:550
  181.0 39.9 %cross_forward.1 = (bf16[1024,1536]{1,0:T(8,128)(2,1)}, f32[2,16,1,768]{3,2,1,0:T(1,128)}) custom-call(bf16[1024,1536]{1,0:T(8,128)(2,1)} %fusion.12.refs_0_, bf16[1024,2048]{1,0:T(8,128)(2,1)} %get-tuple-element.141.refs_1_, bf16[1024,2048]{1,0:T(8,128)(2,1)} %get-tuple-element.142.refs_2_, bf16[2,16,1024]{2,1,0:T(8,128)(2,1)} %get-tuple-element.289.refs_3_), custom_call_target="tpu_custom_call" | custom-call | flops 25769803776 | bytes 29360128 | tf_op jit(solution)/shard_map/cross_forward/pallas_call | solution.py:359
  220.9 8.6 %fusion.66 = (f32[1536]{0:T(1024)S(1)}, f32[1536,1024]{1,0:T(8,128)S(1)}) fusion(f32[1024]{0:T(1024)S(1)} %convert_element_type.311, bf16[1024,1536]{1,0:T(8,128)(2,1)} %get-tuple-element.143.refs_4_, bf16[1024,1024]{1,0:T(8,128)(2,1)S(1)} %copy-done, f32[1024]{0:T(1024)S(1)} %bitcast.274, f32[1024]{0:T(1024)S(1)} %bitcast.261, ...), kind=kOutput, calls=%fused_computation.199 | convolution fusion | flops 3232233984 | bytes 17856512 | tf_op jit(solution)/shard_map/er,ed->rd/dot_general | solution.py:617
  233.1 36.1 %ffn_first.1 = (bf16[1536,4096]{1,0:T(8,128)(2,1)}, bf16[1536,4096]{1,0:T(8,128)(2,1)}) custom-call(bf16[1536,1024]{1,0:T(8,128)(2,1)} %fusion.9.x_ref, bf16[1024,4096]{1,0:T(8,128)(2,1)} %w_ref.1, f32[1,4096]{1,0:T(1,128)} %bitcast.279), custom_call_target="tpu_custom_call" | custom-call | flops 12884901888 | bytes 25165824 | tf_op jit(solution)/shard_map/ffn_first/pallas_call | solution.py:590
  269.1 19.7 %fusion.67 = (f32[1536]{0:T(1024)S(1)}, f32[1536,1024]{1,0:T(8,128)S(1)}) fusion(f32[1024]{0:T(1024)S(1)} %convert_element_type.313, bf16[1536,4096]{1,0:T(8,128)(2,1)} %get-tuple-element.144, bf16[4096,1024]{1,0:T(8,128)(2,1)} %param.39, f32[1024]{0:T(1024)S(1)} %bitcast.272, f32[1024]{0:T(1024)S(1)} %bitcast.265, f32[1536]{0:T(1024)S(1)} %add_rsqrt_fusion.1, ...), kind=kOutput, calls=%fused_computation.200 | convolution fusion | flops 12895909888 | bytes 33585152 | tf_op jit(solution)/shard_map/rf,fd->rd/dot_general | solution.py:617
  301.6 15.3 %convolution_convert_fusion.1 = bf16[4096,1024]{1,0:T(8,128)(2,1)} fusion(bf16[1536,4096]{1,0:T(8,128)(2,1)S(1)} %bitcast.290, bf16[1536,1024]{1,0:T(8,128)(2,1)S(1)} %get-tuple-element.199), kind=kOutput, calls=%fused_computation.3 | convolution fusion | flops 12889096192 | bytes 24117248 | tf_op jit(solution)/shard_map/rf,rd->fd/dot_general | solution.py:617
  317.0 21.6 %multiply_convert_fusion = bf16[1536,4096]{1,0:T(8,128)(2,1)} fusion(bf16[1536,4096]{1,0:T(8,128)(2,1)} %get-tuple-element.147, bf16[1536,1024]{1,0:T(8,128)(2,1)} %copy-done.6, bf16[4096,1024]{1,0:T(8,128)(2,1)} %param.39), kind=kOutput, calls=%fused_computation.1 | convolution fusion | flops 12903776256 | bytes 36700160 | tf_op jit(solution)/shard_map/rd,fd->rf/dot_general | solution.py:617
  338.6 19.4 %convolution_convert_fusion = bf16[1024,4096]{1,0:T(8,128)(2,1)} fusion(bf16[1536,1024]{1,0:T(8,128)(2,1)} %fusion.9.x_ref, bf16[1536,4096]{1,0:T(8,128)(2,1)} %multiply_convert_fusion), kind=kOutput, calls=%fused_computation.2 | convolution fusion | flops 12889096192 | bytes 24117248 | tf_op jit(solution)/shard_map/rd,rf->df/dot_general | solution.py:617
  358.0 28.6 %multiply_reduce_fusion = (f32[1024]{0:T(1024)}, f32[1536]{0:T(1024)S(1)}, f32[1536]{0:T(1024)S(1)}, f32[1024]{0:T(1024)}, f32[1536,1024]{1,0:T(8,128)}) fusion(f32[1536,1024]{1,0:T(8,128)} %copy-done.3, f32[1536]{0:T(1024)S(1)} %add_rsqrt_fusion.1, f32[1536]{0:T(1024)S(1)} %broadcast_multiply_fusion.7, f32[1024]{0:T(1024)S(1)} %bitcast.266, ...), kind=kOutput, calls=%fused_computation.17 | convolution fusion | flops 12900625408 | bytes 39882752 | tf_op jit(solution)/shard_map/rf,df->rd/dot_general | solution.py:617
  386.6 8.2 fusion.52
  407.8 60.6 %cross_backward.1 = (bf16[1024,1536]{1,0:T(8,128)(2,1)}, bf16[1024,2048]{1,0:T(8,128)(2,1)}, bf16[1024,2048]{1,0:T(8,128)(2,1)}) custom-call(bf16[1024,1536]{1,0:T(8,128)(2,1)} %fusion.12.refs_0_, bf16[1024,2048]{1,0:T(8,128)(2,1)} %get-tuple-element.141.refs_1_, bf16[1024,2048]{1,0:T(8,128)(2,1)} %get-tuple-element.142.refs_2_, ...), custom_call_target="tpu_custom_call" | custom-call | flops 64424509440 | bytes 73400320 | tf_op jit(solution)/shard_map/cross_backward/pallas_call | solution.py:376
  468.4 28.3 %reduce-scatter.9.cloned.1.call-done = bf16[128,4096]{1,0:T(8,128)(2,1)} async-done(((bf16[1024,4096]{1,0:T(8,128)(2,1)}), bf16[128,4096]{1,0:T(8,128)(2,1)}) %reduce-scatter.9.cloned.1.call-update) | async-done | bytes 1048592 | tf_op jit(solution)/shard_map/reduce_scatter | solution.py:1266
  496.7 14.4 %encoder_rows.1 = bf16[2048,1024]{1,0:T(8,128)(2,1)} custom-call(bf16[1024,2048]{1,0:T(8,128)(2,1)} %get-tuple-element.156.refs_0_.refs_3_, bf16[1024,2048]{1,0:T(8,128)(2,1)} %get-tuple-element.157.refs_1_.refs_4_, bf16[3,1024,1024]{2,1,0:T(8,128)(2,1)} %refs_3_.3, bf16[3,1024,1024]{2,1,0:T(8,128)(2,1)} %refs_3_.3), custom_call_target="tpu_custom_call" | custom-call | flops 8589934592 | bytes 25165824 | tf_op jit(solution)/shard_map/encoder_rows/pallas_call | solution.py:522
  514.0 20.6 %cross_weights.1 = (bf16[8,384,1024]{2,1,0:T(8,128)(2,1)}, f32[3,1024,128]{2,1,0:T(8,128)}) custom-call(bf16[1536,1024]{1,0:T(8,128)(2,1)} %copy-done.12, bf16[2048,1024]{1,0:T(8,128)(2,1)} %bitcast.288, bf16[1024,1536]{1,0:T(8,128)(2,1)} %get-tuple-element.164.refs_2_, bf16[1024,2048]{1,0:T(8,128)(2,1)} %get-tuple-element.156.refs_0_.refs_3_, ...), custom_call_target="tpu_custom_call" | custom-call | flops 11811160064 | bytes 46137344 | tf_op jit(solution)/shard_map/cross_weights/pallas_call | solution.py:481
  539.3 11.5 %multiply_reduce_fusion.1 = (f32[1024]{0:T(1024)S(1)}, f32[1536]{0:T(1024)S(1)}, f32[1536]{0:T(1024)S(1)}, f32[1024]{0:T(1024)S(1)}, f32[1536,1024]{1,0:T(8,128)S(1)}) fusion(f32[1536,1024]{1,0:T(8,128)} %copy-done.2, f32[1536]{0:T(1024)S(1)} %copy-done.23, f32[1536]{0:T(1024)S(1)} %copy-done.21, f32[1024]{0:T(1024)S(1)} %bitcast.262, ...), kind=kOutput, calls=%fused_computation.18 | convolution fusion | flops 3236948992 | bytes 24154112 | tf_op jit(solution)/shard_map/er,de->rd/dot_general | solution.py:617
  562.7 7.6 fusion.11.refs_10_
  570.4 40.3 %self_backward.2 = (bf16[1024,1536]{1,0:T(8,128)(2,1)}, bf16[2,1024,1536]{2,1,0:T(8,128)(2,1)}, bf16[512,1536]{1,0:T(8,128)(2,1)}, bf16[2,1024,768]{2,1,0:T(8,128)(2,1)}) custom-call(bf16[1024,1536]{1,0:T(8,128)(2,1)} %multiply_convert_fusion.2.refs_0_, bf16[1024,1536]{1,0:T(8,128)(2,1)} %convolution_convert_fusion.4.refs_1_, ...), custom_call_target="tpu_custom_call" | custom-call | flops 32212254720 | bytes 36700160 | tf_op jit(solution)/shard_map/self_backward/pallas_call | solution.py:405
  610.7 7.2 far_rows.2
  629.3 40.0 %self_backward.3 = (bf16[1024,1536]{1,0:T(8,128)(2,1)}, bf16[2,1024,1536]{2,1,0:T(8,128)(2,1)}, bf16[512,1536]{1,0:T(8,128)(2,1)}, bf16[2,1024,768]{2,1,0:T(8,128)(2,1)}) custom-call(bf16[1024,1536]{1,0:T(8,128)(2,1)} %multiply_convert_fusion.2.refs_0_, ...), custom_call_target="tpu_custom_call", output_to_operand_aliasing={{0}: (11, {}), {1}: (12, {}), {2}: (13, {})} | custom-call | flops 32212254720 | bytes 36700160 | tf_op jit(solution)/shard_map/self_backward/pallas_call | solution.py:405
  669.4 7.4 far_rows.3
  682.2 32.4 %self_weights.1 = (bf16[32,112,1024]{2,1,0:T(8,128)(2,1)}, f32[4,1024,128]{2,1,0:T(8,128)}) custom-call(bf16[1536,1024]{1,0:T(8,128)(2,1)} %bitcast.244, bf16[768,1024]{1,0:T(8,128)(2,1)} %pad_maximum_fusion.1.x_ref.refs_1_, bf16[768,1024]{1,0:T(8,128)(2,1)} %pad_maximum_fusion.2.x_ref.refs_2_, bf16[1024,1536]{1,0:T(8,128)(2,1)} %get-tuple-element.201.refs_3_.refs_0_, ...), custom_call_target="tpu_custom_call" | custom-call | flops 19327352832 | bytes 75497472 | tf_op jit(solution)/shard_map/self_weights/pallas_call | solution.py:481
  746.8 19.9 %near_rows.1 = bf16[1536,1024]{1,0:T(8,128)(2,1)} custom-call(bf16[1024,1536]{1,0:T(8,128)(2,1)} %get-tuple-element.201.refs_3_.refs_0_, bf16[2,1024,1536]{2,1,0:T(8,128)(2,1)} %get-tuple-element.185.refs_4_.refs_5_.refs_1_.refs_2_, bf16[2,1024,1536]{2,1,0:T(8,128)(2,1)} %get-tuple-element.185.refs_4_.refs_5_.refs_1_.refs_2_, ...), custom_call_target="tpu_custom_call" | custom-call | flops 11274289152 | bytes 27787264 | tf_op jit(solution)/shard_map/near_rows/pallas_call | solution.py:522
  788.7 7.5 collective-permute-done.21
  798.0 8.4 collective-permute-start.23
  807.9 8.4 collective-permute-done.23
  818.3 9.3 %collective-permute-done.24 = bf16[128,1024]{1,0:T(8,128)(2,1)S(1)} collective-permute-done((bf16[128,1024]{1,0:T(8,128)(2,1)S(1)}, bf16[128,1024]{1,0:T(8,128)(2,1)S(1)}, u32[]{:S(2)}, u32[]{:S(2)}) %collective-permute-start.24) | collective-permute-done | bytes 262176 | tf_op jit(solution)/shard_map/ppermute | solution.py:1304
  (313 shorter events, 227.7 us)
Async XLA Ops:
  7.2 159.6 %all-gather.2.cloned.1.call-start = ((), (), s32[]{:S(2)}) async-start(), calls=%async_computation.6 | async-start | bytes 5242880 | tf_op jit(solution)/shard_map/all_gather | solution.py:1224
  9.6 49.1 %collective-permute-start.2 = (bf16[256,1024]{1,0:T(8,128)(2,1)}, bf16[256,1024]{1,0:T(8,128)(2,1)}, u32[]{:S(2)}, u32[]{:S(2)}) collective-permute-start(bf16[256,1024]{1,0:T(8,128)(2,1)} %get-tuple-element.260), channel_id=1, source_target_pairs={{0,1},{1,2},{2,3},{4,5},{5,6},{6,7},{8,9},{9,10},{10,11},{12,13},{... | collective-permute-start | bytes 1572872 | tf_op jit(solution)/shard_map/ppermute | solution.py:1207
  15.4 43.4 %collective-permute-start.1 = (bf16[256,1024]{1,0:T(8,128)(2,1)}, bf16[256,1024]{1,0:T(8,128)(2,1)}, u32[]{:S(2)}, u32[]{:S(2)}) collective-permute-start(bf16[256,1024]{1,0:T(8,128)(2,1)} %get-tuple-element.260), channel_id=1, source_target_pairs={{0,2},{1,3},{4,6},{5,7},{8,10},{9,11},{12,14},{13,15},{16,18},{17,... | collective-permute-start | bytes 1572872 | tf_op jit(solution)/shard_map/ppermute | solution.py:1207
  19.9 38.9 %collective-permute-start = (bf16[256,1024]{1,0:T(8,128)(2,1)}, bf16[256,1024]{1,0:T(8,128)(2,1)}, u32[]{:S(2)}, u32[]{:S(2)}) collective-permute-start(bf16[256,1024]{1,0:T(8,128)(2,1)} %get-tuple-element.260), channel_id=1, source_target_pairs={{0,3},{4,7},{8,11},{12,15},{16,19},{20,23},{24,27},{28,31}} | collective-permute-start | bytes 1572872 | tf_op jit(solution)/shard_map/ppermute | solution.py:1207
  61.4 46.1 %collective-permute-start.5 = (bf16[256,1024]{1,0:T(8,128)(2,1)}, bf16[256,1024]{1,0:T(8,128)(2,1)S(1)}, u32[]{:S(2)}, u32[]{:S(2)}) collective-permute-start(bf16[256,1024]{1,0:T(8,128)(2,1)} %get-tuple-element.127), channel_id=1, source_target_pairs={{0,1},{1,2},{2,3},{4,5},{5,6},{6,7},{8,9},{9,10},{10,11},{12,13},{... | collective-permute-start | bytes 1572872 | tf_op jit(solution)/shard_map/ppermute | solution.py:1207
  65.9 41.6 %collective-permute-start.4 = (bf16[256,1024]{1,0:T(8,128)(2,1)}, bf16[256,1024]{1,0:T(8,128)(2,1)S(1)}, u32[]{:S(2)}, u32[]{:S(2)}) collective-permute-start(bf16[256,1024]{1,0:T(8,128)(2,1)} %get-tuple-element.127), channel_id=1, source_target_pairs={{0,2},{1,3},{4,6},{5,7},{8,10},{9,11},{12,14},{13,15},{16,18},{17,... | collective-permute-start | bytes 1572872 | tf_op jit(solution)/shard_map/ppermute | solution.py:1207
  71.2 40.9 %collective-permute-start.3 = (bf16[256,1024]{1,0:T(8,128)(2,1)}, bf16[256,1024]{1,0:T(8,128)(2,1)}, u32[]{:S(2)}, u32[]{:S(2)}) collective-permute-start(bf16[256,1024]{1,0:T(8,128)(2,1)} %get-tuple-element.127), channel_id=1, source_target_pairs={{0,3},{4,7},{8,11},{12,15},{16,19},{20,23},{24,27},{28,31}} | collective-permute-start | bytes 1572872 | tf_op jit(solution)/shard_map/ppermute | solution.py:1207
  80.6 387.8 %reduce-scatter.7.cloned.1.call-start = ((), (), s32[]{:S(2)}) async-start(), calls=%async_computation.7 | async-start | bytes 9437184 | tf_op jit(solution)/shard_map/reduce_scatter | solution.py:1266
  316.9 179.8 %reduce-scatter.9.cloned.1.call-start = ((), (), s32[]{:S(2)}) async-start(), calls=%async_computation.8 | async-start | bytes 9437184 | tf_op jit(solution)/shard_map/reduce_scatter | solution.py:1266
  358.0 311.4 %reduce-scatter.11.cloned.1.call-start = ((), (), s32[]{:S(2)}) async-start(), calls=%async_computation.9 | async-start | bytes 5242880 | tf_op jit(solution)/shard_map/reduce_scatter | solution.py:1341
  511.2 265.8 %reduce-scatter.13.cloned.1.call-start = ((), (), s32[]{:S(2)}) async-start(), calls=%async_computation.10 | async-start | bytes 2359296 | tf_op jit(solution)/shard_map/reduce_scatter | solution.py:1266
  512.4 22.3 %collective-permute-start.6 = (bf16[256,1024]{1,0:T(8,128)(2,1)S(1)}, bf16[256,1024]{1,0:T(8,128)(2,1)S(1)}, u32[]{:S(2)}, u32[]{:S(2)}) collective-permute-start(bf16[256,1024]{1,0:T(8,128)(2,1)S(1)} %fusion.34), channel_id=1, source_target_pairs={{0,1},{1,2},{2,3},{3,0},{4,5},{5,6},{6,7},{7,4},{8,9},{9,10},{10,1... | collective-permute-start | bytes 1572872 | tf_op jit(solution)/shard_map/ppermute | solution.py:1304
  534.6 242.3 %reduce-scatter.17.cloned.1.call-start = ((), (), s32[]{:S(2)}) async-start(), calls=%async_computation.12 | async-start | bytes 2359296 | tf_op jit(solution)/shard_map/reduce_scatter | solution.py:1266
  535.7 88.7 %collective-permute-start.7 = (bf16[256,1024]{1,0:T(8,128)(2,1)}, bf16[256,1024]{1,0:T(8,128)(2,1)}, u32[]{:S(2)}, u32[]{:S(2)}) collective-permute-start(bf16[256,1024]{1,0:T(8,128)(2,1)} %fusion.26), channel_id=1, source_target_pairs={{0,1},{1,2},{2,3},{3,0},{4,5},{5,6},{6,7},{7,4},{8,9},{9,10},{10,1... | collective-permute-start | bytes 1572872 | tf_op jit(solution)/shard_map/ppermute | solution.py:1304
  570.4 206.5 %reduce-scatter.15.cloned.1.call-start = ((), (), s32[]{:S(2)}) async-start(), calls=%async_computation.11 | async-start | bytes 7077888 | tf_op jit(solution)/shard_map/reduce_scatter | solution.py:1266
  620.5 48.8 %collective-permute-start.10 = (bf16[256,1024]{1,0:T(8,128)(2,1)}, bf16[256,1024]{1,0:T(8,128)(2,1)S(1)}, u32[]{:S(2)}, u32[]{:S(2)}) collective-permute-start(bf16[256,1024]{1,0:T(8,128)(2,1)} %get-tuple-element.265), channel_id=1, source_target_pairs={{3,0},{7,4},{11,8},{15,12},{19,16},{23,20},{27,24},{31,28}} | collective-permute-start | bytes 1572872 | tf_op jit(solution)/shard_map/ppermute | solution.py:1387
  621.8 47.6 %collective-permute-start.9 = (bf16[256,1024]{1,0:T(8,128)(2,1)}, bf16[256,1024]{1,0:T(8,128)(2,1)S(1)}, u32[]{:S(2)}, u32[]{:S(2)}) collective-permute-start(bf16[256,1024]{1,0:T(8,128)(2,1)} %get-tuple-element.266), channel_id=1, source_target_pairs={{2,0},{3,1},{6,4},{7,5},{10,8},{11,9},{14,12},{15,13},{18,16},{19,... | collective-permute-start | bytes 1572872 | tf_op jit(solution)/shard_map/ppermute | solution.py:1387
  623.1 46.3 %collective-permute-start.8 = (bf16[256,1024]{1,0:T(8,128)(2,1)}, bf16[256,1024]{1,0:T(8,128)(2,1)}, u32[]{:S(2)}, u32[]{:S(2)}) collective-permute-start(bf16[256,1024]{1,0:T(8,128)(2,1)} %get-tuple-element.267), channel_id=1, source_target_pairs={{1,0},{2,1},{3,2},{5,4},{6,5},{7,6},{9,8},{10,9},{11,10},{13,12},{... | collective-permute-start | bytes 1572872 | tf_op jit(solution)/shard_map/ppermute | solution.py:1387
  625.7 43.7 %collective-permute-start.11 = (bf16[256,1024]{1,0:T(8,128)(2,1)S(1)}, bf16[256,1024]{1,0:T(8,128)(2,1)}, u32[]{:S(2)}, u32[]{:S(2)}) collective-permute-start(bf16[256,1024]{1,0:T(8,128)(2,1)S(1)} %fusion.25), channel_id=1, source_target_pairs={{0,1},{1,2},{2,3},{3,0},{4,5},{5,6},{6,7},{7,4},{8,9},{9,10},{10,1... | collective-permute-start | bytes 1572872 | tf_op jit(solution)/shard_map/ppermute | solution.py:1304
  678.3 36.3 %collective-permute-start.14 = (bf16[256,1024]{1,0:T(8,128)(2,1)S(1)}, bf16[256,1024]{1,0:T(8,128)(2,1)}, u32[]{:S(2)}, u32[]{:S(2)}) collective-permute-start(bf16[256,1024]{1,0:T(8,128)(2,1)S(1)} %get-tuple-element.262), channel_id=1, source_target_pairs={{3,0},{7,4},{11,8},{15,12},{19,16},{23,20},{27,24},{31,28}} | collective-permute-start | bytes 1572872 | tf_op jit(solution)/shard_map/ppermute | solution.py:1387
  679.6 36.0 %collective-permute-start.13 = (bf16[256,1024]{1,0:T(8,128)(2,1)S(1)}, bf16[256,1024]{1,0:T(8,128)(2,1)}, u32[]{:S(2)}, u32[]{:S(2)}) collective-permute-start(bf16[256,1024]{1,0:T(8,128)(2,1)S(1)} %get-tuple-element.263), channel_id=1, source_target_pairs={{2,0},{3,1},{6,4},{7,5},{10,8},{11,9},{14,12},{15,13},{18,16},{19,... | collective-permute-start | bytes 1572872 | tf_op jit(solution)/shard_map/ppermute | solution.py:1387
  680.9 34.7 %collective-permute-start.12 = (bf16[256,1024]{1,0:T(8,128)(2,1)S(1)}, bf16[256,1024]{1,0:T(8,128)(2,1)}, u32[]{:S(2)}, u32[]{:S(2)}) collective-permute-start(bf16[256,1024]{1,0:T(8,128)(2,1)S(1)} %get-tuple-element.264), channel_id=1, source_target_pairs={{1,0},{2,1},{3,2},{5,4},{6,5},{7,6},{9,8},{10,9},{11,10},{13,12},{... | collective-permute-start | bytes 1572872 | tf_op jit(solution)/shard_map/ppermute | solution.py:1387
  719.8 13.7 %collective-permute-start.15 = (bf16[4,448,1024]{2,1,0:T(8,128)(2,1)}, bf16[4,448,1024]{2,1,0:T(8,128)(2,1)}, u32[]{:S(2)}, u32[]{:S(2)}) collective-permute-start(bf16[4,448,1024]{2,1,0:T(8,128)(2,1)} %dynamic-slice_bitcast_fusion), channel_id=1, source_target_pairs={{0,4},{4,0},{8,12},{12,8},{16,20},{20,16},{24,28},{28,24},{1,5},{5... | collective-permute-start | bytes 11010056 | tf_op jit(solution)/shard_map/ppermute | solution.py:1275
  740.2 31.4 %collective-permute-start.17 = (bf16[2,224,1024]{2,1,0:T(8,128)(2,1)}, bf16[2,224,1024]{2,1,0:T(8,128)(2,1)}, u32[]{:S(2)}, u32[]{:S(2)}) collective-permute-start(bf16[2,224,1024]{2,1,0:T(8,128)(2,1)} %dynamic-slice_bitcast_fusion.1), channel_id=1, source_target_pairs={{0,16},{4,20},{8,24},{12,28},{16,0},{20,4},{24,8},{28,12},{1,17},{... | collective-permute-start | bytes 2752520 | tf_op jit(solution)/shard_map/ppermute | solution.py:1275
  742.3 32.1 %collective-permute-start.16 = (bf16[2,224,1024]{2,1,0:T(8,128)(2,1)}, bf16[2,224,1024]{2,1,0:T(8,128)(2,1)}, u32[]{:S(2)}, u32[]{:S(2)}) collective-permute-start(bf16[2,224,1024]{2,1,0:T(8,128)(2,1)} %dynamic-slice_bitcast_fusion.2), channel_id=1, source_target_pairs={{0,8},{4,12},{8,0},{12,4},{16,24},{20,28},{24,16},{28,20},{1,9},{5... | collective-permute-start | bytes 2752520 | tf_op jit(solution)/shard_map/ppermute | solution.py:1275
  782.4 24.1 %collective-permute-start.19 = (bf16[224,1024]{1,0:T(8,128)(2,1)S(1)}, bf16[224,1024]{1,0:T(8,128)(2,1)S(1)}, u32[]{:S(2)}, u32[]{:S(2)}) collective-permute-start(bf16[224,1024]{1,0:T(8,128)(2,1)S(1)} %dynamic-slice_bitcast_fusion.3), channel_id=1, source_target_pairs={{0,8},{4,12},{8,0},{12,4},{16,24},{20,28},{24,16},{28,20},{1,9},{5... | collective-permute-start | bytes 1376264 | tf_op jit(solution)/shard_map/ppermute | solution.py:1275
  785.2 22.5 %collective-permute-start.18 = (bf16[224,1024]{1,0:T(8,128)(2,1)S(1)}, bf16[224,1024]{1,0:T(8,128)(2,1)S(1)}, u32[]{:S(2)}, u32[]{:S(2)}) collective-permute-start(bf16[224,1024]{1,0:T(8,128)(2,1)S(1)} %dynamic-slice_bitcast_fusion.4), channel_id=1, source_target_pairs={{0,16},{4,20},{8,24},{12,28},{16,0},{20,4},{24,8},{28,12},{1,17},{... | collective-permute-start | bytes 1376264 | tf_op jit(solution)/shard_map/ppermute | solution.py:1275
  798.0 18.3 %collective-permute-start.23 = (bf16[160,1024]{1,0:T(8,128)(2,1)S(1)}, bf16[160,1024]{1,0:T(8,128)(2,1)S(1)}, u32[]{:S(2)}, u32[]{:S(2)}) collective-permute-start(bf16[160,1024]{1,0:T(8,128)(2,1)S(1)} %dynamic-slice_bitcast_fusion.5), channel_id=1, source_target_pairs={{0,1},{1,2},{2,3},{3,0},{4,5},{5,6},{6,7},{7,4},{8,9},{9,10},{10,1... | collective-permute-start | bytes 983048 | tf_op jit(solution)/shard_map/ppermute | solution.py:1304
  816.5 11.1 %collective-permute-start.24 = (bf16[128,1024]{1,0:T(8,128)(2,1)S(1)}, bf16[128,1024]{1,0:T(8,128)(2,1)S(1)}, u32[]{:S(2)}, u32[]{:S(2)}) collective-permute-start(bf16[128,1024]{1,0:T(8,128)(2,1)S(1)} %fusion.44), channel_id=1, source_target_pairs={{0,1},{1,2},{2,3},{3,0},{4,5},{5,6},{6,7},{7,4},{8,9},{9,10},{10,1... | collective-permute-start | bytes 786440 | tf_op jit(solution)/shard_map/ppermute | solution.py:1304
  816.7 17.9 %collective-permute-start.27 = (bf16[160,1024]{1,0:T(8,128)(2,1)S(1)}, bf16[160,1024]{1,0:T(8,128)(2,1)S(1)}, u32[]{:S(2)}, u32[]{:S(2)}) collective-permute-start(bf16[160,1024]{1,0:T(8,128)(2,1)S(1)} %fusion.30), channel_id=1, source_target_pairs={{0,1},{1,2},{2,3},{3,0},{4,5},{5,6},{6,7},{7,4},{8,9},{9,10},{10,1... | collective-permute-start | bytes 983048 | tf_op jit(solution)/shard_map/ppermute | solution.py:1304
  827.7 12.6 %collective-permute-start.25 = (bf16[128,1024]{1,0:T(8,128)(2,1)S(1)}, bf16[128,1024]{1,0:T(8,128)(2,1)S(1)}, u32[]{:S(2)}, u32[]{:S(2)}) collective-permute-start(bf16[128,1024]{1,0:T(8,128)(2,1)S(1)} %fusion.40), channel_id=1, source_target_pairs={{0,1},{1,2},{2,3},{3,0},{4,5},{5,6},{6,7},{7,4},{8,9},{9,10},{10,1... | collective-permute-start | bytes 786440 | tf_op jit(solution)/shard_map/ppermute | solution.py:1304
  834.7 12.5 %collective-permute-start.28 = (bf16[160,1024]{1,0:T(8,128)(2,1)S(1)}, bf16[160,1024]{1,0:T(8,128)(2,1)S(1)}, u32[]{:S(2)}, u32[]{:S(2)}) collective-permute-start(bf16[160,1024]{1,0:T(8,128)(2,1)S(1)} %fusion.29), channel_id=1, source_target_pairs={{0,1},{1,2},{2,3},{3,0},{4,5},{5,6},{6,7},{7,4},{8,9},{9,10},{10,1... | collective-permute-start | bytes 983048 | tf_op jit(solution)/shard_map/ppermute | solution.py:1304
  (53 other events, 932.3 us)
Sparse Core Ops, SparseCore 0:
  80.7 86.0 all-gather.1
  317.0 104.4 reduce-scatter.6
  425.4 71.2 reduce-scatter.8
  511.3 96.6 reduce-scatter.10
  611.4 39.7 reduce-scatter.12
  654.4 41.2 reduce-scatter.16
  699.4 70.2 reduce-scatter.14

commit v5 on v4

--- a/solution.py
+++ b/solution.py
@@ -1440,7 +1440,7 @@
     part_self, came[-1] = after((part_self, came[-1]))
 
     def near_rows(arrays):
-        dq, came, sums = arrays
+        dq, came = arrays
         moved = jnp.concatenate(
             [functools.reduce(jnp.add, [piece.astype(high_type) for piece in came[b]]) for b in range(B)], 0
         )
@@ -1451,7 +1451,9 @@
             moved,
             S * T,
             "near_rows",
-        ), sums
+        )
+
+    lengths = []
 
     def vector_sums(arrays):
         sums, part_sums, cross_sums = arrays
@@ -1467,30 +1469,30 @@
             jnp.stack([grad_shift_self, grad_shift_cross, grad_shift_ffn]),
         ]
         blocks = [piece.reshape(seq_parts, -1) for piece in vectors]
-        summed = jnp.concatenate(blocks, 1)
-        for bit in range(3):
-            summed = summed + lax.ppermute(summed, "dp", [(i, i ^ (1 << bit)) for i in range(8)])
-        return summed, [piece.shape[1] for piece in blocks]
-
-    lengths = []
+        lengths.extend(piece.shape[1] for piece in blocks)
+        return pairwise(jnp.concatenate(blocks, 1), 0)
+
+    def pairwise(value, bit):
+        return value + lax.ppermute(value, "dp", [(i, i ^ (1 << bit)) for i in range(8)])
 
     cross_steps = None
 
     def second_window(arrays):
         nonlocal cross_steps
-        cross_steps = over_seq(*arrays[3:])
-        summed, found = vector_sums(arrays[:3])
-        lengths.extend(found)
-        return summed, next(cross_steps)
+        cross_steps = over_seq(*arrays[1:])
+        return pairwise(pairwise(arrays[0], 1), 2), next(cross_steps)
 
     part_self, summands = after((part_self, (grad_self, grad_cross, grad_pre, grad_ffn)))
     sums = [column_sum(summand) for summand in summands]
-    mat_self, (grad_hidden, sums), (summed, cross_item) = over_dp_by_steps(
+    def first_window(arrays):
+        return near_rows(arrays[:2]), vector_sums(arrays[2:])
+
+    mat_self, (grad_hidden, _), (summed, cross_item) = over_dp_by_steps(
         part_self.reshape(-1, width),
-        near_rows,
-        (dq, came, sums),
+        first_window,
+        (dq, came, sums, part_sums, cross_sums),
         second_window,
-        (part_sums, cross_sums, mat_cross_out, mat_cross_qkv, mat_self_out),
+        (mat_cross_out, mat_cross_qkv, mat_self_out),
     )
     grad_hidden = grad_hidden.reshape(hidden.shape)
     done_cross_out, done_cross_qkv, done_self_out = finish(cross_steps, cross_item)

time: 872 us -> 877 us (level)
  transfers between devices with their start and end apart: 36 -> 36, of which waited for: 12 -> 11; matrix products, arithmetic and copies ran while one was open for 26% -> 27% of each run, Pallas kernels for 34% -> 34%
where the time goes in v5:
time: 877 us; the launch traced here: 866 us
  Pallas kernels  400 us (46%)
  matrix products  186 us (21%)
  waiting for transfers between devices  81.1 us (9%)
  other arithmetic  79.3 us (9%)
  starting transfers between devices  58.4 us (7%)
  local copies, waits for them, and re-layouts  45.3 us (5%)
  between operations  15.9 us (2%)
    dot_general x17, matrix products, dot(): return jnp.einsum(spec, left, right, preferred_element_type=high_type)  186 us
    pallas_call x4, Pallas kernels, self_call(): pl.pallas_call(by_head(body, group, [SIZE] * 5 + [BUCKETS, None, None] +...  134 us
    pallas_call x1, Pallas kernels, cross_backward(): pl.pallas_call(by_head(cross_backward_kernel, group, [SIZE, SIZE, SIZE, N...  60.6 us
    pallas_call x2, Pallas kernels, weight_grads(): pl.pallas_call(functools.partial(weight_grads_kernel, xs=len(xs), terms=t...  52.9 us
    pallas_call x4, Pallas kernels, back_rows(): pl.pallas_call(functools.partial(back_rows_kernel, pairs=len(gs), base=ba...  48.4 us
    pallas_call x1, Pallas kernels, cross_forward(): pl.pallas_call(by_head(cross_forward_kernel, group, [SIZE, SIZE, SIZE, No...  39.9 us
    pallas_call x1, Pallas kernels, ffn_first(): pl.pallas_call(functools.partial(ffn_kernel, step=FFN_STEP), grid=(hidden...  36.1 us
    ppermute x9, waiting for transfers between devices, over_seq(): came = (yield lax.ppermute(held.astype(low_type), 'seq', ring))  35.6 us
  transfers between devices with their start and end apart: 36, of which 11 were waited for; matrix products, arithmetic and copies ran while one was open for 27% of the time, Pallas kernels for 34%

profile of v5, /device:TPU:0, one launch (start us, length us, event | category | flops | bytes accessed | tf_op | source)
XLA Modules:
  0.0 866.3 jit_solution(10247873589487624104)
XLA Ops:
  30.8 7.8 convolution_convert_fusion.4.refs_1_
  80.6 26.8 %self_forward.2 = (bf16[1024,1536]{1,0:T(8,128)(2,1)}, f32[2,16,1,768]{3,2,1,0:T(1,128)}) custom-call(bf16[1024,1536]{1,0:T(8,128)(2,1)} %multiply_convert_fusion.2.refs_0_, bf16[1024,1536]{1,0:T(8,128)(2,1)} %convolution_convert_fusion.4.refs_1_, bf16[1024,1536]{1,0:T(8,128)(2,1)} %add_convert_fusion.1.refs_2_, ...), custom_call_target="tpu_custom_call" | custom-call | flops 12884901888 | bytes 14680064 | tf_op jit(solution)/shard_map/self_forward/pallas_call | solution.py:405
  114.4 7.1 keys_and_values.4
  121.5 26.9 %self_forward.3 = (bf16[1024,1536]{1,0:T(8,128)(2,1)}, f32[2,16,1,768]{3,2,1,0:T(1,128)}) custom-call(bf16[1024,1536]{1,0:T(8,128)(2,1)} %multiply_convert_fusion.2.refs_0_, bf16[1024,1536]{1,0:T(8,128)(2,1)} %convolution_convert_fusion.4.refs_1_, bf16[1024,1536]{1,0:T(8,128)(2,1)} %add_convert_fusion.1.refs_2_, ...), custom_call_target="tpu_custom_call", output_to_operand_aliasing={{0}: (8, {}), {1}: (9, {})} | custom-call | flops 12884901888 | bytes 14680064 | tf_op jit(solution)/shard_map/self_forward/pallas_call | solution.py:405
  148.3 7.6 fusion.65
  166.8 14.1 %keys_and_values.5 = (bf16[1024,2048]{1,0:T(8,128)(2,1)}, bf16[1024,2048]{1,0:T(8,128)(2,1)}) custom-call(bf16[2048,1024]{1,0:T(8,128)(2,1)} %bitcast.287, bf16[3,1024,1024]{2,1,0:T(8,128)(2,1)} %refs_3_.3, bf16[3,1024,1024]{2,1,0:T(8,128)(2,1)} %refs_3_.3, f32[1024,1]{1,0:T(8,128)} %copy.53.b_ref), custom_call_target="tpu_custom_call" | custom-call | flops 8589934592 | bytes 16777216 | tf_op jit(solution)/shard_map/keys_and_values/pallas_call | solution.py:550
  180.9 39.9 %cross_forward.1 = (bf16[1024,1536]{1,0:T(8,128)(2,1)}, f32[2,16,1,768]{3,2,1,0:T(1,128)}) custom-call(bf16[1024,1536]{1,0:T(8,128)(2,1)} %fusion.12.refs_0_, bf16[1024,2048]{1,0:T(8,128)(2,1)} %get-tuple-element.138.refs_1_, bf16[1024,2048]{1,0:T(8,128)(2,1)} %get-tuple-element.139.refs_2_, bf16[2,16,1024]{2,1,0:T(8,128)(2,1)} %get-tuple-element.283.refs_3_), custom_call_target="tpu_custom_call" | custom-call | flops 25769803776 | bytes 29360128 | tf_op jit(solution)/shard_map/cross_forward/pallas_call | solution.py:359
  220.9 8.6 fusion.66
  233.1 36.1 %ffn_first.1 = (bf16[1536,4096]{1,0:T(8,128)(2,1)}, bf16[1536,4096]{1,0:T(8,128)(2,1)}) custom-call(bf16[1536,1024]{1,0:T(8,128)(2,1)} %fusion.9.x_ref, bf16[1024,4096]{1,0:T(8,128)(2,1)} %w_ref.1, f32[1,4096]{1,0:T(1,128)} %bitcast.279), custom_call_target="tpu_custom_call" | custom-call | flops 12884901888 | bytes 25165824 | tf_op jit(solution)/shard_map/ffn_first/pallas_call | solution.py:590
  269.2 19.7 %fusion.67 = (f32[1536]{0:T(1024)S(1)}, f32[1536,1024]{1,0:T(8,128)S(1)}) fusion(f32[1024]{0:T(1024)S(1)} %convert_element_type.313, bf16[1536,4096]{1,0:T(8,128)(2,1)} %get-tuple-element.141, bf16[4096,1024]{1,0:T(8,128)(2,1)} %param.39, f32[1024]{0:T(1024)S(1)} %bitcast.272, f32[1024]{0:T(1024)S(1)} %bitcast.265, f32[1536]{0:T(1024)S(1)} %add_rsqrt_fusion.1, ...), kind=kOutput, calls=%fused_computation.200 | convolution fusion | flops 12895909888 | bytes 33585152 | tf_op jit(solution)/shard_map/rf,fd->rd/dot_general | solution.py:617
  301.6 15.3 %convolution_convert_fusion.1 = bf16[4096,1024]{1,0:T(8,128)(2,1)} fusion(bf16[1536,4096]{1,0:T(8,128)(2,1)S(1)} %bitcast.290, bf16[1536,1024]{1,0:T(8,128)(2,1)S(1)} %get-tuple-element.196), kind=kOutput, calls=%fused_computation.3 | convolution fusion | flops 12889096192 | bytes 24117248 | tf_op jit(solution)/shard_map/rf,rd->fd/dot_general | solution.py:617
  317.0 21.6 %multiply_convert_fusion = bf16[1536,4096]{1,0:T(8,128)(2,1)} fusion(bf16[1536,4096]{1,0:T(8,128)(2,1)} %get-tuple-element.144, bf16[1536,1024]{1,0:T(8,128)(2,1)} %copy-done.6, bf16[4096,1024]{1,0:T(8,128)(2,1)} %param.39), kind=kOutput, calls=%fused_computation.1 | convolution fusion | flops 12903776256 | bytes 36700160 | tf_op jit(solution)/shard_map/rd,fd->rf/dot_general | solution.py:617
  338.6 19.3 %convolution_convert_fusion = bf16[1024,4096]{1,0:T(8,128)(2,1)} fusion(bf16[1536,1024]{1,0:T(8,128)(2,1)} %fusion.9.x_ref, bf16[1536,4096]{1,0:T(8,128)(2,1)} %multiply_convert_fusion), kind=kOutput, calls=%fused_computation.2 | convolution fusion | flops 12889096192 | bytes 24117248 | tf_op jit(solution)/shard_map/rd,rf->df/dot_general | solution.py:617
  358.0 28.7 %multiply_reduce_fusion = (f32[1024]{0:T(1024)}, f32[1536]{0:T(1024)S(1)}, f32[1536]{0:T(1024)S(1)}, f32[1024]{0:T(1024)}, f32[1536,1024]{1,0:T(8,128)}) fusion(f32[1536,1024]{1,0:T(8,128)} %copy-done.3, f32[1536]{0:T(1024)S(1)} %add_rsqrt_fusion.1, f32[1536]{0:T(1024)S(1)} %broadcast_multiply_fusion.7, f32[1024]{0:T(1024)S(1)} %bitcast.266, ...), kind=kOutput, calls=%fused_computation.17 | convolution fusion | flops 12900625408 | bytes 39882752 | tf_op jit(solution)/shard_map/rf,df->rd/dot_general | solution.py:617
  386.6 8.2 fusion.52
  407.8 60.6 %cross_backward.1 = (bf16[1024,1536]{1,0:T(8,128)(2,1)}, bf16[1024,2048]{1,0:T(8,128)(2,1)}, bf16[1024,2048]{1,0:T(8,128)(2,1)}) custom-call(bf16[1024,1536]{1,0:T(8,128)(2,1)} %fusion.12.refs_0_, bf16[1024,2048]{1,0:T(8,128)(2,1)} %get-tuple-element.138.refs_1_, bf16[1024,2048]{1,0:T(8,128)(2,1)} %get-tuple-element.139.refs_2_, ...), custom_call_target="tpu_custom_call" | custom-call | flops 64424509440 | bytes 73400320 | tf_op jit(solution)/shard_map/cross_backward/pallas_call | solution.py:376
  468.4 28.4 %reduce-scatter.9.cloned.1.call-done = bf16[128,4096]{1,0:T(8,128)(2,1)} async-done(((bf16[1024,4096]{1,0:T(8,128)(2,1)}), bf16[128,4096]{1,0:T(8,128)(2,1)}) %reduce-scatter.9.cloned.1.call-update) | async-done | bytes 1048592 | tf_op jit(solution)/shard_map/reduce_scatter | solution.py:1266
  496.8 14.4 %encoder_rows.1 = bf16[2048,1024]{1,0:T(8,128)(2,1)} custom-call(bf16[1024,2048]{1,0:T(8,128)(2,1)} %get-tuple-element.153.refs_0_.refs_3_, bf16[1024,2048]{1,0:T(8,128)(2,1)} %get-tuple-element.154.refs_1_.refs_4_, bf16[3,1024,1024]{2,1,0:T(8,128)(2,1)} %refs_3_.3, bf16[3,1024,1024]{2,1,0:T(8,128)(2,1)} %refs_3_.3), custom_call_target="tpu_custom_call" | custom-call | flops 8589934592 | bytes 25165824 | tf_op jit(solution)/shard_map/encoder_rows/pallas_call | solution.py:522
  514.0 20.6 %cross_weights.1 = (bf16[8,384,1024]{2,1,0:T(8,128)(2,1)}, f32[3,1024,128]{2,1,0:T(8,128)}) custom-call(bf16[1536,1024]{1,0:T(8,128)(2,1)} %copy-done.12, bf16[2048,1024]{1,0:T(8,128)(2,1)} %bitcast.288, bf16[1024,1536]{1,0:T(8,128)(2,1)} %get-tuple-element.161.refs_2_, bf16[1024,2048]{1,0:T(8,128)(2,1)} %get-tuple-element.153.refs_0_.refs_3_, ...), custom_call_target="tpu_custom_call" | custom-call | flops 11811160064 | bytes 46137344 | tf_op jit(solution)/shard_map/cross_weights/pallas_call | solution.py:481
  539.5 11.5 %multiply_reduce_fusion.1 = (f32[1024]{0:T(1024)S(1)}, f32[1536]{0:T(1024)S(1)}, f32[1536]{0:T(1024)S(1)}, f32[1024]{0:T(1024)S(1)}, f32[1536,1024]{1,0:T(8,128)S(1)}) fusion(f32[1536,1024]{1,0:T(8,128)} %copy-done.2, f32[1536]{0:T(1024)S(1)} %copy-done.22, f32[1536]{0:T(1024)S(1)} %copy-done.20, f32[1024]{0:T(1024)S(1)} %bitcast.262, ...), kind=kOutput, calls=%fused_computation.18 | convolution fusion | flops 3236948992 | bytes 24154112 | tf_op jit(solution)/shard_map/er,de->rd/dot_general | solution.py:617
  562.9 7.6 fusion.11.refs_10_
  570.6 40.3 %self_backward.2 = (bf16[1024,1536]{1,0:T(8,128)(2,1)}, bf16[2,1024,1536]{2,1,0:T(8,128)(2,1)}, bf16[512,1536]{1,0:T(8,128)(2,1)}, bf16[2,1024,768]{2,1,0:T(8,128)(2,1)}) custom-call(bf16[1024,1536]{1,0:T(8,128)(2,1)} %multiply_convert_fusion.2.refs_0_, bf16[1024,1536]{1,0:T(8,128)(2,1)} %convolution_convert_fusion.4.refs_1_, ...), custom_call_target="tpu_custom_call" | custom-call | flops 32212254720 | bytes 36700160 | tf_op jit(solution)/shard_map/self_backward/pallas_call | solution.py:405
  610.9 7.1 far_rows.2
  629.4 40.0 %self_backward.3 = (bf16[1024,1536]{1,0:T(8,128)(2,1)}, bf16[2,1024,1536]{2,1,0:T(8,128)(2,1)}, bf16[512,1536]{1,0:T(8,128)(2,1)}, bf16[2,1024,768]{2,1,0:T(8,128)(2,1)}) custom-call(bf16[1024,1536]{1,0:T(8,128)(2,1)} %multiply_convert_fusion.2.refs_0_, ...), custom_call_target="tpu_custom_call", output_to_operand_aliasing={{0}: (11, {}), {1}: (12, {}), {2}: (13, {})} | custom-call | flops 32212254720 | bytes 36700160 | tf_op jit(solution)/shard_map/self_backward/pallas_call | solution.py:405
  669.5 7.4 far_rows.3
  683.2 32.3 %self_weights.1 = (bf16[32,112,1024]{2,1,0:T(8,128)(2,1)}, f32[4,1024,128]{2,1,0:T(8,128)}) custom-call(bf16[1536,1024]{1,0:T(8,128)(2,1)} %bitcast.244, bf16[768,1024]{1,0:T(8,128)(2,1)} %pad_maximum_fusion.1.x_ref.refs_1_, bf16[768,1024]{1,0:T(8,128)(2,1)} %pad_maximum_fusion.2.x_ref.refs_2_, bf16[1024,1536]{1,0:T(8,128)(2,1)} %get-tuple-element.200.refs_3_.refs_0_, ...), custom_call_target="tpu_custom_call" | custom-call | flops 19327352832 | bytes 75497472 | tf_op jit(solution)/shard_map/self_weights/pallas_call | solution.py:481
  734.0 7.1 fusion
  756.7 19.4 %near_rows.1 = bf16[1536,1024]{1,0:T(8,128)(2,1)} custom-call(bf16[1024,1536]{1,0:T(8,128)(2,1)} %get-tuple-element.200.refs_3_.refs_0_, bf16[2,1024,1536]{2,1,0:T(8,128)(2,1)} %get-tuple-element.182.refs_4_.refs_5_.refs_1_.refs_2_, bf16[2,1024,1536]{2,1,0:T(8,128)(2,1)} %get-tuple-element.182.refs_4_.refs_5_.refs_1_.refs_2_, ...), custom_call_target="tpu_custom_call" | custom-call | flops 11274289152 | bytes 27787264 | tf_op jit(solution)/shard_map/near_rows/pallas_call | solution.py:522
  790.9 8.9 %collective-permute-done.21 = f32[4,4480]{1,0:T(4,128)S(1)} collective-permute-done((f32[4,4480]{1,0:T(4,128)S(1)}, f32[4,4480]{1,0:T(4,128)S(1)}, u32[]{:S(2)}, u32[]{:S(2)}) %collective-permute-start.21) | collective-permute-done | bytes 71712 | tf_op jit(solution)/shard_map/ppermute | solution.py:1476
  800.2 10.4 %collective-permute-start.23 = (bf16[160,1024]{1,0:T(8,128)(2,1)S(1)}, bf16[160,1024]{1,0:T(8,128)(2,1)S(1)}, u32[]{:S(2)}, u32[]{:S(2)}) collective-permute-start(bf16[160,1024]{1,0:T(8,128)(2,1)S(1)} %dynamic-slice_bitcast_fusion.5), channel_id=1, source_target_pairs={{0,1},{1,2},{2,3},{3,0},{4,5},{5,6},{6,7},{7,4},{8,9},{9,10},{10,1... | collective-permute-start | bytes 983048 | tf_op jit(solution)/shard_map/ppermute | solution.py:1304
  812.2 9.0 %collective-permute-done.23 = bf16[160,1024]{1,0:T(8,128)(2,1)S(1)} collective-permute-done((bf16[160,1024]{1,0:T(8,128)(2,1)S(1)}, bf16[160,1024]{1,0:T(8,128)(2,1)S(1)}, u32[]{:S(2)}, u32[]{:S(2)}) %collective-permute-start.23) | collective-permute-done | bytes 327712 | tf_op jit(solution)/shard_map/ppermute | solution.py:1304
  823.2 9.3 %collective-permute-done.24 = bf16[128,1024]{1,0:T(8,128)(2,1)S(1)} collective-permute-done((bf16[128,1024]{1,0:T(8,128)(2,1)S(1)}, bf16[128,1024]{1,0:T(8,128)(2,1)S(1)}, u32[]{:S(2)}, u32[]{:S(2)}) %collective-permute-start.24) | collective-permute-done | bytes 262176 | tf_op jit(solution)/shard_map/ppermute | solution.py:1304
  (311 shorter events, 228.4 us)
Async XLA Ops:
  7.2 159.6 %all-gather.2.cloned.1.call-start = ((), (), s32[]{:S(2)}) async-start(), calls=%async_computation.6 | async-start | bytes 5242880 | tf_op jit(solution)/shard_map/all_gather | solution.py:1224
  9.6 49.1 %collective-permute-start.2 = (bf16[256,1024]{1,0:T(8,128)(2,1)}, bf16[256,1024]{1,0:T(8,128)(2,1)}, u32[]{:S(2)}, u32[]{:S(2)}) collective-permute-start(bf16[256,1024]{1,0:T(8,128)(2,1)} %get-tuple-element.254), channel_id=1, source_target_pairs={{0,1},{1,2},{2,3},{4,5},{5,6},{6,7},{8,9},{9,10},{10,11},{12,13},{... | collective-permute-start | bytes 1572872 | tf_op jit(solution)/shard_map/ppermute | solution.py:1207
  15.3 43.4 %collective-permute-start.1 = (bf16[256,1024]{1,0:T(8,128)(2,1)}, bf16[256,1024]{1,0:T(8,128)(2,1)}, u32[]{:S(2)}, u32[]{:S(2)}) collective-permute-start(bf16[256,1024]{1,0:T(8,128)(2,1)} %get-tuple-element.254), channel_id=1, source_target_pairs={{0,2},{1,3},{4,6},{5,7},{8,10},{9,11},{12,14},{13,15},{16,18},{17,... | collective-permute-start | bytes 1572872 | tf_op jit(solution)/shard_map/ppermute | solution.py:1207
  19.9 38.9 %collective-permute-start = (bf16[256,1024]{1,0:T(8,128)(2,1)}, bf16[256,1024]{1,0:T(8,128)(2,1)}, u32[]{:S(2)}, u32[]{:S(2)}) collective-permute-start(bf16[256,1024]{1,0:T(8,128)(2,1)} %get-tuple-element.254), channel_id=1, source_target_pairs={{0,3},{4,7},{8,11},{12,15},{16,19},{20,23},{24,27},{28,31}} | collective-permute-start | bytes 1572872 | tf_op jit(solution)/shard_map/ppermute | solution.py:1207
  61.4 46.0 %collective-permute-start.5 = (bf16[256,1024]{1,0:T(8,128)(2,1)}, bf16[256,1024]{1,0:T(8,128)(2,1)S(1)}, u32[]{:S(2)}, u32[]{:S(2)}) collective-permute-start(bf16[256,1024]{1,0:T(8,128)(2,1)} %get-tuple-element.124), channel_id=1, source_target_pairs={{0,1},{1,2},{2,3},{4,5},{5,6},{6,7},{8,9},{9,10},{10,11},{12,13},{... | collective-permute-start | bytes 1572872 | tf_op jit(solution)/shard_map/ppermute | solution.py:1207
  65.9 41.6 %collective-permute-start.4 = (bf16[256,1024]{1,0:T(8,128)(2,1)}, bf16[256,1024]{1,0:T(8,128)(2,1)S(1)}, u32[]{:S(2)}, u32[]{:S(2)}) collective-permute-start(bf16[256,1024]{1,0:T(8,128)(2,1)} %get-tuple-element.124), channel_id=1, source_target_pairs={{0,2},{1,3},{4,6},{5,7},{8,10},{9,11},{12,14},{13,15},{16,18},{17,... | collective-permute-start | bytes 1572872 | tf_op jit(solution)/shard_map/ppermute | solution.py:1207
  71.2 40.9 %collective-permute-start.3 = (bf16[256,1024]{1,0:T(8,128)(2,1)}, bf16[256,1024]{1,0:T(8,128)(2,1)}, u32[]{:S(2)}, u32[]{:S(2)}) collective-permute-start(bf16[256,1024]{1,0:T(8,128)(2,1)} %get-tuple-element.124), channel_id=1, source_target_pairs={{0,3},{4,7},{8,11},{12,15},{16,19},{20,23},{24,27},{28,31}} | collective-permute-start | bytes 1572872 | tf_op jit(solution)/shard_map/ppermute | solution.py:1207
  80.6 387.8 %reduce-scatter.7.cloned.1.call-start = ((), (), s32[]{:S(2)}) async-start(), calls=%async_computation.7 | async-start | bytes 9437184 | tf_op jit(solution)/shard_map/reduce_scatter | solution.py:1266
  317.0 179.8 %reduce-scatter.9.cloned.1.call-start = ((), (), s32[]{:S(2)}) async-start(), calls=%async_computation.8 | async-start | bytes 9437184 | tf_op jit(solution)/shard_map/reduce_scatter | solution.py:1266
  357.9 311.5 %reduce-scatter.11.cloned.1.call-start = ((), (), s32[]{:S(2)}) async-start(), calls=%async_computation.9 | async-start | bytes 5242880 | tf_op jit(solution)/shard_map/reduce_scatter | solution.py:1341
  511.2 273.5 %reduce-scatter.13.cloned.1.call-start = ((), (), s32[]{:S(2)}) async-start(), calls=%async_computation.10 | async-start | bytes 2359296 | tf_op jit(solution)/shard_map/reduce_scatter | solution.py:1266
  512.5 22.2 %collective-permute-start.6 = (bf16[256,1024]{1,0:T(8,128)(2,1)S(1)}, bf16[256,1024]{1,0:T(8,128)(2,1)S(1)}, u32[]{:S(2)}, u32[]{:S(2)}) collective-permute-start(bf16[256,1024]{1,0:T(8,128)(2,1)S(1)} %fusion.34), channel_id=1, source_target_pairs={{0,1},{1,2},{2,3},{3,0},{4,5},{5,6},{6,7},{7,4},{8,9},{9,10},{10,1... | collective-permute-start | bytes 1572872 | tf_op jit(solution)/shard_map/ppermute | solution.py:1304
  534.7 250.0 %reduce-scatter.17.cloned.1.call-start = ((), (), s32[]{:S(2)}) async-start(), calls=%async_computation.12 | async-start | bytes 2359296 | tf_op jit(solution)/shard_map/reduce_scatter | solution.py:1266
  535.7 88.9 %collective-permute-start.7 = (bf16[256,1024]{1,0:T(8,128)(2,1)}, bf16[256,1024]{1,0:T(8,128)(2,1)}, u32[]{:S(2)}, u32[]{:S(2)}) collective-permute-start(bf16[256,1024]{1,0:T(8,128)(2,1)} %fusion.26), channel_id=1, source_target_pairs={{0,1},{1,2},{2,3},{3,0},{4,5},{5,6},{6,7},{7,4},{8,9},{9,10},{10,1... | collective-permute-start | bytes 1572872 | tf_op jit(solution)/shard_map/ppermute | solution.py:1304
  570.6 214.2 %reduce-scatter.15.cloned.1.call-start = ((), (), s32[]{:S(2)}) async-start(), calls=%async_computation.11 | async-start | bytes 7077888 | tf_op jit(solution)/shard_map/reduce_scatter | solution.py:1266
  620.7 48.7 %collective-permute-start.10 = (bf16[256,1024]{1,0:T(8,128)(2,1)}, bf16[256,1024]{1,0:T(8,128)(2,1)S(1)}, u32[]{:S(2)}, u32[]{:S(2)}) collective-permute-start(bf16[256,1024]{1,0:T(8,128)(2,1)} %get-tuple-element.259), channel_id=1, source_target_pairs={{3,0},{7,4},{11,8},{15,12},{19,16},{23,20},{27,24},{31,28}} | collective-permute-start | bytes 1572872 | tf_op jit(solution)/shard_map/ppermute | solution.py:1387
  622.0 47.5 %collective-permute-start.9 = (bf16[256,1024]{1,0:T(8,128)(2,1)}, bf16[256,1024]{1,0:T(8,128)(2,1)S(1)}, u32[]{:S(2)}, u32[]{:S(2)}) collective-permute-start(bf16[256,1024]{1,0:T(8,128)(2,1)} %get-tuple-element.260), channel_id=1, source_target_pairs={{2,0},{3,1},{6,4},{7,5},{10,8},{11,9},{14,12},{15,13},{18,16},{19,... | collective-permute-start | bytes 1572872 | tf_op jit(solution)/shard_map/ppermute | solution.py:1387
  623.3 46.2 %collective-permute-start.8 = (bf16[256,1024]{1,0:T(8,128)(2,1)}, bf16[256,1024]{1,0:T(8,128)(2,1)}, u32[]{:S(2)}, u32[]{:S(2)}) collective-permute-start(bf16[256,1024]{1,0:T(8,128)(2,1)} %get-tuple-element.261), channel_id=1, source_target_pairs={{1,0},{2,1},{3,2},{5,4},{6,5},{7,6},{9,8},{10,9},{11,10},{13,12},{... | collective-permute-start | bytes 1572872 | tf_op jit(solution)/shard_map/ppermute | solution.py:1387
  625.8 43.6 %collective-permute-start.11 = (bf16[256,1024]{1,0:T(8,128)(2,1)S(1)}, bf16[256,1024]{1,0:T(8,128)(2,1)}, u32[]{:S(2)}, u32[]{:S(2)}) collective-permute-start(bf16[256,1024]{1,0:T(8,128)(2,1)S(1)} %fusion.25), channel_id=1, source_target_pairs={{0,1},{1,2},{2,3},{3,0},{4,5},{5,6},{6,7},{7,4},{8,9},{9,10},{10,1... | collective-permute-start | bytes 1572872 | tf_op jit(solution)/shard_map/ppermute | solution.py:1304
  679.3 36.3 %collective-permute-start.14 = (bf16[256,1024]{1,0:T(8,128)(2,1)}, bf16[256,1024]{1,0:T(8,128)(2,1)}, u32[]{:S(2)}, u32[]{:S(2)}) collective-permute-start(bf16[256,1024]{1,0:T(8,128)(2,1)} %get-tuple-element.256), channel_id=1, source_target_pairs={{3,0},{7,4},{11,8},{15,12},{19,16},{23,20},{27,24},{31,28}} | collective-permute-start | bytes 1572872 | tf_op jit(solution)/shard_map/ppermute | solution.py:1387
  680.6 35.9 %collective-permute-start.13 = (bf16[256,1024]{1,0:T(8,128)(2,1)}, bf16[256,1024]{1,0:T(8,128)(2,1)}, u32[]{:S(2)}, u32[]{:S(2)}) collective-permute-start(bf16[256,1024]{1,0:T(8,128)(2,1)} %get-tuple-element.257), channel_id=1, source_target_pairs={{2,0},{3,1},{6,4},{7,5},{10,8},{11,9},{14,12},{15,13},{18,16},{19,... | collective-permute-start | bytes 1572872 | tf_op jit(solution)/shard_map/ppermute | solution.py:1387
  681.9 34.7 %collective-permute-start.12 = (bf16[256,1024]{1,0:T(8,128)(2,1)S(1)}, bf16[256,1024]{1,0:T(8,128)(2,1)}, u32[]{:S(2)}, u32[]{:S(2)}) collective-permute-start(bf16[256,1024]{1,0:T(8,128)(2,1)S(1)} %get-tuple-element.258), channel_id=1, source_target_pairs={{1,0},{2,1},{3,2},{5,4},{6,5},{7,6},{9,8},{10,9},{11,10},{13,12},{... | collective-permute-start | bytes 1572872 | tf_op jit(solution)/shard_map/ppermute | solution.py:1387
  720.8 13.1 %collective-permute-start.15 = (bf16[4,448,1024]{2,1,0:T(8,128)(2,1)}, bf16[4,448,1024]{2,1,0:T(8,128)(2,1)}, u32[]{:S(2)}, u32[]{:S(2)}) collective-permute-start(bf16[4,448,1024]{2,1,0:T(8,128)(2,1)} %dynamic-slice_bitcast_fusion), channel_id=1, source_target_pairs={{0,4},{4,0},{8,12},{12,8},{16,20},{20,16},{24,28},{28,24},{1,5},{5... | collective-permute-start | bytes 11010056 | tf_op jit(solution)/shard_map/ppermute | solution.py:1275
  744.3 31.9 %collective-permute-start.18 = (f32[4,4480]{1,0:T(4,128)S(1)}, f32[4,4480]{1,0:T(4,128)}, u32[]{:S(2)}, u32[]{:S(2)}) collective-permute-start(f32[4,4480]{1,0:T(4,128)S(1)} %constant_dynamic-update-slice_fusion), channel_id=1, source_target_pairs={{0,4},{4,0},{8,12},{12,8},{16,20},{20,16},{24,28},{28,24},{1,5},{5... | collective-permute-start | bytes 215048 | tf_op jit(solution)/shard_map/ppermute | solution.py:1476
  748.5 31.0 %collective-permute-start.17 = (bf16[2,224,1024]{2,1,0:T(8,128)(2,1)}, bf16[2,224,1024]{2,1,0:T(8,128)(2,1)}, u32[]{:S(2)}, u32[]{:S(2)}) collective-permute-start(bf16[2,224,1024]{2,1,0:T(8,128)(2,1)} %dynamic-slice_bitcast_fusion.1), channel_id=1, source_target_pairs={{0,16},{4,20},{8,24},{12,28},{16,0},{20,4},{24,8},{28,12},{1,17},{... | collective-permute-start | bytes 2752520 | tf_op jit(solution)/shard_map/ppermute | solution.py:1275
  750.9 31.3 %collective-permute-start.16 = (bf16[2,224,1024]{2,1,0:T(8,128)(2,1)}, bf16[2,224,1024]{2,1,0:T(8,128)(2,1)}, u32[]{:S(2)}, u32[]{:S(2)}) collective-permute-start(bf16[2,224,1024]{2,1,0:T(8,128)(2,1)} %dynamic-slice_bitcast_fusion.2), channel_id=1, source_target_pairs={{0,8},{4,12},{8,0},{12,4},{16,24},{20,28},{24,16},{28,20},{1,9},{5... | collective-permute-start | bytes 2752520 | tf_op jit(solution)/shard_map/ppermute | solution.py:1275
  785.9 24.8 %collective-permute-start.20 = (bf16[224,1024]{1,0:T(8,128)(2,1)S(1)}, bf16[224,1024]{1,0:T(8,128)(2,1)}, u32[]{:S(2)}, u32[]{:S(2)}) collective-permute-start(bf16[224,1024]{1,0:T(8,128)(2,1)S(1)} %dynamic-slice_bitcast_fusion.3), channel_id=1, source_target_pairs={{0,8},{4,12},{8,0},{12,4},{16,24},{20,28},{24,16},{28,20},{1,9},{5... | collective-permute-start | bytes 1376264 | tf_op jit(solution)/shard_map/ppermute | solution.py:1275
  787.5 12.3 %collective-permute-start.21 = (f32[4,4480]{1,0:T(4,128)S(1)}, f32[4,4480]{1,0:T(4,128)S(1)}, u32[]{:S(2)}, u32[]{:S(2)}) collective-permute-start(f32[4,4480]{1,0:T(4,128)S(1)} %add.359), channel_id=1, source_target_pairs={{0,8},{4,12},{8,0},{12,4},{16,24},{20,28},{24,16},{28,20},{1,9},{5... | collective-permute-start | bytes 215048 | tf_op jit(solution)/shard_map/ppermute | solution.py:1476
  789.0 23.0 %collective-permute-start.19 = (bf16[224,1024]{1,0:T(8,128)(2,1)S(1)}, bf16[224,1024]{1,0:T(8,128)(2,1)S(1)}, u32[]{:S(2)}, u32[]{:S(2)}) collective-permute-start(bf16[224,1024]{1,0:T(8,128)(2,1)S(1)} %dynamic-slice_bitcast_fusion.4), channel_id=1, source_target_pairs={{0,16},{4,20},{8,24},{12,28},{16,0},{20,4},{24,8},{28,12},{1,17},{... | collective-permute-start | bytes 1376264 | tf_op jit(solution)/shard_map/ppermute | solution.py:1275
  800.2 21.0 %collective-permute-start.23 = (bf16[160,1024]{1,0:T(8,128)(2,1)S(1)}, bf16[160,1024]{1,0:T(8,128)(2,1)S(1)}, u32[]{:S(2)}, u32[]{:S(2)}) collective-permute-start(bf16[160,1024]{1,0:T(8,128)(2,1)S(1)} %dynamic-slice_bitcast_fusion.5), channel_id=1, source_target_pairs={{0,1},{1,2},{2,3},{3,0},{4,5},{5,6},{6,7},{7,4},{8,9},{9,10},{10,1... | collective-permute-start | bytes 983048 | tf_op jit(solution)/shard_map/ppermute | solution.py:1304
  821.6 17.9 %collective-permute-start.27 = (bf16[160,1024]{1,0:T(8,128)(2,1)S(1)}, bf16[160,1024]{1,0:T(8,128)(2,1)S(1)}, u32[]{:S(2)}, u32[]{:S(2)}) collective-permute-start(bf16[160,1024]{1,0:T(8,128)(2,1)S(1)} %fusion.30), channel_id=1, source_target_pairs={{0,1},{1,2},{2,3},{3,0},{4,5},{5,6},{6,7},{7,4},{8,9},{9,10},{10,1... | collective-permute-start | bytes 983048 | tf_op jit(solution)/shard_map/ppermute | solution.py:1304
  832.6 12.6 %collective-permute-start.25 = (bf16[128,1024]{1,0:T(8,128)(2,1)S(1)}, bf16[128,1024]{1,0:T(8,128)(2,1)S(1)}, u32[]{:S(2)}, u32[]{:S(2)}) collective-permute-start(bf16[128,1024]{1,0:T(8,128)(2,1)S(1)} %fusion.40), channel_id=1, source_target_pairs={{0,1},{1,2},{2,3},{3,0},{4,5},{5,6},{6,7},{7,4},{8,9},{9,10},{10,1... | collective-permute-start | bytes 786440 | tf_op jit(solution)/shard_map/ppermute | solution.py:1304
  (52 other events, 941.1 us)
Sparse Core Ops, SparseCore 0:
  80.7 86.0 all-gather.1
  317.1 104.4 reduce-scatter.6
  425.4 71.2 reduce-scatter.8
  511.4 96.6 reduce-scatter.10
  611.5 39.7 reduce-scatter.12
  654.4 41.1 reduce-scatter.16
  699.4 70.0 reduce-scatter.14
